TPU v7x, 32 devices: a whole 2x2x4 slice. The times are simulated.
32 devices in a mesh: ctx: 32 (over z, y, x, core), head: 1.
Axes of the slice: x: 2, y: 2, z: 4, core: 2. Of those that a mesh axis runs over, the one named last changes fastest.
Arguments:
- shared_qk: bfloat16 [4096, 2048], P('ctx', 'head'), may hold values from -6 to 6
- values: bfloat16 [4096, 2048], P('ctx', 'head'), may hold values from -12 to 12
- out_grad: bfloat16 [4096, 2048], P('ctx', 'head'), may hold values from -6 to 6
- out_weight: bfloat16 [2048, 2048], P('ctx', 'head'), may hold values from -0.125 to 0.125
- buckets: int32 [2, 4096], P(None, 'ctx'), may hold values from 0 to 31, as said below
Outputs:
- mixed: bfloat16 [4096, 2048], P('ctx', 'head')
- grad_qk: bfloat16 [4096, 2048], P('ctx', 'head')
- grad_values: bfloat16 [4096, 2048], P('ctx', 'head')
- grad_weight: float32 [2048, 2048], P('ctx', 'head')
Inputs may be any that keep to these rules, and one draw needn't show every extreme that they name: `buckets`: in each round at most 8 of the tokens of one device share a bucket, and one bucket takes exactly 8 tokens from every device.
All inputs are finite; a program needn't handle non-finite values.
Results may differ from a plain program's by a relative error of at most 0.012.
The roundings to bfloat16 on the way count: a program that leaves them out, or rounds other values in their place, can miss the bound.
Values may be sent and summed in bfloat16 or wider, within the bound.
A program may use at most 128 MiB of HBM per device.

v0:
```python
import math

import jax
import jax.numpy as jnp
from jax import lax
from jax.sharding import PartitionSpec as P

HEAD_DIM = 128
SPAN = 128


self_penalty = 10000.0
masked_score = -1e30


def with_zero_row(matrix):
    return jnp.concatenate([matrix, jnp.zeros((1,) + matrix.shape[1:], matrix.dtype)], axis=0)


def key_windows(rows):
    row_count = rows.shape[0]
    leading = jnp.zeros((SPAN,) + rows.shape[1:], rows.dtype)
    earlier = jnp.concatenate([leading, rows[: row_count - SPAN]], axis=0)
    shape_out = (row_count // SPAN, SPAN) + rows.shape[1:]
    return jnp.concatenate([earlier.reshape(shape_out), rows.reshape(shape_out)], axis=1)


def fold_windows(stacked):
    current = stacked[:, SPAN:]
    earlier = stacked[:, :SPAN]
    return current + jnp.concatenate([earlier[1:], jnp.zeros_like(earlier[:1])], axis=0)


def span_probs(queries, key_rows, key_live):
    scores = jnp.einsum(
        "qhd,khd->hqk", queries, key_rows, preferred_element_type=jnp.float32
    ) * HEAD_DIM ** (-0.5)
    itself = jnp.arange(2 * SPAN)[None, :] == jnp.arange(SPAN)[:, None] + SPAN
    scores = jnp.where(itself[None], scores - self_penalty, scores)
    scores = jnp.where(key_live[None, None, :], scores, masked_score)
    largest = jnp.max(scores, axis=-1, keepdims=True)
    lifted = jnp.exp(scores - largest)
    summed = jnp.sum(lifted, axis=-1, keepdims=True)
    return (lifted / summed, (largest + jnp.log(summed))[..., 0])


def owner_forward(own_qk, own_values, occupied, local_heads):
    blocks = own_qk.shape[0] // SPAN
    queries = own_qk.reshape(blocks, SPAN, local_heads, HEAD_DIM)
    key_rows = key_windows(own_qk).reshape(blocks, 2 * SPAN, local_heads, HEAD_DIM)
    value_rows = key_windows(own_values).reshape(blocks, 2 * SPAN, local_heads, HEAD_DIM)
    live_keys = key_windows(occupied)

    def one_block(pieces):
        block_query, block_key, block_value, block_live = pieces
        probability, log_total = span_probs(block_query, block_key, block_live)
        result = jnp.einsum(
            "hqk,khd->qhd",
            probability.astype(jnp.bfloat16),
            block_value,
            preferred_element_type=jnp.float32,
        )
        return (result.astype(jnp.bfloat16).reshape(SPAN, local_heads * HEAD_DIM), log_total.T)

    outputs, log_totals = lax.map(one_block, (queries, key_rows, value_rows, live_keys))
    return (outputs.reshape(-1, local_heads * HEAD_DIM), log_totals.reshape(-1, local_heads))


def owner_backward(own_qk, own_values, occupied, own_grad, own_shift, local_heads):
    blocks = own_qk.shape[0] // SPAN
    queries = own_qk.reshape(blocks, SPAN, local_heads, HEAD_DIM)
    key_rows = key_windows(own_qk).reshape(blocks, 2 * SPAN, local_heads, HEAD_DIM)
    value_rows = key_windows(own_values).reshape(blocks, 2 * SPAN, local_heads, HEAD_DIM)
    live_keys = key_windows(occupied)
    grad_rows = own_grad.reshape(blocks, SPAN, local_heads, HEAD_DIM)
    shift_rows = own_shift.reshape(blocks, SPAN, local_heads)

    def one_block(pieces):
        block_query, block_key, block_value, block_live, block_grad, block_shift = pieces
        probability, log_total = span_probs(block_query, block_key, block_live)
        prob_grad = jnp.einsum(
            "qhd,khd->hqk", block_grad, block_value, preferred_element_type=jnp.float32
        )
        score_grad = (probability * (prob_grad - block_shift.T[:, :, None])).astype(jnp.bfloat16)
        query_grad = jnp.einsum(
            "hqk,khd->qhd", score_grad, block_key, preferred_element_type=jnp.float32
        ) * HEAD_DIM ** (-0.5)
        key_grad = jnp.einsum(
            "hqk,qhd->khd", score_grad, block_query, preferred_element_type=jnp.float32
        ) * HEAD_DIM ** (-0.5)
        value_grad = jnp.einsum(
            "hqk,qhd->khd",
            probability.astype(jnp.bfloat16),
            block_grad,
            preferred_element_type=jnp.float32,
        )
        return (query_grad, key_grad, value_grad)

    query_grad, key_grad, value_grad = lax.map(
        one_block, (queries, key_rows, value_rows, live_keys, grad_rows, shift_rows)
    )
    row_width = local_heads * HEAD_DIM
    qk_rows = (query_grad + fold_windows(key_grad)).reshape(-1, row_width).astype(jnp.bfloat16)
    value_out = fold_windows(value_grad).reshape(-1, row_width).astype(jnp.bfloat16)
    return (qk_rows, value_out)


def route_round(bucket_row, peer_count, per_peer, token_rows):
    owners = jnp.arange(peer_count, dtype=jnp.int32)
    member = (bucket_row[:, None] == owners[None, :]).astype(jnp.int32)
    earlier = jnp.cumsum(member, axis=0) - member
    position = jnp.sum(earlier * member, axis=1)
    slot_index = bucket_row * per_peer + position
    slot_token = (
        jnp.full((peer_count * per_peer,), token_rows, jnp.int32)
        .at[slot_index]
        .set(jnp.arange(token_rows, dtype=jnp.int32))
    )
    return (slot_index, slot_token)


def compact_slots(slot_marks, capacity):
    target = jnp.cumsum(slot_marks) - 1
    target = jnp.where(slot_marks > 0, target, capacity).astype(jnp.int32)
    source_slot = (
        jnp.full((capacity,), capacity, jnp.int32)
        .at[target]
        .set(jnp.arange(capacity, dtype=jnp.int32), mode="drop")
    )
    return (source_slot, target)


def per_device(shared_qk, values, out_grad, out_weight, buckets):
    token_rows, row_width = shared_qk.shape
    local_heads = row_width // HEAD_DIM
    peer_count = lax.axis_size("ctx")
    capacity = 2 * token_rows
    per_peer = capacity // peer_count
    rounds = buckets.shape[0]
    routes = [
        route_round(buckets[round_index], peer_count, per_peer, token_rows)
        for round_index in range(rounds)
    ]
    padded_qk = with_zero_row(shared_qk)
    padded_values = with_zero_row(values)
    whole_weight = lax.all_gather(out_weight, "ctx", axis=0, tiled=True)
    groups = [[round_index] for round_index in range(rounds)]

    def outgoing(matrix, round_index):
        return matrix[routes[round_index][1]].reshape((peer_count, per_peer) + matrix.shape[1:])

    def homeward(received, round_index):
        flat_rows = received.reshape((peer_count * per_peer,) + received.shape[2:])
        return flat_rows[routes[round_index][0]]

    round_outputs = [None] * rounds
    round_logs = [None] * rounds
    owner_state = [None] * rounds
    for round_group in groups:
        send_qk = jnp.stack(
            [outgoing(padded_qk, round_index) for round_index in round_group], axis=1
        )
        send_values = jnp.stack(
            [outgoing(padded_values, round_index) for round_index in round_group], axis=1
        )
        slot_marks = jnp.stack(
            [
                (routes[round_index][1] < token_rows)
                .astype(jnp.int32)
                .reshape(peer_count, per_peer)
                for round_index in round_group
            ],
            axis=1,
        )
        got_qk, got_values, got_marks = (
            lax.all_to_all(send_qk, "ctx", split_axis=0, concat_axis=0, tiled=True),
            lax.all_to_all(send_values, "ctx", split_axis=0, concat_axis=0, tiled=True),
            lax.all_to_all(slot_marks, "ctx", split_axis=0, concat_axis=0, tiled=True),
        )
        returned_rows = []
        returned_logs = []
        for member_index, round_index in enumerate(round_group):
            source_slot, target = compact_slots(got_marks[:, member_index].reshape(-1), capacity)
            own_qk = with_zero_row(got_qk[:, member_index].reshape(capacity, row_width))[
                source_slot
            ]
            own_values = with_zero_row(got_values[:, member_index].reshape(capacity, row_width))[
                source_slot
            ]
            occupied = source_slot < capacity
            rows_out, logs_out = owner_forward(own_qk, own_values, occupied, local_heads)
            owner_state[round_index] = (own_qk, own_values, occupied, source_slot, target)
            returned_rows.append(
                with_zero_row(rows_out)[target].reshape(peer_count, per_peer, row_width)
            )
            returned_logs.append(
                with_zero_row(logs_out)[target].reshape(peer_count, per_peer, local_heads)
            )
        back_rows, back_logs = (
            lax.all_to_all(
                jnp.stack(returned_rows, axis=1).astype(jnp.float32),
                "ctx",
                split_axis=0,
                concat_axis=0,
                tiled=True,
            ).astype(jnp.bfloat16),
            lax.all_to_all(
                jnp.stack(returned_logs, axis=1), "ctx", split_axis=0, concat_axis=0, tiled=True
            ),
        )
        for member_index, round_index in enumerate(round_group):
            round_outputs[round_index] = homeward(back_rows[:, member_index], round_index)
            round_logs[round_index] = homeward(back_logs[:, member_index], round_index)
    log_stack = jnp.stack(round_logs)
    largest = jnp.max(log_stack, axis=0)
    lifted = jnp.exp(log_stack - largest)
    round_weight = lifted / jnp.sum(lifted, axis=0)
    row_stack = (
        jnp.stack(round_outputs)
        .astype(jnp.float32)
        .reshape(rounds, token_rows, local_heads, HEAD_DIM)
    )
    attended = (
        jnp.sum(round_weight[..., None] * row_stack, axis=0)
        .reshape(token_rows, row_width)
        .astype(jnp.bfloat16)
    )
    partial_value = lax.dot_general(
        attended, whole_weight, (((1,), (1,)), ((), ())), preferred_element_type=jnp.float32
    )
    mixed = lax.psum_scatter(partial_value, "head", scatter_dimension=1, tiled=True).astype(
        jnp.bfloat16
    )
    full_grad = lax.all_gather(out_grad, "head", axis=1, tiled=True)
    attended_grad = jnp.dot(full_grad, whole_weight, preferred_element_type=jnp.float32)
    token_total = token_rows * peer_count
    grad_weight = lax.psum_scatter(
        lax.dot_general(
            full_grad, attended, (((0,), (0,)), ((), ())), preferred_element_type=jnp.float32
        ),
        "ctx",
        scatter_dimension=0,
        tiled=True,
    ) * (1.0 / math.sqrt(token_total))
    grad_heads = attended_grad.reshape(token_rows, local_heads, HEAD_DIM)
    inner = jnp.sum(
        grad_heads * attended.astype(jnp.float32).reshape(token_rows, local_heads, HEAD_DIM),
        axis=-1,
    )
    qk_total = jnp.zeros((token_rows, row_width), jnp.float32)
    value_total = jnp.zeros((token_rows, row_width), jnp.float32)
    for round_group in groups:
        send_grad = jnp.stack(
            [
                outgoing(
                    with_zero_row(
                        (round_weight[round_index][..., None] * grad_heads)
                        .reshape(token_rows, row_width)
                        .astype(jnp.bfloat16)
                    ),
                    round_index,
                )
                for round_index in round_group
            ],
            axis=1,
        )
        send_shift = jnp.stack(
            [
                outgoing(with_zero_row(round_weight[round_index] * inner), round_index)
                for round_index in round_group
            ],
            axis=1,
        )
        got_grad, got_shift = (
            lax.all_to_all(
                send_grad.astype(jnp.float32), "ctx", split_axis=0, concat_axis=0, tiled=True
            ).astype(send_grad.dtype),
            lax.all_to_all(send_shift, "ctx", split_axis=0, concat_axis=0, tiled=True),
        )
        returned_qk = []
        returned_values = []
        for member_index, round_index in enumerate(round_group):
            own_qk, own_values, occupied, source_slot, target = owner_state[round_index]
            own_grad = with_zero_row(got_grad[:, member_index].reshape(capacity, row_width))[
                source_slot
            ]
            own_shift = with_zero_row(got_shift[:, member_index].reshape(capacity, local_heads))[
                source_slot
            ]
            qk_rows, value_rows = owner_backward(
                own_qk, own_values, occupied, own_grad, own_shift, local_heads
            )
            returned_qk.append(
                with_zero_row(qk_rows)[target].reshape(peer_count, per_peer, row_width)
            )
            returned_values.append(
                with_zero_row(value_rows)[target].reshape(peer_count, per_peer, row_width)
            )
        back_qk, back_values = (
            lax.all_to_all(
                jnp.stack(returned_qk, axis=1), "ctx", split_axis=0, concat_axis=0, tiled=True
            ),
            lax.all_to_all(
                jnp.stack(returned_values, axis=1), "ctx", split_axis=0, concat_axis=0, tiled=True
            ),
        )
        for member_index, round_index in enumerate(round_group):
            qk_total = qk_total + homeward(back_qk[:, member_index], round_index).astype(
                jnp.float32
            )
            value_total = value_total + homeward(back_values[:, member_index], round_index).astype(
                jnp.float32
            )
    return (mixed, qk_total.astype(jnp.bfloat16), value_total.astype(jnp.bfloat16), grad_weight)


def solution(mesh):
    in_specs = (
        P("ctx", "head"),
        P("ctx", "head"),
        P("ctx", "head"),
        P("ctx", "head"),
        P(None, "ctx"),
    )
    out_specs = (P("ctx", "head"), P("ctx", "head"), P("ctx", "head"), P("ctx", "head"))
    return jax.shard_map(
        per_device, mesh=mesh, in_specs=in_specs, out_specs=out_specs, check_vma=False
    )
```

profile of v0, /device:TPU:0, one launch (start us, length us, event | category | flops | bytes accessed | tf_op | source)
XLA Modules:
  0.0 619.1 jit_solution(15307058896283939601)
XLA Ops:
  11.1 7.3 %all-to-all-start.5 = ((s32[32,1,8]{2,1,0:T(1,128)}), s32[32,1,8]{2,1,0:T(1,128)S(1)}, u32[]{:S(2)}, u32[]{:S(2)}) async-start(s32[32,1,8]{2,1,0:T(1,128)} %bitcast.66), calls=%async_computation.5 | async-start | bytes 32768 | tf_op jit(solution)/shard_map/all_to_all | solution.py:178
  20.1 5.4 all-to-all-done.5
  25.5 2.5 all-to-all-start.1
  31.5 3.6 all-to-all-done.1
  35.1 2.6 all-to-all-start.4
  40.2 23.8 %all-to-all-done.4 = bf16[32,1,8,2048]{3,2,1,0:T(8,128)(2,1)S(1)} async-done(((bf16[32,1,8,2048]{3,2,1,0:T(8,128)(2,1)}), bf16[32,1,8,2048]{3,2,1,0:T(8,128)(2,1)S(1)}, u32[]{:S(2)}, u32[]{:S(2)}) %all-to-all-start.4) | async-done | bytes 1048608 | tf_op jit(solution)/shard_map/all_to_all | solution.py:177
  64.0 3.7 all-to-all-start.6
  70.0 23.8 %all-to-all-done.6 = bf16[32,1,8,2048]{3,2,1,0:T(8,128)(2,1)} async-done(((bf16[32,1,8,2048]{3,2,1,0:T(8,128)(2,1)}), bf16[32,1,8,2048]{3,2,1,0:T(8,128)(2,1)}, u32[]{:S(2)}, u32[]{:S(2)}) %all-to-all-start.6) | async-done | bytes 1048608 | tf_op jit(solution)/shard_map/all_to_all | solution.py:176
  93.9 3.7 all-to-all-start
  107.2 22.2 %all-to-all-done = bf16[32,1,8,2048]{3,2,1,0:T(8,128)(2,1)} async-done(((bf16[32,1,8,2048]{3,2,1,0:T(8,128)(2,1)}), bf16[32,1,8,2048]{3,2,1,0:T(8,128)(2,1)}, u32[]{:S(2)}, u32[]{:S(2)}) %all-to-all-start) | async-done | bytes 1048608 | tf_op jit(solution)/shard_map/all_to_all | solution.py:177
  129.4 4.0 all-to-all-start.2
  148.5 20.6 %all-to-all-done.2 = bf16[32,1,8,2048]{3,2,1,0:T(8,128)(2,1)} async-done(((bf16[32,1,8,2048]{3,2,1,0:T(8,128)(2,1)}), bf16[32,1,8,2048]{3,2,1,0:T(8,128)(2,1)}, u32[]{:S(2)}, u32[]{:S(2)}) %all-to-all-start.2) | async-done | bytes 1048608 | tf_op jit(solution)/shard_map/all_to_all | solution.py:176
  179.0 15.1 %while.61 = (s32[]{:T(128)}, bf16[2,128,2048]{2,1,0:T(8,128)(2,1)}, f32[2,128,16]{1,2,0:T(8,128)S(1)}, bf16[2,256,16,128]{3,1,2,0:T(8,128)(2,1)}, pred[2,256]{1,...) while((s32[]{:T(128)}, bf16[2,128,2048]{2,1,0:T(8,128)(2,1)}, ...), condition=%wide.region_19.20_spmd, body=%wide.region_16.19_spmd.sunk | while | flops 273971328 | bytes 20057224 | solution.py:65
  195.6 4.0 all-to-all-start.7
  204.8 12.0 %while.60 = (s32[]{:T(128)}, bf16[2,128,2048]{2,1,0:T(8,128)(2,1)}, f32[2,128,16]{1,2,0:T(8,128)S(1)}, bf16[2,256,16,128]{3,1,2,0:T(8,128)(2,1)}, pred[2,256]{1,...) while((s32[]{:T(128)}, bf16[2,128,2048]{2,1,0:T(8,128)(2,1)}, ...), condition=%wide.region_9.10_spmd, body=%wide.region_6.9_spmd.sunk | while | flops 273971328 | bytes 20057224 | solution.py:65
  218.4 5.9 all-to-all-start.3
  228.0 3.4 all-to-all-done.3
  231.4 2.6 all-to-all-start.9
  237.7 22.5 %all-to-all-done.9 = bf16[32,1,8,2048]{3,2,1,0:T(8,128)(2,1)S(1)} async-done(((bf16[32,1,8,2048]{3,2,1,0:T(8,128)(2,1)}), bf16[32,1,8,2048]{3,2,1,0:T(8,128)(2,1)S(1)}, u32[]{:S(2)}, u32[]{:S(2)}) %all-to-all-start.9) | async-done | bytes 1048608 | tf_op jit(solution)/shard_map/all_to_all | solution.py:200
  260.3 3.5 all-to-all-start.8
  268.9 21.1 %all-to-all-done.8 = bf16[32,1,8,2048]{3,2,1,0:T(8,128)(2,1)S(1)} async-done(((bf16[32,1,8,2048]{3,2,1,0:T(8,128)(2,1)}), bf16[32,1,8,2048]{3,2,1,0:T(8,128)(2,1)S(1)}, u32[]{:S(2)}, u32[]{:S(2)}) %all-to-all-start.8) | async-done | bytes 1048608 | tf_op jit(solution)/shard_map/all_to_all | solution.py:200
  291.9 8.1 %convolution_bitcast_fusion = f32[2048,2048]{0,1:T(8,128)} fusion(bf16[128,2048]{1,0:T(8,128)(2,1)S(1)} %copy-done, bf16[16,8,16,128]{3,2,1,0:T(8,128)(2,1)S(1)} %bitcast.471), kind=kOutput, calls=%fused_computation.158 | convolution fusion | flops 1073741824 | bytes 17825792 | tf_op jit(solution)/shard_map/dot_general | solution.py:238
  300.0 17.6 %copy.136 = f32[2048,2048]{1,0:T(8,128)} copy(f32[2048,2048]{0,1:T(8,128)} %convolution_bitcast_fusion) | data formatting | bytes 33554432
  318.4 5.5 fusion.123
  325.8 3.6 all-to-all-start.14
  330.9 5.6 all-to-all-done.14
  336.6 2.5 all-to-all-start.11
  341.5 4.7 all-to-all-done.11
  346.2 3.7 all-to-all-start.13
  349.9 2.4 gather_fusion.16
  355.5 27.1 %all-to-all-done.13 = bf16[32,1,8,2048]{3,2,1,0:T(8,128)(2,1)S(1)} async-done(((bf16[32,1,8,2048]{3,2,1,0:T(8,128)(2,1)}), bf16[32,1,8,2048]{3,2,1,0:T(8,128)(2,1)S(1)}, u32[]{:S(2)}, u32[]{:S(2)}) %all-to-all-start.13) | async-done | bytes 1048608 | tf_op jit(solution)/shard_map/all_to_all | solution.py:275
  382.6 7.5 %all-to-all-start.10 = ((bf16[32,1,8,2048]{3,2,1,0:T(8,128)(2,1)}), bf16[32,1,8,2048]{3,2,1,0:T(8,128)(2,1)}, u32[]{:S(2)}, u32[]{:S(2)}) async-start(bf16[32,1,8,2048]{3,2,1,0:T(8,128)(2,1)} %bitcast.344), calls=%async_computation.10 | async-start | bytes 2097152 | tf_op jit(solution)/shard_map/all_to_all | solution.py:275
  394.4 2.4 broadcast.513.clone
  396.9 2.5 broadcast.513.clone.1
  399.3 35.2 %while.63 = (s32[]{:T(128)}, f32[2,128,16,128]{1,3,2,0:T(8,128)}, f32[2,256,16,128]{1,3,2,0:T(8,128)}, f32[2,256,16,128]{1,3,2,0:T(8,128)}, bf16[2,256,16,128]{3...) while((s32[]{:T(128)}, f32[2,128,16,128]{1,3,2,0:T(8,128)}, ...), condition=%wide.region_30.31_spmd, body=%wide.region_27.30_spmd.sunk | while | flops 815041152 | bytes 75128080 | solution.py:99
  399.4 3.3 fusion.222
  403.9 2.8 multiply_convert_fusion.5
  410.6 6.3 %bitcast_dynamic-update-slice_fusion.17 = f32[2,256,16,128]{1,3,2,0:T(8,128)} fusion(f32[2,256,16,128]{1,3,2,0:T(8,128)} %get-tuple-element.945, s32[]{:T(128)S(6)} %copy.269, f32[16,128]{1,0:T(8,128)S(1)} %get-tuple-element.882, bf16[1,128,16,128]{3,2,1,0:T(8,128)(2,1)S(1)} %constant_dynamic-slice_fusion.5, ...), kind=kOutput, calls=%fused_computation.119.clone.1 | convolution fusion | flops 272107776 | bytes 4237312 | tf_op jit(solution)/shard_map/while/body/eval_jaxpr/hqk,qhd->khd/dot_general | solution.py:91
  417.0 3.3 fusion.222
  421.4 2.8 multiply_convert_fusion.5
  428.2 6.3 %bitcast_dynamic-update-slice_fusion.17 = f32[2,256,16,128]{1,3,2,0:T(8,128)} fusion(f32[2,256,16,128]{1,3,2,0:T(8,128)} %get-tuple-element.945, s32[]{:T(128)S(6)} %copy.269, f32[16,128]{1,0:T(8,128)S(1)} %get-tuple-element.882, bf16[1,128,16,128]{3,2,1,0:T(8,128)(2,1)S(1)} %constant_dynamic-slice_fusion.5, ...), kind=kOutput, calls=%fused_computation.119.clone.1 | convolution fusion | flops 272107776 | bytes 4237312 | tf_op jit(solution)/shard_map/while/body/eval_jaxpr/hqk,qhd->khd/dot_general | solution.py:91
  442.3 6.3 %all-to-all-start.15 = ((bf16[32,1,8,2048]{3,2,1,0:T(8,128)(2,1)}), bf16[32,1,8,2048]{3,2,1,0:T(8,128)(2,1)S(1)}, u32[]{:S(2)}, u32[]{:S(2)}) async-start(bf16[32,1,8,2048]{3,2,1,0:T(8,128)(2,1)} %bitcast.108), calls=%async_computation.15 | async-start | bytes 2097152 | tf_op jit(solution)/shard_map/all_to_all | solution.py:300
  452.3 2.5 copy.179
  456.3 2.4 broadcast.513.clone.2
  458.8 2.5 broadcast.513.clone.3
  461.2 36.5 %while.62 = (s32[]{:T(128)}, f32[2,128,16,128]{1,3,2,0:T(8,128)}, f32[2,256,16,128]{1,3,2,0:T(8,128)}, f32[2,256,16,128]{1,3,2,0:T(8,128)}, bf16[2,256,16,128]{3...) while((s32[]{:T(128)}, f32[2,128,16,128]{1,3,2,0:T(8,128)}, ...), condition=%wide.region_26.27_spmd, body=%wide.region_23.26_spmd.sunk | while | flops 815041152 | bytes 79322384 | solution.py:99
  461.4 3.5 fusion.210
  466.0 2.8 multiply_convert_fusion.4
  473.0 6.5 %bitcast_dynamic-update-slice_fusion.15 = f32[2,256,16,128]{1,3,2,0:T(8,128)} fusion(f32[2,256,16,128]{1,3,2,0:T(8,128)} %get-tuple-element.978, s32[]{:T(128)S(6)} %copy.281, f32[16,128]{1,0:T(8,128)S(1)} %get-tuple-element.870, bf16[1,128,16,128]{3,2,1,0:T(8,128)(2,1)S(1)} %constant_dynamic-slice_fusion.4, ...), kind=kOutput, calls=%fused_computation.77.clone.1 | convolution fusion | flops 272107776 | bytes 4237312 | tf_op jit(solution)/shard_map/while/body/eval_jaxpr/hqk,qhd->khd/dot_general | solution.py:91
  479.6 3.5 fusion.210
  484.3 2.8 multiply_convert_fusion.4
  491.3 6.4 %bitcast_dynamic-update-slice_fusion.15 = f32[2,256,16,128]{1,3,2,0:T(8,128)} fusion(f32[2,256,16,128]{1,3,2,0:T(8,128)} %get-tuple-element.978, s32[]{:T(128)S(6)} %copy.281, f32[16,128]{1,0:T(8,128)S(1)} %get-tuple-element.870, bf16[1,128,16,128]{3,2,1,0:T(8,128)(2,1)S(1)} %constant_dynamic-slice_fusion.4, ...), kind=kOutput, calls=%fused_computation.77.clone.1 | convolution fusion | flops 272107776 | bytes 4237312 | tf_op jit(solution)/shard_map/while/body/eval_jaxpr/hqk,qhd->khd/dot_general | solution.py:91
  499.7 3.1 add_convert_fusion.3
  507.8 6.1 all-to-all-start.12
  515.2 2.8 add_convert_fusion
  522.7 23.1 %all-to-all-done.12 = bf16[32,1,8,2048]{3,2,1,0:T(8,128)(2,1)} async-done(((bf16[32,1,8,2048]{3,2,1,0:T(8,128)(2,1)}), bf16[32,1,8,2048]{3,2,1,0:T(8,128)(2,1)}, u32[]{:S(2)}, u32[]{:S(2)}) %all-to-all-start.12) | async-done | bytes 1048608 | tf_op jit(solution)/shard_map/all_to_all | solution.py:300
  545.7 4.7 all-to-all-start.17
  551.8 2.8 add_convert_fusion.1
  559.2 17.5 %all-to-all-done.17 = bf16[32,1,8,2048]{3,2,1,0:T(8,128)(2,1)} async-done(((bf16[32,1,8,2048]{3,2,1,0:T(8,128)(2,1)}), bf16[32,1,8,2048]{3,2,1,0:T(8,128)(2,1)}, u32[]{:S(2)}, u32[]{:S(2)}) %all-to-all-start.17) | async-done | bytes 1048608 | tf_op jit(solution)/shard_map/all_to_all | solution.py:303
  576.7 3.6 all-to-all-start.16
  580.3 7.1 %convolution_convert_fusion.2 = bf16[128,2048]{1,0:T(8,128)(2,1)} fusion(bf16[2048,2048]{1,0:T(8,128)(2,1)} %all-gather.2.cloned.1.call-done, bf16[16,8,16,128]{3,2,1,0:T(8,128)(2,1)S(1)} %bitcast.472), kind=kOutput, calls=%fused_computation.159 | convolution fusion | flops 1074003968 | bytes 9437184 | tf_op jit(solution)/shard_map/dot_general | solution.py:228
  588.4 2.9 gather_fusion.21
  591.3 2.9 gather_fusion.31
  594.3 12.3 %all-to-all-done.16 = bf16[32,1,8,2048]{3,2,1,0:T(8,128)(2,1)S(1)} async-done(((bf16[32,1,8,2048]{3,2,1,0:T(8,128)(2,1)}), bf16[32,1,8,2048]{3,2,1,0:T(8,128)(2,1)S(1)}, u32[]{:S(2)}, u32[]{:S(2)}) %all-to-all-start.16) | async-done | bytes 1048608 | tf_op jit(solution)/shard_map/all_to_all | solution.py:303
  (361 shorter events, 170.6 us)
Async XLA Ops:
  7.2 284.8 %copy-start = (bf16[128,2048]{1,0:T(8,128)(2,1)S(1)}, bf16[128,2048]{1,0:T(8,128)(2,1)}, u32[]{:S(2)}) copy-start(bf16[128,2048]{1,0:T(8,128)(2,1)} %param.15) | copy-start | bytes 1572868
  11.1 14.4 %all-to-all-start.5 = ((s32[32,1,8]{2,1,0:T(1,128)}), s32[32,1,8]{2,1,0:T(1,128)S(1)}, u32[]{:S(2)}, u32[]{:S(2)}) async-start(s32[32,1,8]{2,1,0:T(1,128)} %bitcast.66), calls=%async_computation.5 | async-start | bytes 32768 | tf_op jit(solution)/shard_map/all_to_all | solution.py:178
  25.5 9.6 %all-to-all-start.1 = ((s32[32,1,8]{2,1,0:T(1,128)}), s32[32,1,8]{2,1,0:T(1,128)S(1)}, u32[]{:S(2)}, u32[]{:S(2)}) async-start(s32[32,1,8]{2,1,0:T(1,128)} %bitcast.45), calls=%async_computation.1 | async-start | bytes 32768 | tf_op jit(solution)/shard_map/all_to_all | solution.py:178
  31.5 6.3 %copy-start.30 = (bf16[128,2048]{1,0:T(8,128)(2,1)S(1)}, bf16[128,2048]{1,0:T(8,128)(2,1)}, u32[]{:S(2)}) copy-start(bf16[128,2048]{1,0:T(8,128)(2,1)} %param.13) | copy-start | bytes 1572868
  35.1 28.9 %all-to-all-start.4 = ((bf16[32,1,8,2048]{3,2,1,0:T(8,128)(2,1)}), bf16[32,1,8,2048]{3,2,1,0:T(8,128)(2,1)S(1)}, u32[]{:S(2)}, u32[]{:S(2)}) async-start(bf16[32,1,8,2048]{3,2,1,0:T(8,128)(2,1)} %bitcast.64), calls=%async_computation.4 | async-start | bytes 2097152 | tf_op jit(solution)/shard_map/all_to_all | solution.py:177
  64.0 29.9 %all-to-all-start.6 = ((bf16[32,1,8,2048]{3,2,1,0:T(8,128)(2,1)}), bf16[32,1,8,2048]{3,2,1,0:T(8,128)(2,1)}, u32[]{:S(2)}, u32[]{:S(2)}) async-start(bf16[32,1,8,2048]{3,2,1,0:T(8,128)(2,1)} %bitcast.72), calls=%async_computation.6 | async-start | bytes 2097152 | tf_op jit(solution)/shard_map/all_to_all | solution.py:176
  93.9 35.6 %all-to-all-start = ((bf16[32,1,8,2048]{3,2,1,0:T(8,128)(2,1)}), bf16[32,1,8,2048]{3,2,1,0:T(8,128)(2,1)}, u32[]{:S(2)}, u32[]{:S(2)}) async-start(bf16[32,1,8,2048]{3,2,1,0:T(8,128)(2,1)} %bitcast.43), calls=%async_computation | async-start | bytes 2097152 | tf_op jit(solution)/shard_map/all_to_all | solution.py:177
  97.6 220.0 %all-gather.2.cloned.1.call-start = ((), (), s32[]{:S(2)}) async-start(), calls=%async_computation.19 | async-start | bytes 8650752 | tf_op jit(solution)/shard_map/all_gather | solution.py:146
  129.4 39.7 %all-to-all-start.2 = ((bf16[32,1,8,2048]{3,2,1,0:T(8,128)(2,1)}), bf16[32,1,8,2048]{3,2,1,0:T(8,128)(2,1)}, u32[]{:S(2)}, u32[]{:S(2)}) async-start(bf16[32,1,8,2048]{3,2,1,0:T(8,128)(2,1)} %bitcast.51), calls=%async_computation.2 | async-start | bytes 2097152 | tf_op jit(solution)/shard_map/all_to_all | solution.py:176
  133.6 101.7 %copy-start.31 = (s32[1024]{0:T(1024)}, s32[1024]{0:T(1024)S(1)}, u32[]{:S(2)}) copy-start(s32[1024]{0:T(1024)S(1)} %pad_clamp_fusion.5) | copy-start | bytes 12292
  172.0 2.4 copy-start.24
  173.2 1.5 copy-start.25
  174.8 1.4 copy-start.20
  176.1 2.8 copy-start.26
  180.8 1.6 copy-start.27
  188.3 1.6 copy-start.27
  194.0 7.6 %copy-start.2 = (bf16[2,256,16,128]{3,1,2,0:T(8,128)(2,1)}, bf16[2,256,16,128]{3,1,2,0:T(8,128)(2,1)S(1)}, u32[]{:S(2)}) copy-start(bf16[2,256,16,128]{3,1,2,0:T(8,128)(2,1)S(1)} %get-tuple-element.1006) | copy-start | bytes 6291460
  195.6 22.8 %all-to-all-start.7 = ((f32[32,1,128]{2,1,0:T(1,128)}), f32[32,1,128]{2,1,0:T(1,128)S(1)}, u32[]{:S(2)}, u32[]{:S(2)}) async-start(f32[32,1,128]{2,1,0:T(1,128)} %reshape.915), calls=%async_computation.7 | async-start | bytes 32768 | tf_op jit(solution)/shard_map/all_to_all | solution.py:207
  199.6 1.7 copy-start.22
  199.6 2.0 copy-start.21
  201.9 2.5 copy-start.28
  203.2 1.6 copy-start.4
  206.8 1.6 copy-start.29
  212.8 1.6 copy-start.29
  216.8 7.5 %copy-start.10 = (bf16[2,128,16,128]{3,1,2,0:T(8,128)(2,1)}, bf16[2,128,16,128]{3,1,2,0:T(8,128)(2,1)S(1)}, u32[]{:S(2)}) copy-start(bf16[2,128,16,128]{3,1,2,0:T(8,128)(2,1)S(1)} %get-tuple-element.1008) | copy-start | bytes 3145732
  218.4 13.0 %all-to-all-start.3 = ((f32[32,1,128]{2,1,0:T(1,128)}), f32[32,1,128]{2,1,0:T(1,128)S(1)}, u32[]{:S(2)}, u32[]{:S(2)}) async-start(f32[32,1,128]{2,1,0:T(1,128)} %reshape.917), calls=%async_computation.3 | async-start | bytes 32768 | tf_op jit(solution)/shard_map/all_to_all | solution.py:207
  231.4 28.9 %all-to-all-start.9 = ((bf16[32,1,8,2048]{3,2,1,0:T(8,128)(2,1)}), bf16[32,1,8,2048]{3,2,1,0:T(8,128)(2,1)S(1)}, u32[]{:S(2)}, u32[]{:S(2)}) async-start(bf16[32,1,8,2048]{3,2,1,0:T(8,128)(2,1)} %bitcast.345), calls=%async_computation.9 | async-start | bytes 2097152 | tf_op jit(solution)/shard_map/all_to_all | solution.py:200
  260.3 29.8 %all-to-all-start.8 = ((bf16[32,1,8,2048]{3,2,1,0:T(8,128)(2,1)}), bf16[32,1,8,2048]{3,2,1,0:T(8,128)(2,1)S(1)}, u32[]{:S(2)}, u32[]{:S(2)}) async-start(bf16[32,1,8,2048]{3,2,1,0:T(8,128)(2,1)} %bitcast.478), calls=%async_computation.8 | async-start | bytes 2097152 | tf_op jit(solution)/shard_map/all_to_all | solution.py:200
  263.8 345.6 %reduce-scatter.4.cloned.1.call-start = ((), (), s32[]{:S(2)}) async-start(), calls=%async_computation.20 | async-start | bytes 17301504
  264.0 4.8 copy-start.34
  264.1 26.0 %copy-start.33 = (s32[1024]{0:T(1024)}, s32[1024]{0:T(1024)S(1)}, u32[]{:S(2)}) copy-start(s32[1024]{0:T(1024)S(1)} %pad_clamp_fusion.4) | copy-start | bytes 12292
  325.8 10.7 %all-to-all-start.14 = ((f32[32,1,128]{2,1,0:T(1,128)}), f32[32,1,128]{2,1,0:T(1,128)S(1)}, u32[]{:S(2)}, u32[]{:S(2)}) async-start(f32[32,1,128]{2,1,0:T(1,128)} %reshape.919), calls=%async_computation.14 | async-start | bytes 32768 | tf_op jit(solution)/shard_map/all_to_all | solution.py:278
  336.6 9.6 %all-to-all-start.11 = ((f32[32,1,128]{2,1,0:T(1,128)}), f32[32,1,128]{2,1,0:T(1,128)S(1)}, u32[]{:S(2)}, u32[]{:S(2)}) async-start(f32[32,1,128]{2,1,0:T(1,128)} %reshape.921), calls=%async_computation.11 | async-start | bytes 32768 | tf_op jit(solution)/shard_map/all_to_all | solution.py:278
  346.2 36.4 %all-to-all-start.13 = ((bf16[32,1,8,2048]{3,2,1,0:T(8,128)(2,1)}), bf16[32,1,8,2048]{3,2,1,0:T(8,128)(2,1)S(1)}, u32[]{:S(2)}, u32[]{:S(2)}) async-start(bf16[32,1,8,2048]{3,2,1,0:T(8,128)(2,1)} %bitcast.343), calls=%async_computation.13 | async-start | bytes 2097152 | tf_op jit(solution)/shard_map/all_to_all | solution.py:275
  382.6 59.7 %all-to-all-start.10 = ((bf16[32,1,8,2048]{3,2,1,0:T(8,128)(2,1)}), bf16[32,1,8,2048]{3,2,1,0:T(8,128)(2,1)}, u32[]{:S(2)}, u32[]{:S(2)}) async-start(bf16[32,1,8,2048]{3,2,1,0:T(8,128)(2,1)} %bitcast.344), calls=%async_computation.10 | async-start | bytes 2097152 | tf_op jit(solution)/shard_map/all_to_all | solution.py:275
  396.9 2.5 copy-start.3
  403.8 2.8 copy-start.16
  403.8 3.8 copy-start.8
  406.7 1.5 copy-start.12
  407.2 1.5 copy-start.17
  408.7 1.9 copy-start.9
  421.4 2.8 copy-start.16
  421.4 3.9 copy-start.8
  424.2 1.5 copy-start.12
  424.8 1.5 copy-start.17
  426.3 1.9 copy-start.9
  434.5 2.0 copy-start.18
  442.3 65.5 %all-to-all-start.15 = ((bf16[32,1,8,2048]{3,2,1,0:T(8,128)(2,1)}), bf16[32,1,8,2048]{3,2,1,0:T(8,128)(2,1)S(1)}, u32[]{:S(2)}, u32[]{:S(2)}) async-start(bf16[32,1,8,2048]{3,2,1,0:T(8,128)(2,1)} %bitcast.108), calls=%async_computation.15 | async-start | bytes 2097152 | tf_op jit(solution)/shard_map/all_to_all | solution.py:300
  458.8 2.5 copy-start.11
  466.0 2.8 copy-start.5
  466.0 3.2 copy-start.13
  466.0 4.5 copy-start.6
  469.7 1.4 copy-start.14
  471.1 1.9 copy-start.7
  484.3 2.8 copy-start.5
  484.3 3.2 copy-start.13
  484.3 4.5 copy-start.6
  488.0 1.4 copy-start.14
  489.3 1.9 copy-start.7
  497.7 2.0 copy-start.15
  507.8 37.9 %all-to-all-start.12 = ((bf16[32,1,8,2048]{3,2,1,0:T(8,128)(2,1)}), bf16[32,1,8,2048]{3,2,1,0:T(8,128)(2,1)}, u32[]{:S(2)}, u32[]{:S(2)}) async-start(bf16[32,1,8,2048]{3,2,1,0:T(8,128)(2,1)} %bitcast.481), calls=%async_computation.12 | async-start | bytes 2097152 | tf_op jit(solution)/shard_map/all_to_all | solution.py:300
  545.7 30.9 %all-to-all-start.17 = ((bf16[32,1,8,2048]{3,2,1,0:T(8,128)(2,1)}), bf16[32,1,8,2048]{3,2,1,0:T(8,128)(2,1)}, u32[]{:S(2)}, u32[]{:S(2)}) async-start(bf16[32,1,8,2048]{3,2,1,0:T(8,128)(2,1)} %bitcast.480), calls=%async_computation.17 | async-start | bytes 2097152 | tf_op jit(solution)/shard_map/all_to_all | solution.py:303
  576.7 29.9 %all-to-all-start.16 = ((bf16[32,1,8,2048]{3,2,1,0:T(8,128)(2,1)}), bf16[32,1,8,2048]{3,2,1,0:T(8,128)(2,1)S(1)}, u32[]{:S(2)}, u32[]{:S(2)}) async-start(bf16[32,1,8,2048]{3,2,1,0:T(8,128)(2,1)} %bitcast.482), calls=%async_computation.16 | async-start | bytes 2097152 | tf_op jit(solution)/shard_map/all_to_all | solution.py:303
  609.4 2.6 copy-start.1
  (3 other events, 3.3 us)
Sparse Core Ops, SparseCore 0:
  101.3 94.5 all-gather.1
  317.8 226.8 reduce-scatter.3
where the time goes:
time: 629 us; the launch traced here: 619 us
  waiting for transfers between devices  237 us (38%)
  local copies, waits for them, and re-layouts  175 us (28%)
  matrix products  88.6 us (14%)
  starting transfers between devices  78.4 us (12%)
  other arithmetic  23.9 us (4%)
  between operations  15.5 us (2%)
    all_to_all x2, waiting for transfers between devices, per_device(): lax.all_to_all(send_values, 'ctx', split_axis=0, concat_axis=0, tiled=True)  46 us
    unnamed x83, local copies, waits for them, and re-layouts  44.6 us
    all_to_all x2, waiting for transfers between devices, per_device(): lax.all_to_all(send_qk, 'ctx', split_axis=0, concat_axis=0, tiled=True)  44.5 us
    all_to_all x2, waiting for transfers between devices, per_device(): lax.all_to_all(jnp.stack(returned_rows, axis=1).astype(jnp.float32), 'ctx...  43.6 us
    all_to_all x2, waiting for transfers between devices, per_device(): lax.all_to_all(jnp.stack(returned_values, axis=1), 'ctx', split_axis=0, c...  29.7 us
    all_to_all x2, waiting for transfers between devices, per_device(): lax.all_to_all(send_grad.astype(jnp.float32), 'ctx', split_axis=0, concat...  27.1 us
    dot_general x4, matrix products, one_block(): jnp.einsum('hqk,qhd->khd', probability.astype(jnp.bfloat16), block_grad,...  25.6 us
    all_to_all x2, waiting for transfers between devices, per_device(): lax.all_to_all(jnp.stack(returned_qk, axis=1), 'ctx', split_axis=0, conca...  23.1 us
  transfers between devices with their start and end apart: 20, of which 15 were waited for; matrix products, arithmetic and copies ran while one was open for 42% of the time, Pallas kernels for 0%

commit v1 on v0

--- a/solution.py
+++ b/solution.py
@@ -3,6 +3,8 @@
 import jax
 import jax.numpy as jnp
 from jax import lax
+from jax.experimental import pallas as pl
+from jax.experimental.pallas import tpu as pltpu
 from jax.sharding import PartitionSpec as P
 
 HEAD_DIM = 128
@@ -130,7 +132,7 @@
     return (source_slot, target)
 
 
-def per_device(shared_qk, values, out_grad, out_weight, buckets):
+def bucket_owner_device(shared_qk, values, out_grad, out_weight, buckets):
     token_rows, row_width = shared_qk.shape
     local_heads = row_width // HEAD_DIM
     peer_count = lax.axis_size("ctx")
@@ -314,6 +316,270 @@
     return (mixed, qk_total.astype(jnp.bfloat16), value_total.astype(jnp.bfloat16), grad_weight)
 
 
+PLANES = 4
+TALL = 256
+VMEM_BYTES = 48 * 1024 * 1024
+
+
+def contract(left, right, left_dim, right_dim):
+    return lax.dot_general(
+        left, right, (((left_dim,), (right_dim,)), ((), ())), preferred_element_type=jnp.float32
+    )
+
+
+def slot_pick(slot_ref, source):
+    slot_ids = lax.broadcasted_iota(jnp.int32, (TALL, SPAN), 0)
+    return (slot_ids == slot_ref[pl.ds(source, 1), :]).astype(jnp.bfloat16)
+
+
+def bucket_scores(rows, code_ref, bucket):
+    scores = contract(rows, rows, 1, 1) * HEAD_DIM ** (-0.5)
+    key_ids = lax.broadcasted_iota(jnp.int32, (TALL, TALL), 0)
+    query_ids = lax.broadcasted_iota(jnp.int32, (TALL, TALL), 1)
+    scores = jnp.where(key_ids == query_ids, scores - self_penalty, scores)
+    code_row = code_ref[pl.ds(bucket, 1), :]
+    code_column = jnp.broadcast_to(code_row, (SPAN, TALL)).T
+    code_column = jnp.concatenate([code_column, code_column], axis=1)
+    seen = (code_column > 0.5) & (code_column <= jnp.maximum(code_row, 1.0))
+    return jnp.where(seen, scores, masked_score)
+
+
+def forward_kernel(mine_ref, other_ref, slot_ref, code_ref, out_ref, log_ref, grouped, results):
+    sources, slots = grouped.shape[0], grouped.shape[1]
+    per_peer = TALL // sources
+    buckets = slots // per_peer
+
+    def group(source, carry):
+        rows = jnp.concatenate([mine_ref[source], other_ref[source]], axis=0)
+        grouped[source] = contract(slot_pick(slot_ref, source), rows, 1, 0)
+        return carry
+
+    lax.fori_loop(0, sources, group, 0, unroll=2)
+
+    def attend(bucket, carry):
+        place = pl.ds(pl.multiple_of(bucket * per_peer, per_peer), per_peer)
+        rows = grouped[:, place, :].reshape(TALL, 2 * HEAD_DIM).astype(jnp.bfloat16)
+        scores = bucket_scores(rows[:, :HEAD_DIM], code_ref, bucket)
+        largest = jnp.max(scores, axis=0, keepdims=True)
+        lifted = jnp.exp(scores - largest)
+        summed = jnp.sum(lifted, axis=0, keepdims=True)
+        probability = (lifted / summed).astype(jnp.bfloat16)
+        result = contract(probability, rows[:, HEAD_DIM:], 0, 0)
+        results[:, place, :] = result.reshape(sources, per_peer, HEAD_DIM)
+        log_ref[pl.ds(bucket, 1), :] = largest + jnp.log(summed)
+        return carry
+
+    lax.fori_loop(0, buckets, attend, 0, unroll=2)
+
+    def scatter(source, carry):
+        rows = results[source].astype(jnp.bfloat16)
+        out_ref[source] = contract(slot_pick(slot_ref, source), rows, 0, 0).astype(jnp.bfloat16)
+        return carry
+
+    lax.fori_loop(0, sources, scatter, 0, unroll=2)
+
+
+def backward_kernel(
+    mine_ref, other_ref, grad_ref, slot_ref, code_ref, log_ref, shift_ref, out_ref, grouped, results
+):
+    sources, slots = grouped.shape[0], grouped.shape[1]
+    per_peer = TALL // sources
+    buckets = slots // per_peer
+    both = 2 * HEAD_DIM
+
+    def group(source, carry):
+        rows = jnp.concatenate([mine_ref[source], other_ref[source]], axis=0)
+        pick = slot_pick(slot_ref, source)
+        grouped[source, :, :both] = contract(pick, rows, 1, 0)
+        grouped[source, :, both:] = contract(pick, grad_ref[source], 1, 0)
+        return carry
+
+    lax.fori_loop(0, sources, group, 0, unroll=2)
+
+    def attend(bucket, carry):
+        place = pl.ds(pl.multiple_of(bucket * per_peer, per_peer), per_peer)
+        rows = grouped[:, place, :].reshape(TALL, 3 * HEAD_DIM).astype(jnp.bfloat16)
+        qk_rows, value_rows, grad_rows = (
+            rows[:, :HEAD_DIM],
+            rows[:, HEAD_DIM:both],
+            rows[:, both:],
+        )
+        scores = bucket_scores(qk_rows, code_ref, bucket)
+        probability = jnp.exp(scores - log_ref[pl.ds(bucket, 1), :])
+        prob_grad = contract(value_rows, grad_rows, 1, 1)
+        score_grad = (probability * (prob_grad - shift_ref[pl.ds(bucket, 1), :])).astype(
+            jnp.bfloat16
+        )
+        qk_grad = contract(score_grad, qk_rows, 0, 0) + contract(score_grad, qk_rows, 1, 0)
+        value_grad = contract(probability.astype(jnp.bfloat16), grad_rows, 1, 0)
+        results[:, place, :HEAD_DIM] = (qk_grad * HEAD_DIM ** (-0.5)).reshape(
+            sources, per_peer, HEAD_DIM
+        )
+        results[:, place, HEAD_DIM:] = value_grad.reshape(sources, per_peer, HEAD_DIM)
+        return carry
+
+    lax.fori_loop(0, buckets, attend, 0, unroll=2)
+
+    def scatter(source, carry):
+        rows = results[source].astype(jnp.bfloat16)
+        out_ref[source] = contract(slot_pick(slot_ref, source), rows, 0, 0).astype(jnp.bfloat16)
+        return carry
+
+    lax.fori_loop(0, sources, scatter, 0, unroll=2)
+
+
+def kernel_call(body, out_shape, scratch_shapes, arguments):
+    return pl.pallas_call(
+        body,
+        out_shape=out_shape,
+        in_specs=[pl.BlockSpec(memory_space=pltpu.VMEM)] * len(arguments),
+        out_specs=jax.tree.map(lambda _: pl.BlockSpec(memory_space=pltpu.VMEM), out_shape),
+        scratch_shapes=scratch_shapes,
+        compiler_params=pltpu.CompilerParams(vmem_limit_bytes=VMEM_BYTES),
+    )(*arguments)
+
+
+def head_owner_device(shared_qk, values, out_grad, out_weight, buckets):
+    token_rows, row_width = shared_qk.shape
+    heads = row_width // HEAD_DIM
+    peers = lax.axis_size("ctx")
+    per_peer = 2 * token_rows // peers
+    half = token_rows // 2
+    slots = peers * per_peer
+    core = lax.axis_index("ctx") % 2
+    first = core == 0
+    partners = [(device, device ^ 1) for device in range(peers)]
+
+    def exchange(block):
+        return lax.ppermute(block, "ctx", partners)
+
+    def swapped(block):
+        return jnp.concatenate([block[:, half:], block[:, :half]], axis=1)
+
+    def everywhere(block):
+        return lax.all_to_all(block, "ctx", split_axis=0, concat_axis=0, tiled=True)
+
+    def by_head(rows):
+        return rows.reshape(2, half, heads, HEAD_DIM).transpose(2, 0, 1, 3)
+
+    def by_token(blocks):
+        return blocks.reshape(heads, 2, half, HEAD_DIM).transpose(1, 2, 0, 3).reshape(
+            token_rows, row_width
+        )
+
+    all_buckets = lax.all_gather(buckets, "ctx", axis=0)
+    whole_weight = lax.all_gather(out_weight, "ctx", axis=0, tiled=True)
+
+    own = jnp.where(first, all_buckets[:, 0], all_buckets[:, 1])
+    order = jnp.arange(token_rows, dtype=jnp.int32)
+    same = (own[:, :, None] == own[:, None, :]) & (order[None, :] < order[:, None])[None]
+    position = jnp.sum(same.astype(jnp.int32), axis=2)
+    slot = own * per_peer + position
+    slot = jnp.where(first, slot, swapped(slot))
+    bucket_ids = jnp.arange(peers, dtype=jnp.int32)
+    counts = jnp.sum((own[:, :, None] == bucket_ids).astype(jnp.int32), axis=1)
+    before = (bucket_ids[None, :] < bucket_ids[:, None]).astype(jnp.int32)
+    starts = jnp.sum(before[:, :, None] * counts[None], axis=1)
+    within = jnp.arange(per_peer, dtype=jnp.int32)
+    live = within < counts[:, :, None]
+    code = jnp.where(live, jnp.where(starts[:, :, None] + within >= SPAN, 2.0, 1.0), 0.0)
+    code = code.astype(jnp.float32).transpose(1, 0, 2).reshape(peers, peers * per_peer)
+
+    sent = jnp.concatenate([by_head(shared_qk), by_head(values)], axis=-1)
+    mine = everywhere(sent.reshape(peers, half, 2 * HEAD_DIM))
+    other = exchange(mine)
+
+    result, log_slots = kernel_call(
+        forward_kernel,
+        (
+            jax.ShapeDtypeStruct((peers, token_rows, HEAD_DIM), jnp.bfloat16),
+            jax.ShapeDtypeStruct((peers, peers * per_peer), jnp.float32),
+        ),
+        [
+            pltpu.VMEM((peers, slots, 2 * HEAD_DIM), jnp.float32),
+            pltpu.VMEM((peers, slots, HEAD_DIM), jnp.float32),
+        ],
+        (mine, other, slot, code),
+    )
+
+    attended_grad = jnp.dot(out_grad, whole_weight, preferred_element_type=jnp.float32).astype(
+        jnp.bfloat16
+    )
+    grad_mine = everywhere(by_head(attended_grad).reshape(peers, half, HEAD_DIM))
+    grad_rows = jnp.concatenate([grad_mine, exchange(grad_mine)], axis=1).astype(jnp.float32)
+
+    chosen = slot[:, :, None] == jnp.arange(slots, dtype=jnp.int32)
+    log_by_source = log_slots.reshape(peers, peers, per_peer).transpose(1, 0, 2).reshape(peers, slots)
+    log_own = jnp.sum(jnp.where(chosen, log_by_source[:, None, :], 0.0), axis=2)
+    log_other = swapped(exchange(log_own))
+    result_other = swapped(exchange(result))
+    largest = jnp.maximum(log_own, log_other)
+    lifted_own, lifted_other = jnp.exp(log_own - largest), jnp.exp(log_other - largest)
+    lifted_sum = lifted_own + lifted_other
+    weight_own, weight_other = lifted_own / lifted_sum, lifted_other / lifted_sum
+    attended = (
+        weight_own[:, :, None] * result.astype(jnp.float32)
+        + weight_other[:, :, None] * result_other.astype(jnp.float32)
+    ).astype(jnp.bfloat16)
+
+    inner = jnp.sum(grad_rows * attended.astype(jnp.float32), axis=-1)
+    shift = weight_own * inner
+    query_grad = (weight_own[:, :, None] * grad_rows).astype(jnp.bfloat16)
+    shift_slots = jnp.sum(jnp.where(chosen, shift[:, :, None], 0.0), axis=1)
+    shift_slots = (
+        shift_slots.reshape(peers, peers, per_peer).transpose(1, 0, 2).reshape(peers, slots)
+    )
+
+    attended_rows = by_token(everywhere(attended[:, :half]))
+
+    grads = kernel_call(
+        backward_kernel,
+        jax.ShapeDtypeStruct((peers, token_rows, 2 * HEAD_DIM), jnp.bfloat16),
+        [
+            pltpu.VMEM((peers, slots, 3 * HEAD_DIM), jnp.float32),
+            pltpu.VMEM((peers, slots, 2 * HEAD_DIM), jnp.float32),
+        ],
+        (mine, other, query_grad, slot, code, log_slots, shift_slots),
+    )
+    grads_other = exchange(grads[:, half:])
+    total = (grads[:, :half].astype(jnp.float32) + grads_other.astype(jnp.float32)).astype(
+        jnp.bfloat16
+    )
+    back = everywhere(total)
+    grad_qk = by_token(back[:, :, :HEAD_DIM])
+    grad_values = by_token(back[:, :, HEAD_DIM:])
+
+    mixed = contract(attended_rows, whole_weight, 1, 1).astype(jnp.bfloat16)
+
+    plane = peers // PLANES
+    groups = [[level * plane + place for place in range(plane)] for level in range(PLANES)]
+    plane_grad = lax.all_gather(out_grad, "ctx", axis=0, tiled=True, axis_index_groups=groups)
+    plane_attended = lax.all_to_all(
+        attended_rows, "ctx", split_axis=1, concat_axis=0, tiled=True, axis_index_groups=groups
+    )
+    partial = contract(plane_grad, plane_attended, 0, 0) * (1.0 / math.sqrt(token_rows * peers))
+    shares = everywhere(
+        partial.astype(jnp.bfloat16).reshape(peers, row_width // peers, row_width // plane)
+    )
+    shares = shares.reshape((PLANES, plane) + shares.shape[1:]).astype(jnp.float32)
+    grad_weight = jnp.sum(shares, axis=0).transpose(1, 0, 2).reshape(-1, row_width)
+    return (mixed, grad_qk, grad_values, grad_weight)
+
+
+def per_device(shared_qk, values, out_grad, out_weight, buckets):
+    token_rows, row_width = shared_qk.shape
+    peers = lax.axis_size("ctx")
+    fits = (
+        lax.axis_size("head") == 1
+        and buckets.shape[0] == 2
+        and peers == 2 * (row_width // HEAD_DIM)
+        and 2 * token_rows == TALL
+        and TALL // peers == 8
+    )
+    whole = head_owner_device if fits else bucket_owner_device
+    return whole(shared_qk, values, out_grad, out_weight, buckets)
+
+
 def solution(mesh):
     in_specs = (
         P("ctx", "head"),

time: 629 us -> 256 us (0.41); the launches traced: 619 us -> 255 us
  waiting for transfers between devices: 237 us -> 64.5 us
  local copies, waits for them, and re-layouts: 175 us -> 17.7 us
  matrix products: 88.6 us -> 15.3 us
  blocking collectives: 0 us -> 57.2 us
  starting transfers between devices: 78.4 us -> 29.8 us
  Pallas kernels: 0 us -> 42.6 us
  other arithmetic: 23.9 us -> 13 us
    all_to_all x18 -> x6, waiting for transfers between devices: 237 us -> 44.5 us  [the longest x5 37.4 us: everywhere(): return lax.all_to_all(block, 'ctx', split_axis=0, concat_axis=0, tiled=True)]
    dot_general x27 -> x3, matrix products: 74.9 us -> 15.3 us  [the longest x2 10.7 us: contract(): lax.dot_general(left, right, (((left_dim,), (right_dim,)), ((), ())), pre...]
    all_gather x0 -> x1, blocking collectives: none -> 57.2 us  [head_owner_device(): all_buckets = lax.all_gather(buckets, 'ctx', axis=0)]
    gather x32 -> x0, local copies, waits for them, and re-layouts: 53 us -> none  [the longest x8 15.6 us: outgoing(): matrix[routes[round_index][1]]]
    all_to_all x18 -> x6, starting transfers between devices: 78.1 us -> 28.4 us  [the longest x5 24.2 us: everywhere(): return lax.all_to_all(block, 'ctx', split_axis=0, concat_axis=0, tiled=True)]
    pallas_call x0 -> x2, Pallas kernels: none -> 42.6 us  [kernel_call(): pl.pallas_call(body, out_shape=out_shape, in_specs=[pl.BlockSpec(memory_s...]
    unnamed x83 -> x15, local copies, waits for them, and re-layouts: 44.6 us -> 6.74 us
    all_gather x1 -> x2, waiting for transfers between devices: 0.02 us -> 17.9 us  [the longest x1 17.9 us: head_owner_device(): whole_weight = lax.all_gather(out_weight, 'ctx', axis=0, tiled=True)]
  transfers between devices with their start and end apart: 20 -> 13, of which waited for: 15 -> 5; matrix products, arithmetic and copies ran while one was open for 42% -> 17% of each run, Pallas kernels for 0% -> 17%
where the time goes in v1:
time: 256 us; the launch traced here: 255 us
  waiting for transfers between devices  64.5 us (25%)
  blocking collectives  57.2 us (22%)
  Pallas kernels  42.6 us (17%)
  starting transfers between devices  29.8 us (12%)
  local copies, waits for them, and re-layouts  17.7 us (7%)
  matrix products  15.3 us (6%)
  between operations  14.4 us (6%)
  other arithmetic  13 us (5%)
    all_gather x1, blocking collectives, head_owner_device(): all_buckets = lax.all_gather(buckets, 'ctx', axis=0)  57.2 us
    pallas_call x2, Pallas kernels, kernel_call(): pl.pallas_call(body, out_shape=out_shape, in_specs=[pl.BlockSpec(memory_s...  42.6 us
    all_to_all x5, waiting for transfers between devices, everywhere(): return lax.all_to_all(block, 'ctx', split_axis=0, concat_axis=0, tiled=True)  37.4 us
    all_to_all x5, starting transfers between devices, everywhere(): return lax.all_to_all(block, 'ctx', split_axis=0, concat_axis=0, tiled=True)  24.2 us
    all_gather x1, waiting for transfers between devices, head_owner_device(): whole_weight = lax.all_gather(out_weight, 'ctx', axis=0, tiled=True)  17.9 us
    dot_general x2, matrix products, contract(): lax.dot_general(left, right, (((left_dim,), (right_dim,)), ((), ())), pre...  10.7 us
    all_to_all x1, waiting for transfers between devices, head_owner_device(): lax.all_to_all(attended_rows, 'ctx', split_axis=1, concat_axis=0, tiled=T...  7.19 us
    unnamed x15, local copies, waits for them, and re-layouts  6.74 us
  transfers between devices with their start and end apart: 13, of which 5 were waited for; matrix products, arithmetic and copies ran while one was open for 17% of the time, Pallas kernels for 17%

profile of v1, /device:TPU:0, one launch (start us, length us, event | category | flops | bytes accessed | tf_op | source)
XLA Modules:
  0.0 254.7 jit_solution(1482238951785572351)
XLA Ops:
  7.2 0.7 all-gather.5.cloned.1.call-update
  7.9 1.1 copy.87
  9.1 1.1 copy.88
  10.2 0.3 copy_bitcast_fusion.2
  10.5 1.2 pad_maximum_fusion
  11.7 7.3 %all-to-all-start = ((bf16[32,64,256]{2,1,0:T(8,128)(2,1)}), bf16[32,64,256]{2,1,0:T(8,128)(2,1)S(1)}, u32[]{:S(2)}, u32[]{:S(2)}) async-start(bf16[32,64,256]{2,1,0:T(8,128)(2,1)} %bitcast.4), calls=%async_computation | async-start | bytes 2097152 | tf_op jit(solution)/shard_map/all_to_all | solution.py:460
  19.0 0.7 all-gather.7.cloned.1.call-update
  19.8 57.2 %all-gather.1 = s32[32,2,128]{2,1,0:T(2,128)S(1)} all-gather(s32[1,2,128]{2,1,0:T(2,128)S(1)} %bitcast.104), channel_id=2, replica_groups=mesh['ctx'=32,'head'=1] {'ctx'}, dimensions={0}, use_global_device_ids=true | all-gather | bytes 33792 | tf_op jit(solution)/shard_map/all_gather | solution.py:470
  77.1 0.6 convert_reduce_fusion.2
  77.7 0.2 multiply_reduce_fusion
  77.9 1.3 convert_reduce_fusion.1
  79.3 0.4 collective-permute-start
  79.7 0.1 fusion.14
  79.8 0.1 copy.69
  79.9 0.1 lt.74
  80.0 17.9 %all-gather.5.cloned.1.call-done = bf16[2048,2048]{1,0:T(8,128)(2,1)} async-done(((bf16[64,2048]{1,0:T(8,128)(2,1)}), bf16[2048,2048]{1,0:T(8,128)(2,1)}) %all-gather.5.cloned.1.call-update) | async-done | bytes 8388624 | tf_op jit(solution)/shard_map/all_gather | solution.py:471
  97.9 4.6 %fusion.4 = bf16[16,8,16,128]{3,1,2,0:T(8,128)(2,1)S(1)} fusion(bf16[128,2048]{1,0:T(8,128)(2,1)S(1)} %copy-done.3, bf16[2048,2048]{1,0:T(8,128)(2,1)} %all-gather.5.cloned.1.call-done), kind=kOutput, calls=%fused_computation.16 | convolution fusion | flops 1074003968 | bytes 9437184 | tf_op jit(solution)/shard_map/dot_general | solution.py:505
  102.6 0.1 copy.90
  102.7 0.9 copy.75
  103.6 3.4 %all-to-all-start.2 = ((bf16[32,64,128]{2,1,0:T(8,128)(2,1)}), bf16[32,64,128]{2,1,0:T(8,128)(2,1)}, u32[]{:S(2)}, u32[]{:S(2)}) async-start(bf16[32,64,128]{2,1,0:T(8,128)(2,1)} %bitcast.15), calls=%async_computation.2 | async-start | bytes 1048576 | tf_op jit(solution)/shard_map/all_to_all | solution.py:460
  107.0 0.1 add_select_fusion.slot_ref
  107.1 21.5 %shard_map.84 = (bf16[32,128,128]{2,1,0:T(8,128)(2,1)S(1)}, f32[32,256]{1,0:T(8,128)S(1)}) custom-call(bf16[32,64,256]{2,1,0:T(8,128)(2,1)S(1)} %all-to-all-done.mine_ref, bf16[32,64,256]{2,1,0:T(8,128)(2,1)S(1)} %collective-permute-done.other_ref, s32[32,128]{1,0:T(8,128)S(1)} %add_select_fusion.slot_ref, f32[32,256]{1,0:T(8,128)S(1)} %select_select_fusion.code_ref), custom_call_target="tpu_custom_call" | custom-call | tf_op jit(solution)/shard_map/pallas_call | solution.py:432
  128.6 0.2 collective-permute-start.2
  128.9 0.1 copy.71
  129.0 0.1 copy.72
  129.1 0.1 copy.73
  129.2 1.4 select_reduce_fusion.1
  130.6 0.4 collective-permute-start.1
  131.0 0.2 collective-permute-start.3
  131.1 0.7 collective-permute-done.1
  131.8 0.1 fusion.13
  131.9 0.1 add_divide_fusion.1
  132.0 1.3 fusion.11
  133.3 4.0 %fusion.3 = (f32[32,128]{1,0:T(8,128)S(1)}, bf16[32,128,128]{2,1,0:T(8,128)(2,1)S(1)}, bf16[32,128,128]{2,1,0:T(8,128)(2,1)}) fusion(bf16[32,64,128]{2,1,0:T(8,128)(2,1)S(1)} %collective-permute-done.3, bf16[32,64,128]{2,1,0:T(8,128)(2,1)} %all-to-all-done.2, bf16[32,64,128]{2,1,0:T(8,128)(2,1)S(1)} %get-tuple-element.14, ...), kind=kLoop, calls=%fused_computation.11 | loop fusion | flops 9433088 | bytes 5292032 | tf_op jit(solution)/shard_map/reduce_sum | solution.py:525
  137.3 0.8 slice.60
  138.2 5.9 %all-to-all-start.1 = ((bf16[32,64,128]{2,1,0:T(8,128)(2,1)}), bf16[32,64,128]{2,1,0:T(8,128)(2,1)}, u32[]{:S(2)}, u32[]{:S(2)}) async-start(bf16[32,64,128]{2,1,0:T(8,128)(2,1)} %slice.60), calls=%async_computation.1 | async-start | bytes 1048576 | tf_op jit(solution)/shard_map/all_to_all | solution.py:460
  144.1 1.4 select_reduce_fusion
  145.5 0.1 copy.76
  145.6 0.1 copy.77
  145.8 1.2 copy-done
  147.0 1.2 copy-done.2
  148.2 21.0 %shard_map.85 = bf16[32,128,256]{2,1,0:T(8,128)(2,1)S(1)} custom-call(bf16[32,64,256]{2,1,0:T(8,128)(2,1)S(1)} %all-to-all-done.mine_ref, bf16[32,64,256]{2,1,0:T(8,128)(2,1)S(1)} %copy-done.2, bf16[32,128,128]{2,1,0:T(8,128)(2,1)S(1)} %copy-done, s32[32,128]{1,0:T(8,128)S(1)} %add_select_fusion.slot_ref, f32[32,256]{1,0:T(8,128)S(1)} %select_select_fusion.code_ref, ...), custom_call_target="tpu_custom_call" | custom-call | tf_op jit(solution)/shard_map/pallas_call | solution.py:432
  169.3 1.0 slice.62
  170.3 0.2 collective-permute-start.4
  170.5 1.4 copy.105
  171.9 0.2 all_to_all.33
  172.1 0.9 copy.81
  173.0 4.1 %all-to-all-start.4 = ((bf16[128,8,256]{2,0,1:T(8,128)(2,1)}), bf16[128,8,256]{2,0,1:T(8,128)(2,1)}, u32[]{:S(2)}, u32[]{:S(2)}) async-start(bf16[128,8,256]{2,0,1:T(8,128)(2,1)} %copy.81), calls=%async_computation.4 | async-start | bytes 1048576 | tf_op jit(solution)/shard_map/all_to_all | solution.py:557
  177.1 2.6 %add_convert_fusion = bf16[32,64,256]{2,1,0:T(8,128)(2,1)} fusion(bf16[32,64,256]{2,1,0:T(8,128)(2,1)} %collective-permute-done.4, bf16[32,128,256]{2,1,0:T(8,128)(2,1)S(1)} %shard_map.85), kind=kLoop, calls=%fused_computation.13 | loop fusion | flops 2097152 | bytes 3145728 | tf_op jit(solution)/shard_map/convert_element_type | solution.py:545
  179.7 7.2 %all-to-all-done.4 = bf16[128,8,256]{2,0,1:T(8,128)(2,1)} async-done(((bf16[128,8,256]{2,0,1:T(8,128)(2,1)}), bf16[128,8,256]{2,0,1:T(8,128)(2,1)}, u32[]{:S(2)}, u32[]{:S(2)}) %all-to-all-start.4) | async-done | bytes 524320 | tf_op jit(solution)/shard_map/all_to_all | solution.py:557
  186.9 3.9 %all-to-all-start.3 = ((bf16[32,64,256]{2,1,0:T(8,128)(2,1)}), bf16[32,64,256]{2,1,0:T(8,128)(2,1)S(1)}, u32[]{:S(2)}, u32[]{:S(2)}) async-start(bf16[32,64,256]{2,1,0:T(8,128)(2,1)} %add_convert_fusion), calls=%async_computation.3 | async-start | bytes 2097152 | tf_op jit(solution)/shard_map/all_to_all | solution.py:460
  190.8 3.6 %fusion.1 = bf16[2048,256]{0,1:T(8,128)(2,1)S(1)} fusion(bf16[1024,256]{1,0:T(8,128)(2,1)} %bitcast.24, bf16[1024,2048]{1,0:T(8,128)(2,1)} %all-gather.7.cloned.1.call-done), kind=kOutput, calls=%fused_computation.7 | convolution fusion | flops 1074790400 | bytes 5767168 | tf_op jit(solution)/shard_map/dot_general | solution.py:325
  194.4 1.4 copy.82
  195.8 21.2 %all-to-all-done.3 = bf16[32,64,256]{2,1,0:T(8,128)(2,1)S(1)} async-done(((bf16[32,64,256]{2,1,0:T(8,128)(2,1)}), bf16[32,64,256]{2,1,0:T(8,128)(2,1)S(1)}, u32[]{:S(2)}, u32[]{:S(2)}) %all-to-all-start.3) | async-done | bytes 1048608 | tf_op jit(solution)/shard_map/all_to_all | solution.py:460
  217.0 3.8 %all-to-all-start.5 = ((bf16[32,64,256]{2,1,0:T(8,128)(2,1)}), bf16[32,64,256]{2,1,0:T(8,128)(2,1)S(1)}, u32[]{:S(2)}, u32[]{:S(2)}) async-start(bf16[32,64,256]{2,1,0:T(8,128)(2,1)} %bitcast.26), calls=%async_computation.5 | async-start | bytes 2097152 | tf_op jit(solution)/shard_map/all_to_all | solution.py:460
  220.8 7.1 %convolution_convert_fusion.1 = bf16[128,2048]{1,0:T(8,128)(2,1)} fusion(bf16[2048,2048]{1,0:T(8,128)(2,1)} %all-gather.5.cloned.1.call-done, bf16[16,8,16,128]{3,2,1,0:T(8,128)(2,1)S(1)} %bitcast.81), kind=kOutput, calls=%fused_computation.9 | convolution fusion | flops 1074003968 | bytes 9437184 | tf_op jit(solution)/shard_map/dot_general | solution.py:325
  227.9 0.3 fusion.10
  228.2 0.3 copy.80
  228.5 0.9 copy.103
  229.4 0.3 copy.79
  229.8 0.9 copy.104
  230.7 16.1 %all-to-all-done.5 = bf16[32,64,256]{2,1,0:T(8,128)(2,1)S(1)} async-done(((bf16[32,64,256]{2,1,0:T(8,128)(2,1)}), bf16[32,64,256]{2,1,0:T(8,128)(2,1)S(1)}, u32[]{:S(2)}, u32[]{:S(2)}) %all-to-all-start.5) | async-done | bytes 1048608 | tf_op jit(solution)/shard_map/all_to_all | solution.py:460
  246.9 0.2 convert_reduce_fusion
  247.0 0.8 copy.86
  (30 shorter events, 0.4 us)
Async XLA Ops:
  7.2 90.8 %all-gather.5.cloned.1.call-start = ((), (), s32[]{:S(2)}) async-start(), calls=%async_computation.6 | async-start | bytes 8650752 | tf_op jit(solution)/shard_map/all_gather | solution.py:471
  10.5 9.3 %copy-start.4 = (s32[2,128]{1,0:T(2,128)S(1)}, s32[2,128]{1,0:T(2,128)}, u32[]{:S(2)}) copy-start(s32[2,128]{1,0:T(2,128)} %param.9) | copy-start | bytes 3076
  11.7 86.2 %copy-start.3 = (bf16[128,2048]{1,0:T(8,128)(2,1)S(1)}, bf16[128,2048]{1,0:T(8,128)(2,1)}, u32[]{:S(2)}) copy-start(bf16[128,2048]{1,0:T(8,128)(2,1)} %param.7) | copy-start | bytes 1572868
  11.7 67.6 %all-to-all-start = ((bf16[32,64,256]{2,1,0:T(8,128)(2,1)}), bf16[32,64,256]{2,1,0:T(8,128)(2,1)S(1)}, u32[]{:S(2)}, u32[]{:S(2)}) async-start(bf16[32,64,256]{2,1,0:T(8,128)(2,1)} %bitcast.4), calls=%async_computation | async-start | bytes 2097152 | tf_op jit(solution)/shard_map/all_to_all | solution.py:460
  19.0 171.8 %all-gather.7.cloned.1.call-start = ((), (), s32[]{:S(2)}) async-start(), calls=%async_computation.7 | async-start | bytes 4718592 | tf_op jit(solution)/shard_map/all_gather | solution.py:556
  79.3 27.8 %collective-permute-start = (bf16[32,64,256]{2,1,0:T(8,128)(2,1)S(1)}, bf16[32,64,256]{2,1,0:T(8,128)(2,1)S(1)}, u32[]{:S(2)}, u32[]{:S(2)}) collective-permute-start(bf16[32,64,256]{2,1,0:T(8,128)(2,1)S(1)} %all-to-all-done.mine_ref), channel_id=1, source_target_pairs={{0,1},{1,0},{2,3},{3,2},{4,5},{5,4},{6,7},{7,6},{8,9},{9,8},{10,11... | collective-permute-start | bytes 3145736 | tf_op jit(solution)/shard_map/ppermute | solution.py:454
  103.6 27.3 %all-to-all-start.2 = ((bf16[32,64,128]{2,1,0:T(8,128)(2,1)}), bf16[32,64,128]{2,1,0:T(8,128)(2,1)}, u32[]{:S(2)}, u32[]{:S(2)}) async-start(bf16[32,64,128]{2,1,0:T(8,128)(2,1)} %bitcast.15), calls=%async_computation.2 | async-start | bytes 1048576 | tf_op jit(solution)/shard_map/all_to_all | solution.py:460
  107.1 26.2 %copy-start.1 = (bf16[32,64,256]{2,1,0:T(8,128)(2,1)}, bf16[32,64,256]{2,1,0:T(8,128)(2,1)S(1)}, u32[]{:S(2)}) copy-start(bf16[32,64,256]{2,1,0:T(8,128)(2,1)S(1)} %collective-permute-done.other_ref) | copy-start | bytes 3145732
  128.6 3.3 %collective-permute-start.2 = (bf16[32,128,128]{2,1,0:T(8,128)(2,1)S(1)}, bf16[32,128,128]{2,1,0:T(8,128)(2,1)}, u32[]{:S(2)}, u32[]{:S(2)}) collective-permute-start(bf16[32,128,128]{2,1,0:T(8,128)(2,1)S(1)} %get-tuple-element.7), channel_id=1, source_target_pairs={{0,1},{1,0},{2,3},{3,2},{4,5},{5,4},{6,7},{7,6},{8,9},{9,8},{10,11... | collective-permute-start | bytes 3145736 | tf_op jit(solution)/shard_map/ppermute | solution.py:454
  130.6 1.2 collective-permute-start.1
  131.0 2.3 collective-permute-start.3
  138.2 32.3 %all-to-all-start.1 = ((bf16[32,64,128]{2,1,0:T(8,128)(2,1)}), bf16[32,64,128]{2,1,0:T(8,128)(2,1)}, u32[]{:S(2)}, u32[]{:S(2)}) async-start(bf16[32,64,128]{2,1,0:T(8,128)(2,1)} %slice.60), calls=%async_computation.1 | async-start | bytes 1048576 | tf_op jit(solution)/shard_map/all_to_all | solution.py:460
  145.8 1.2 copy-start
  147.0 1.2 copy-start.2
  170.3 6.8 %collective-permute-start.4 = (bf16[32,64,256]{2,1,0:T(8,128)(2,1)}, bf16[32,64,256]{2,1,0:T(8,128)(2,1)}, u32[]{:S(2)}, u32[]{:S(2)}) collective-permute-start(bf16[32,64,256]{2,1,0:T(8,128)(2,1)} %slice.62), channel_id=1, source_target_pairs={{0,1},{1,0},{2,3},{3,2},{4,5},{5,4},{6,7},{7,6},{8,9},{9,8},{10,11... | collective-permute-start | bytes 3145736 | tf_op jit(solution)/shard_map/ppermute | solution.py:454
  173.0 13.9 %all-to-all-start.4 = ((bf16[128,8,256]{2,0,1:T(8,128)(2,1)}), bf16[128,8,256]{2,0,1:T(8,128)(2,1)}, u32[]{:S(2)}, u32[]{:S(2)}) async-start(bf16[128,8,256]{2,0,1:T(8,128)(2,1)} %copy.81), calls=%async_computation.4 | async-start | bytes 1048576 | tf_op jit(solution)/shard_map/all_to_all | solution.py:557
  186.9 30.1 %all-to-all-start.3 = ((bf16[32,64,256]{2,1,0:T(8,128)(2,1)}), bf16[32,64,256]{2,1,0:T(8,128)(2,1)S(1)}, u32[]{:S(2)}, u32[]{:S(2)}) async-start(bf16[32,64,256]{2,1,0:T(8,128)(2,1)} %add_convert_fusion), calls=%async_computation.3 | async-start | bytes 2097152 | tf_op jit(solution)/shard_map/all_to_all | solution.py:460
  217.0 29.9 %all-to-all-start.5 = ((bf16[32,64,256]{2,1,0:T(8,128)(2,1)}), bf16[32,64,256]{2,1,0:T(8,128)(2,1)S(1)}, u32[]{:S(2)}, u32[]{:S(2)}) async-start(bf16[32,64,256]{2,1,0:T(8,128)(2,1)} %bitcast.26), calls=%async_computation.5 | async-start | bytes 2097152 | tf_op jit(solution)/shard_map/all_to_all | solution.py:460
Sparse Core Ops, SparseCore 0:
  10.9 87.0 all-gather.4
  99.8 41.1 all-gather.6

commit v2 on v1

--- a/solution.py
+++ b/solution.py
@@ -318,6 +318,7 @@
 
 PLANES = 4
 TALL = 256
+HALF = 64
 VMEM_BYTES = 48 * 1024 * 1024
 
 
@@ -350,7 +351,7 @@
     buckets = slots // per_peer
 
     def group(source, carry):
-        rows = jnp.concatenate([mine_ref[source], other_ref[source]], axis=0)
+        rows = jnp.concatenate([mine_ref[source, :HALF], other_ref[source]], axis=0)
         grouped[source] = contract(slot_pick(slot_ref, source), rows, 1, 0)
         return carry
 
@@ -388,7 +389,7 @@
     both = 2 * HEAD_DIM
 
     def group(source, carry):
-        rows = jnp.concatenate([mine_ref[source], other_ref[source]], axis=0)
+        rows = jnp.concatenate([mine_ref[source, :HALF], other_ref[source]], axis=0)
         pick = slot_pick(slot_ref, source)
         grouped[source, :, :both] = contract(pick, rows, 1, 0)
         grouped[source, :, both:] = contract(pick, grad_ref[source], 1, 0)
@@ -467,9 +468,36 @@
             token_rows, row_width
         )
 
-    all_buckets = lax.all_gather(buckets, "ctx", axis=0)
-    whole_weight = lax.all_gather(out_weight, "ctx", axis=0, tiled=True)
-
+    def own_half(rows):
+        parted = rows.reshape(rows.shape[0], heads, 2, -1)
+        even, odd = parted[:, :, 0], parted[:, :, 1]
+        kept, passed = jnp.where(first, even, odd), jnp.where(first, odd, even)
+        return kept.reshape(rows.shape[0], -1), passed.reshape(rows.shape[0], -1)
+
+    def moved(block, mask):
+        return lax.ppermute(block, "ctx", [(device, device ^ mask) for device in range(peers)])
+
+    half_weight = lax.all_gather(
+        out_weight,
+        "ctx",
+        axis=0,
+        tiled=True,
+        axis_index_groups=[list(range(0, peers, 2)), list(range(1, peers, 2))],
+    )
+
+    tag = jnp.pad(buckets.astype(jnp.bfloat16).reshape(1, -1), ((0, 7), (0, 0)))
+    sent = jnp.concatenate([by_head(shared_qk), by_head(values)], axis=-1)
+    sent = jnp.concatenate(
+        [
+            sent.reshape(peers, half, 2 * HEAD_DIM),
+            jnp.broadcast_to(tag[None], (peers, 8, 2 * HEAD_DIM)),
+        ],
+        axis=1,
+    )
+    mine = everywhere(sent)
+    other = exchange(mine[:, :half])
+
+    all_buckets = mine[:, half].astype(jnp.int32).reshape(peers, 2, token_rows)
     own = jnp.where(first, all_buckets[:, 0], all_buckets[:, 1])
     order = jnp.arange(token_rows, dtype=jnp.int32)
     same = (own[:, :, None] == own[:, None, :]) & (order[None, :] < order[:, None])[None]
@@ -485,10 +513,6 @@
     code = jnp.where(live, jnp.where(starts[:, :, None] + within >= SPAN, 2.0, 1.0), 0.0)
     code = code.astype(jnp.float32).transpose(1, 0, 2).reshape(peers, peers * per_peer)
 
-    sent = jnp.concatenate([by_head(shared_qk), by_head(values)], axis=-1)
-    mine = everywhere(sent.reshape(peers, half, 2 * HEAD_DIM))
-    other = exchange(mine)
-
     result, log_slots = kernel_call(
         forward_kernel,
         (
@@ -502,7 +526,10 @@
         (mine, other, slot, code),
     )
 
-    attended_grad = jnp.dot(out_grad, whole_weight, preferred_element_type=jnp.float32).astype(
+    grad_kept, grad_passed = own_half(out_grad)
+    grad_pair = jnp.concatenate([grad_kept, exchange(grad_passed)], axis=0)
+    grad_part = jnp.dot(grad_pair, half_weight, preferred_element_type=jnp.float32)
+    attended_grad = (grad_part[:token_rows] + exchange(grad_part[token_rows:])).astype(
         jnp.bfloat16
     )
     grad_mine = everywhere(by_head(attended_grad).reshape(peers, half, HEAD_DIM))
@@ -532,6 +559,46 @@
 
     attended_rows = by_token(everywhere(attended[:, :half]))
 
+    attended_pair = jnp.concatenate([attended_rows, exchange(attended_rows)], axis=0)
+    mixed_part = contract(attended_pair, half_weight, 1, 1).astype(jnp.bfloat16)
+    mixed_kept, mixed_got = mixed_part[:token_rows], exchange(mixed_part[token_rows:])
+    mixed_even = jnp.where(first, mixed_kept, mixed_got).reshape(token_rows, heads, 1, -1)
+    mixed_odd = jnp.where(first, mixed_got, mixed_kept).reshape(token_rows, heads, 1, -1)
+    mixed = jnp.concatenate([mixed_even, mixed_odd], axis=2).reshape(token_rows, row_width)
+
+    plane = peers // PLANES
+    groups = [[level * plane + place for place in range(plane)] for level in range(PLANES)]
+    plane_attended = lax.all_to_all(
+        attended_rows, "ctx", split_axis=1, concat_axis=0, tiled=True, axis_index_groups=groups
+    ).reshape(plane, token_rows, row_width // plane)
+    here = lax.axis_index("ctx") % plane
+    plane_attended = jnp.concatenate(
+        [
+            lax.dynamic_index_in_dim(plane_attended, here ^ mask, axis=0, keepdims=False)
+            for mask in (0, 2, 4, 6, 1, 3, 5, 7)
+        ],
+        axis=0,
+    )
+    left, right = out_grad[:, : row_width // 2], out_grad[:, row_width // 2 :]
+    left_two = jnp.concatenate([left, moved(left, 2)], axis=0)
+    right_x = moved(right, 4)
+    right_two = jnp.concatenate([right, right_x], axis=0)
+    left_four = jnp.concatenate([left_two, moved(left_two, 4)], axis=0)
+    right_far = moved(right_two, 2)
+    right_four = jnp.concatenate(
+        [right, right_far[:token_rows], right_x, right_far[token_rows:]], axis=0
+    )
+    core_grad = jnp.concatenate([left_four, right_four], axis=1)
+    plane_grad = jnp.concatenate([core_grad, exchange(core_grad)], axis=0)
+    partial = contract(plane_grad, plane_attended, 0, 0) * (1.0 / math.sqrt(token_rows * peers))
+    partial = partial.astype(jnp.bfloat16).reshape(
+        peers, row_width // peers, row_width // plane
+    )
+    query_grad, partial = lax.optimization_barrier((query_grad, partial))
+    shares = everywhere(partial)
+    shares = shares.reshape((PLANES, plane) + shares.shape[1:]).astype(jnp.float32)
+    grad_weight = jnp.sum(shares, axis=0).transpose(1, 0, 2).reshape(-1, row_width)
+
     grads = kernel_call(
         backward_kernel,
         jax.ShapeDtypeStruct((peers, token_rows, 2 * HEAD_DIM), jnp.bfloat16),
@@ -549,20 +616,6 @@
     grad_qk = by_token(back[:, :, :HEAD_DIM])
     grad_values = by_token(back[:, :, HEAD_DIM:])
 
-    mixed = contract(attended_rows, whole_weight, 1, 1).astype(jnp.bfloat16)
-
-    plane = peers // PLANES
-    groups = [[level * plane + place for place in range(plane)] for level in range(PLANES)]
-    plane_grad = lax.all_gather(out_grad, "ctx", axis=0, tiled=True, axis_index_groups=groups)
-    plane_attended = lax.all_to_all(
-        attended_rows, "ctx", split_axis=1, concat_axis=0, tiled=True, axis_index_groups=groups
-    )
-    partial = contract(plane_grad, plane_attended, 0, 0) * (1.0 / math.sqrt(token_rows * peers))
-    shares = everywhere(
-        partial.astype(jnp.bfloat16).reshape(peers, row_width // peers, row_width // plane)
-    )
-    shares = shares.reshape((PLANES, plane) + shares.shape[1:]).astype(jnp.float32)
-    grad_weight = jnp.sum(shares, axis=0).transpose(1, 0, 2).reshape(-1, row_width)
     return (mixed, grad_qk, grad_values, grad_weight)
 
 

time: 256 us -> 284 us (1.11)
  blocking collectives: 57.2 us -> 0 us
  waiting for transfers between devices: 64.5 us -> 119 us
  local copies, waits for them, and re-layouts: 17.7 us -> 35.1 us
  other arithmetic: 13 us -> 22.2 us
  starting transfers between devices: 29.8 us -> 37.7 us
  matrix products: 15.3 us -> 11.6 us
    all_gather x1 -> x0, blocking collectives: 57.2 us -> none  [head_owner_device(): all_buckets = lax.all_gather(buckets, 'ctx', axis=0)]
    all_gather x2 -> x1, waiting for transfers between devices: 17.9 us -> 43.2 us  [head_owner_device(): lax.all_gather(out_weight, 'ctx', axis=0, tiled=True, axis_index_groups=[...]
    ppermute x0 -> x4, waiting for transfers between devices: none -> 13 us  [moved(): lax.ppermute(block, 'ctx', [(device, device ^ mask) for device in range(p...]
    all_to_all x5, waiting for transfers between devices: 37.4 us -> 46.3 us  [everywhere(): return lax.all_to_all(block, 'ctx', split_axis=0, concat_axis=0, tiled=True)]
    concatenate x0 -> x5, other arithmetic: none -> 7.21 us  [the longest x1 3.12 us: head_owner_device(): core_grad = jnp.concatenate([left_four, right_four], axis=1)]
    ppermute x0 -> x4, starting transfers between devices: none -> 7.16 us  [moved(): lax.ppermute(block, 'ctx', [(device, device ^ mask) for device in range(p...]
    unnamed x15 -> x28, local copies, waits for them, and re-layouts: 6.74 us -> 13 us
    ppermute x5 -> x10, waiting for transfers between devices: 0.68 us -> 5.87 us  [exchange(): return lax.ppermute(block, 'ctx', partners)]
  transfers between devices with their start and end apart: 13 -> 21, of which waited for: 5 -> 10; matrix products, arithmetic and copies ran while one was open for 17% -> 21% of each run, Pallas kernels for 17% -> 15%
where the time goes in v2:
time: 284 us; the launch traced here: 283 us
  waiting for transfers between devices  119 us (42%)
  Pallas kernels  42.5 us (15%)
  starting transfers between devices  37.7 us (13%)
  local copies, waits for them, and re-layouts  35.1 us (12%)
  other arithmetic  22.2 us (8%)
  between operations  14.6 us (5%)
  matrix products  11.6 us (4%)
    all_to_all x5, waiting for transfers between devices, everywhere(): return lax.all_to_all(block, 'ctx', split_axis=0, concat_axis=0, tiled=True)  46.3 us
    all_gather x1, waiting for transfers between devices, head_owner_device(): lax.all_gather(out_weight, 'ctx', axis=0, tiled=True, axis_index_groups=[...  43.2 us
    pallas_call x2, Pallas kernels, kernel_call(): pl.pallas_call(body, out_shape=out_shape, in_specs=[pl.BlockSpec(memory_s...  42.5 us
    all_to_all x5, starting transfers between devices, everywhere(): return lax.all_to_all(block, 'ctx', split_axis=0, concat_axis=0, tiled=True)  24.6 us
    ppermute x4, waiting for transfers between devices, moved(): lax.ppermute(block, 'ctx', [(device, device ^ mask) for device in range(p...  13 us
    unnamed x28, local copies, waits for them, and re-layouts  13 us
    all_to_all x1, waiting for transfers between devices, head_owner_device(): lax.all_to_all(attended_rows, 'ctx', split_axis=1, concat_axis=0, tiled=T...  9.7 us
    dot_general x2, matrix products, contract(): lax.dot_general(left, right, (((left_dim,), (right_dim,)), ((), ())), pre...  8.02 us
  transfers between devices with their start and end apart: 21, of which 10 were waited for; matrix products, arithmetic and copies ran while one was open for 21% of the time, Pallas kernels for 15%

profile of v2, /device:TPU:0, one launch (start us, length us, event | category | flops | bytes accessed | tf_op | source)
XLA Modules:
  0.0 282.5 jit_solution(13836572882549844960)
XLA Ops:
  8.6 1.1 copy.106
  9.7 1.1 copy.105
  11.4 1.2 pad_maximum_fusion
  12.5 7.3 %all-to-all-start = ((bf16[32,72,256]{2,1,0:T(8,128)(2,1)}), bf16[32,72,256]{2,1,0:T(8,128)(2,1)S(1)}, u32[]{:S(2)}, u32[]{:S(2)}) async-start(bf16[32,72,256]{2,1,0:T(8,128)(2,1)} %pad_maximum_fusion), calls=%async_computation | async-start | bytes 2359296 | tf_op jit(solution)/shard_map/all_to_all | solution.py:461
  20.6 1.8 collective-permute-start.10
  22.7 0.8 broadcast_select_fusion.1
  23.5 1.5 collective-permute-start.8
  25.1 13.0 %collective-permute-done.10 = bf16[128,1024]{1,0:T(8,128)(2,1)S(1)} collective-permute-done((bf16[128,1024]{1,0:T(8,128)(2,1)S(1)}, bf16[128,1024]{1,0:T(8,128)(2,1)S(1)}, u32[]{:S(2)}, u32[]{:S(2)}) %collective-permute-start.10) | collective-permute-done | bytes 262176 | tf_op jit(solution)/shard_map/ppermute | solution.py:478
  38.1 0.9 pad_maximum_fusion.5
  39.0 2.2 collective-permute-start.11
  41.2 18.9 %all-to-all-done.mine_ref = bf16[32,72,256]{2,1,0:T(8,128)(2,1)S(1)} async-done(((bf16[32,72,256]{2,1,0:T(8,128)(2,1)}), bf16[32,72,256]{2,1,0:T(8,128)(2,1)S(1)}, u32[]{:S(2)}, u32[]{:S(2)}) %all-to-all-start) | async-done | bytes 1179680 | tf_op jit(solution)/shard_map/all_to_all | solution.py:461
  61.2 43.2 %all-gather.2.cloned.1.call-done = bf16[1024,2048]{1,0:T(8,128)(2,1)} async-done(((bf16[64,2048]{1,0:T(8,128)(2,1)}), bf16[1024,2048]{1,0:T(8,128)(2,1)}) %all-gather.2.cloned.1.call-update) | async-done | bytes 4194320 | tf_op jit(solution)/shard_map/all_gather | solution.py:480
  104.5 3.6 %fusion.29 = f32[256,2048]{1,0:T(8,128)S(1)} fusion(bf16[1024,2048]{1,0:T(8,128)(2,1)} %all-gather.2.cloned.1.call-done, bf16[128,1024]{0,1:T(8,128)(2,1)} %collective-permute-done.5, bf16[128,1024]{0,1:T(8,128)(2,1)} %bitcast.128), kind=kOutput, calls=%fused_computation.44 | convolution fusion | flops 1074790400 | bytes 6815744 | tf_op jit(solution)/shard_map/dot_general | solution.py:531
  108.1 1.3 copy-done.3
  109.4 1.1 slice.116
  110.6 1.3 convert_reduce_fusion.1
  112.6 1.0 copy.83
  113.6 1.7 fusion.28
  115.4 0.9 copy.93
  116.4 3.4 %all-to-all-start.2 = ((bf16[32,64,128]{2,1,0:T(8,128)(2,1)}), bf16[32,64,128]{2,1,0:T(8,128)(2,1)}, u32[]{:S(2)}, u32[]{:S(2)}) async-start(bf16[32,64,128]{2,1,0:T(8,128)(2,1)} %bitcast.21), calls=%async_computation.2 | async-start | bytes 1048576 | tf_op jit(solution)/shard_map/all_to_all | solution.py:461
  120.0 21.5 %shard_map.84 = (bf16[32,128,128]{2,1,0:T(8,128)(2,1)S(1)}, f32[32,256]{1,0:T(8,128)S(1)}) custom-call(bf16[32,72,256]{2,1,0:T(8,128)(2,1)S(1)} %all-to-all-done.mine_ref, bf16[32,64,256]{2,1,0:T(8,128)(2,1)S(1)} %collective-permute-done.other_ref, s32[32,128]{1,0:T(8,128)S(1)} %add_select_fusion.slot_ref, f32[32,256]{1,0:T(8,128)S(1)} %select_select_fusion.code_ref), custom_call_target="tpu_custom_call" | custom-call | tf_op jit(solution)/shard_map/pallas_call | solution.py:433
  141.7 2.0 pad_maximum_fusion.4
  143.7 1.7 collective-permute-start.9
  145.4 0.8 copy.85
  146.1 1.0 copy.86
  147.2 1.4 select_reduce_fusion.1
  148.7 1.9 fusion.42
  151.2 1.3 fusion.40
  152.8 3.6 %fusion.23 = (f32[32,128]{1,0:T(8,128)S(1)}, bf16[32,128,128]{2,1,0:T(8,128)(2,1)S(1)}, bf16[32,128,128]{2,1,0:T(8,128)(2,1)S(1)}) fusion(bf16[32,64,128]{2,1,0:T(8,128)(2,1)S(1)} %collective-permute-done.7, bf16[32,64,128]{2,1,0:T(8,128)(2,1)} %all-to-all-done.2, bf16[32,64,128]{2,1,0:T(8,128)(2,1)S(1)} %get-tuple-element.34, ...), kind=kLoop, calls=%fused_computation.24 | loop fusion | flops 9433088 | bytes 5292032 | tf_op jit(solution)/shard_map/reduce_sum | solution.py:552
  156.4 0.8 slice.110
  157.3 4.7 %all-to-all-start.1 = ((bf16[32,64,128]{2,1,0:T(8,128)(2,1)}), bf16[32,64,128]{2,1,0:T(8,128)(2,1)}, u32[]{:S(2)}, u32[]{:S(2)}) async-start(bf16[32,64,128]{2,1,0:T(8,128)(2,1)} %slice.110), calls=%async_computation.1 | async-start | bytes 1048576 | tf_op jit(solution)/shard_map/all_to_all | solution.py:461
  162.0 3.1 %maximum_maximum_fusion = bf16[512,2048]{1,0:T(8,128)(2,1)} fusion(bf16[128,1024]{1,0:T(8,128)(2,1)} %get-tuple-element.40, bf16[128,1024]{1,0:T(8,128)(2,1)} %copy-done.5, bf16[128,1024]{1,0:T(8,128)(2,1)} %get-tuple-element.39, bf16[128,1024]{1,0:T(8,128)(2,1)} %copy-done.2, bf16[256,1024]{1,0:T(8,128)(2,1)} %collective-permute-done.9, ...), kind=kLoop, calls=%fused_computation.25 | loop fusion | flops 14680064 | bytes 4194304 | tf_op jit(solution)/shard_map/concatenate | solution.py:591
  165.3 12.2 %all-to-all-done.1 = bf16[32,64,128]{2,1,0:T(8,128)(2,1)} async-done(((bf16[32,64,128]{2,1,0:T(8,128)(2,1)}), bf16[32,64,128]{2,1,0:T(8,128)(2,1)}, u32[]{:S(2)}, u32[]{:S(2)}) %all-to-all-start.1) | async-done | bytes 524320 | tf_op jit(solution)/shard_map/all_to_all | solution.py:461
  177.5 2.2 copy.124
  179.7 2.0 all_to_all.28
  181.7 1.9 copy.94
  183.7 4.1 %all-to-all-start.3 = ((bf16[128,8,256]{2,0,1:T(8,128)(2,1)}), bf16[128,8,256]{2,0,1:T(8,128)(2,1)}, u32[]{:S(2)}, u32[]{:S(2)}) async-start(bf16[128,8,256]{2,0,1:T(8,128)(2,1)} %copy.94), calls=%async_computation.3 | async-start | bytes 1048576 | tf_op jit(solution)/shard_map/all_to_all | solution.py:571
  187.9 9.7 %all-to-all-done.3 = bf16[128,8,256]{2,0,1:T(8,128)(2,1)} async-done(((bf16[128,8,256]{2,0,1:T(8,128)(2,1)}), bf16[128,8,256]{2,0,1:T(8,128)(2,1)}, u32[]{:S(2)}, u32[]{:S(2)}) %all-to-all-start.3) | async-done | bytes 524320 | tf_op jit(solution)/shard_map/all_to_all | solution.py:571
  197.6 0.8 bitcast_dynamic-update-slice_fusion.7
  198.4 0.8 bitcast_dynamic-update-slice_fusion.6
  199.3 0.8 bitcast_dynamic-update-slice_fusion.5
  200.1 0.8 bitcast_dynamic-update-slice_fusion.4
  200.9 0.8 bitcast_dynamic-update-slice_fusion.3
  201.8 0.8 bitcast_dynamic-update-slice_fusion.2
  202.6 0.8 bitcast_dynamic-update-slice_fusion.1
  203.5 0.8 bitcast_dynamic-update-slice_fusion
  204.3 4.5 %fusion.19 = bf16[2048,256]{1,0:T(8,128)(2,1)} fusion(bf16[1024,256]{1,0:T(8,128)(2,1)S(1)} %bitcast_dynamic-update-slice_fusion, bf16[512,2048]{1,0:T(8,128)(2,1)} %collective-permute-done.12, bf16[128,1024]{1,0:T(8,128)(2,1)} %get-tuple-element.40, bf16[128,1024]{1,0:T(8,128)(2,1)} %copy-done.5, bf16[128,1024]{1,0:T(8,128)(2,1)} %get-tuple-element.39, ...), kind=kOutput, calls=%fused_computation.22 | convolution fusion | flops 1108344832 | bytes 5767168 | tf_op jit(solution)/shard_map/dot_general | solution.py:326
  208.9 3.6 %all-to-all-start.5 = ((bf16[32,64,256]{2,1,0:T(8,128)(2,1)}), bf16[32,64,256]{2,1,0:T(8,128)(2,1)}, u32[]{:S(2)}, u32[]{:S(2)}) async-start(bf16[32,64,256]{2,1,0:T(8,128)(2,1)} %bitcast.114), calls=%async_computation.5 | async-start | bytes 2097152 | tf_op jit(solution)/shard_map/all_to_all | solution.py:461
  212.5 1.4 select_reduce_fusion
  214.0 0.8 copy.96
  214.7 1.0 copy.97.shift_ref
  215.7 21.0 %shard_map.85 = bf16[32,128,256]{2,1,0:T(8,128)(2,1)S(1)} custom-call(bf16[32,72,256]{2,1,0:T(8,128)(2,1)S(1)} %all-to-all-done.mine_ref, bf16[32,64,256]{2,1,0:T(8,128)(2,1)S(1)} %collective-permute-done.other_ref, bf16[32,128,128]{2,1,0:T(8,128)(2,1)S(1)} %get-tuple-element.10.grad_ref, s32[32,128]{1,0:T(8,128)S(1)} %add_select_fusion.slot_ref, ...), custom_call_target="tpu_custom_call" | custom-call | tf_op jit(solution)/shard_map/pallas_call | solution.py:433
  236.9 2.6 collective-permute-done.13
  239.6 1.4 add_convert_fusion
  241.0 5.6 %all-to-all-start.4 = ((bf16[32,64,256]{2,1,0:T(8,128)(2,1)}), bf16[32,64,256]{2,1,0:T(8,128)(2,1)S(1)}, u32[]{:S(2)}, u32[]{:S(2)}) async-start(bf16[32,64,256]{2,1,0:T(8,128)(2,1)} %add_convert_fusion), calls=%async_computation.4 | async-start | bytes 2097152 | tf_op jit(solution)/shard_map/all_to_all | solution.py:461
  247.1 1.7 collective-permute-done.3
  248.7 3.5 %convolution_convert_fusion = bf16[256,1024]{1,0:T(8,128)(2,1)S(1)} fusion(bf16[1024,2048]{1,0:T(8,128)(2,1)} %all-gather.2.cloned.1.call-done, bf16[128,2048]{1,0:T(8,128)(2,1)S(1)} %collective-permute-done.3, bf16[128,2048]{1,0:T(8,128)(2,1)S(1)} %bitcast.126), kind=kOutput, calls=%fused_computation.30 | convolution fusion | flops 1076101120 | bytes 5767168 | tf_op jit(solution)/shard_map/dot_general | solution.py:326
  252.5 1.3 collective-permute-done.4
  254.3 1.0 copy.101
  255.3 1.4 convert_reduce_fusion
  256.8 0.8 copy.104
  257.6 15.2 %all-to-all-done.4 = bf16[32,64,256]{2,1,0:T(8,128)(2,1)S(1)} async-done(((bf16[32,64,256]{2,1,0:T(8,128)(2,1)}), bf16[32,64,256]{2,1,0:T(8,128)(2,1)S(1)}, u32[]{:S(2)}, u32[]{:S(2)}) %all-to-all-start.4) | async-done | bytes 1048608 | tf_op jit(solution)/shard_map/all_to_all | solution.py:461
  273.5 0.9 copy.121
  274.7 0.9 copy.120
  (77 shorter events, 9.1 us)
Async XLA Ops:
  7.2 97.3 %all-gather.2.cloned.1.call-start = ((), (), s32[]{:S(2)}) async-start(), calls=%async_computation.6 | async-start | bytes 4456448 | tf_op jit(solution)/shard_map/all_gather | solution.py:480
  11.4 8.5 %copy-start.4 = (bf16[128,2048]{1,0:T(8,128)(2,1)S(1)}, bf16[128,2048]{1,0:T(8,128)(2,1)}, u32[]{:S(2)}) copy-start(bf16[128,2048]{1,0:T(8,128)(2,1)} %param.7) | copy-start | bytes 1572868
  12.5 47.6 %all-to-all-start = ((bf16[32,72,256]{2,1,0:T(8,128)(2,1)}), bf16[32,72,256]{2,1,0:T(8,128)(2,1)S(1)}, u32[]{:S(2)}, u32[]{:S(2)}) async-start(bf16[32,72,256]{2,1,0:T(8,128)(2,1)} %pad_maximum_fusion), calls=%async_computation | async-start | bytes 2359296 | tf_op jit(solution)/shard_map/all_to_all | solution.py:461
  20.6 39.5 %copy-start.2 = (bf16[128,1024]{1,0:T(8,128)(2,1)}, bf16[128,1024]{1,0:T(8,128)(2,1)S(1)}, u32[]{:S(2)}) copy-start(bf16[128,1024]{1,0:T(8,128)(2,1)S(1)} %get-tuple-element.38) | copy-start | bytes 786436
  20.6 17.5 %collective-permute-start.10 = (bf16[128,1024]{1,0:T(8,128)(2,1)S(1)}, bf16[128,1024]{1,0:T(8,128)(2,1)S(1)}, u32[]{:S(2)}, u32[]{:S(2)}) collective-permute-start(bf16[128,1024]{1,0:T(8,128)(2,1)S(1)} %get-tuple-element.38), channel_id=1, source_target_pairs={{0,4},{1,5},{2,6},{3,7},{4,0},{5,1},{6,2},{7,3},{8,12},{9,13},{10,... | collective-permute-start | bytes 786440 | tf_op jit(solution)/shard_map/ppermute | solution.py:478
  23.5 37.8 %collective-permute-start.5 = (bf16[128,1024]{0,1:T(8,128)(2,1)}, bf16[128,1024]{0,1:T(8,128)(2,1)}, u32[]{:S(2)}, u32[]{:S(2)}) collective-permute-start(bf16[128,1024]{0,1:T(8,128)(2,1)} %bitcast.19), channel_id=1, source_target_pairs={{0,1},{1,0},{2,3},{3,2},{4,5},{5,4},{6,7},{7,6},{8,9},{9,8},{10,11... | collective-permute-start | bytes 786440 | tf_op jit(solution)/shard_map/ppermute | solution.py:455
  23.5 118.2 %collective-permute-start.8 = (bf16[128,1024]{1,0:T(8,128)(2,1)}, bf16[128,1024]{1,0:T(8,128)(2,1)}, u32[]{:S(2)}, u32[]{:S(2)}) collective-permute-start(bf16[128,1024]{1,0:T(8,128)(2,1)} %get-tuple-element.37), channel_id=1, source_target_pairs={{0,2},{1,3},{2,0},{3,1},{4,6},{5,7},{6,4},{7,5},{8,10},{9,11},{10,... | collective-permute-start | bytes 786440 | tf_op jit(solution)/shard_map/ppermute | solution.py:478
  38.1 3.1 %copy-start.5 = (bf16[128,1024]{1,0:T(8,128)(2,1)}, bf16[128,1024]{1,0:T(8,128)(2,1)S(1)}, u32[]{:S(2)}) copy-start(bf16[128,1024]{1,0:T(8,128)(2,1)S(1)} %collective-permute-done.10) | copy-start | bytes 786436
  39.0 109.7 %collective-permute-start.11 = (bf16[256,1024]{1,0:T(8,128)(2,1)}, bf16[256,1024]{1,0:T(8,128)(2,1)}, u32[]{:S(2)}, u32[]{:S(2)}) collective-permute-start(bf16[256,1024]{1,0:T(8,128)(2,1)} %pad_maximum_fusion.5), channel_id=1, source_target_pairs={{0,2},{1,3},{2,0},{3,1},{4,6},{5,7},{6,4},{7,5},{8,10},{9,11},{10,... | collective-permute-start | bytes 1572872 | tf_op jit(solution)/shard_map/ppermute | solution.py:478
  60.2 59.7 %collective-permute-start = (bf16[32,64,256]{2,1,0:T(8,128)(2,1)S(1)}, bf16[32,64,256]{2,1,0:T(8,128)(2,1)S(1)}, u32[]{:S(2)}, u32[]{:S(2)}) collective-permute-start(bf16[32,64,256]{2,1,0:T(8,128)(2,1)S(1)} %slice.105), channel_id=1, source_target_pairs={{0,1},{1,0},{2,3},{3,2},{4,5},{5,4},{6,7},{7,6},{8,9},{9,8},{10,11... | collective-permute-start | bytes 3145736 | tf_op jit(solution)/shard_map/ppermute | solution.py:455
  108.1 1.4 copy-start.3
  110.6 3.0 %collective-permute-start.6 = (f32[128,2048]{1,0:T(8,128)}, f32[128,2048]{1,0:T(8,128)}, u32[]{:S(2)}, u32[]{:S(2)}) collective-permute-start(f32[128,2048]{1,0:T(8,128)} %slice.116), channel_id=1, source_target_pairs={{0,1},{1,0},{2,3},{3,2},{4,5},{5,4},{6,7},{7,6},{8,9},{9,8},{10,11... | collective-permute-start | bytes 3145736 | tf_op jit(solution)/shard_map/ppermute | solution.py:455
  116.4 34.2 %all-to-all-start.2 = ((bf16[32,64,128]{2,1,0:T(8,128)(2,1)}), bf16[32,64,128]{2,1,0:T(8,128)(2,1)}, u32[]{:S(2)}, u32[]{:S(2)}) async-start(bf16[32,64,128]{2,1,0:T(8,128)(2,1)} %bitcast.21), calls=%async_computation.2 | async-start | bytes 1048576 | tf_op jit(solution)/shard_map/all_to_all | solution.py:461
  141.4 11.1 %copy-start = (bf16[32,128,128]{2,1,0:T(8,128)(2,1)}, bf16[32,128,128]{2,1,0:T(8,128)(2,1)S(1)}, u32[]{:S(2)}) copy-start(bf16[32,128,128]{2,1,0:T(8,128)(2,1)S(1)} %get-tuple-element.9) | copy-start | bytes 3145732
  141.4 9.8 %collective-permute-start.2 = (bf16[32,128,128]{2,1,0:T(8,128)(2,1)S(1)}, bf16[32,128,128]{2,1,0:T(8,128)(2,1)}, u32[]{:S(2)}, u32[]{:S(2)}) collective-permute-start(bf16[32,128,128]{2,1,0:T(8,128)(2,1)S(1)} %get-tuple-element.9), channel_id=1, source_target_pairs={{0,1},{1,0},{2,3},{3,2},{4,5},{5,4},{6,7},{7,6},{8,9},{9,8},{10,11... | collective-permute-start | bytes 3145736 | tf_op jit(solution)/shard_map/ppermute | solution.py:455
  143.7 18.4 %collective-permute-start.9 = (bf16[256,1024]{1,0:T(8,128)(2,1)}, bf16[256,1024]{1,0:T(8,128)(2,1)}, u32[]{:S(2)}, u32[]{:S(2)}) collective-permute-start(bf16[256,1024]{1,0:T(8,128)(2,1)} %pad_maximum_fusion.4), channel_id=1, source_target_pairs={{0,4},{1,5},{2,6},{3,7},{4,0},{5,1},{6,2},{7,3},{8,12},{9,13},{10,... | collective-permute-start | bytes 1572872 | tf_op jit(solution)/shard_map/ppermute | solution.py:478
  148.6 2.5 collective-permute-start.1
  150.6 2.2 collective-permute-start.7
  157.3 20.3 %all-to-all-start.1 = ((bf16[32,64,128]{2,1,0:T(8,128)(2,1)}), bf16[32,64,128]{2,1,0:T(8,128)(2,1)}, u32[]{:S(2)}, u32[]{:S(2)}) async-start(bf16[32,64,128]{2,1,0:T(8,128)(2,1)} %slice.110), calls=%async_computation.1 | async-start | bytes 1048576 | tf_op jit(solution)/shard_map/all_to_all | solution.py:461
  165.2 39.2 %collective-permute-start.12 = (bf16[512,2048]{1,0:T(8,128)(2,1)}, bf16[512,2048]{1,0:T(8,128)(2,1)}, u32[]{:S(2)}, u32[]{:S(2)}) collective-permute-start(bf16[512,2048]{1,0:T(8,128)(2,1)} %maximum_maximum_fusion), channel_id=1, source_target_pairs={{0,1},{1,0},{2,3},{3,2},{4,5},{5,4},{6,7},{7,6},{8,9},{9,8},{10,11... | collective-permute-start | bytes 6291464 | tf_op jit(solution)/shard_map/ppermute | solution.py:455
  183.7 13.9 %all-to-all-start.3 = ((bf16[128,8,256]{2,0,1:T(8,128)(2,1)}), bf16[128,8,256]{2,0,1:T(8,128)(2,1)}, u32[]{:S(2)}, u32[]{:S(2)}) async-start(bf16[128,8,256]{2,0,1:T(8,128)(2,1)} %copy.94), calls=%async_computation.3 | async-start | bytes 1048576 | tf_op jit(solution)/shard_map/all_to_all | solution.py:571
  208.9 32.1 %all-to-all-start.5 = ((bf16[32,64,256]{2,1,0:T(8,128)(2,1)}), bf16[32,64,256]{2,1,0:T(8,128)(2,1)}, u32[]{:S(2)}, u32[]{:S(2)}) async-start(bf16[32,64,256]{2,1,0:T(8,128)(2,1)} %bitcast.114), calls=%async_computation.5 | async-start | bytes 2097152 | tf_op jit(solution)/shard_map/all_to_all | solution.py:461
  236.8 9.7 %copy-start.1 = (bf16[16,2,64,128]{3,0,2,1:T(8,128)(2,1)S(1)}, bf16[16,2,64,128]{3,0,2,1:T(8,128)(2,1)}, u32[]{:S(2)}) copy-start(bf16[16,2,64,128]{3,0,2,1:T(8,128)(2,1)} %copy.124) | copy-start | bytes 1572868
  236.9 2.7 collective-permute-start.13
  241.0 31.8 %all-to-all-start.4 = ((bf16[32,64,256]{2,1,0:T(8,128)(2,1)}), bf16[32,64,256]{2,1,0:T(8,128)(2,1)S(1)}, u32[]{:S(2)}, u32[]{:S(2)}) async-start(bf16[32,64,256]{2,1,0:T(8,128)(2,1)} %add_convert_fusion), calls=%async_computation.4 | async-start | bytes 2097152 | tf_op jit(solution)/shard_map/all_to_all | solution.py:461
  246.7 2.0 collective-permute-start.3
  252.2 1.6 collective-permute-start.4
Sparse Core Ops, SparseCore 0:
  10.8 93.6 all-gather.1

commit v3 on v2

--- a/solution.py
+++ b/solution.py
@@ -437,6 +437,9 @@
         out_specs=jax.tree.map(lambda _: pl.BlockSpec(memory_space=pltpu.VMEM), out_shape),
         scratch_shapes=scratch_shapes,
         compiler_params=pltpu.CompilerParams(vmem_limit_bytes=VMEM_BYTES),
+        cost_estimate=pl.CostEstimate(
+            flops=20_000_000_000, bytes_accessed=8_000_000, transcendentals=2_000_000
+        ),
     )(*arguments)
 
 
@@ -468,22 +471,8 @@
             token_rows, row_width
         )
 
-    def own_half(rows):
-        parted = rows.reshape(rows.shape[0], heads, 2, -1)
-        even, odd = parted[:, :, 0], parted[:, :, 1]
-        kept, passed = jnp.where(first, even, odd), jnp.where(first, odd, even)
-        return kept.reshape(rows.shape[0], -1), passed.reshape(rows.shape[0], -1)
-
     def moved(block, mask):
         return lax.ppermute(block, "ctx", [(device, device ^ mask) for device in range(peers)])
-
-    half_weight = lax.all_gather(
-        out_weight,
-        "ctx",
-        axis=0,
-        tiled=True,
-        axis_index_groups=[list(range(0, peers, 2)), list(range(1, peers, 2))],
-    )
 
     tag = jnp.pad(buckets.astype(jnp.bfloat16).reshape(1, -1), ((0, 7), (0, 0)))
     sent = jnp.concatenate([by_head(shared_qk), by_head(values)], axis=-1)
@@ -495,7 +484,49 @@
         axis=1,
     )
     mine = everywhere(sent)
+    mine, late_weight = lax.optimization_barrier((mine, out_weight))
+    half_weight = lax.all_gather(
+        late_weight,
+        "ctx",
+        axis=0,
+        tiled=True,
+        axis_index_groups=[list(range(0, peers, 2)), list(range(1, peers, 2))],
+    )
     other = exchange(mine[:, :half])
+
+    plane = peers // PLANES
+    index = lax.axis_index("ctx")
+    level, here, seat = index // plane, index % plane, index % PLANES
+    masks = (0, 2, 4, 6, 1, 3, 5, 7)
+    down = [
+        [
+            (tier * plane + place, PLANES * place + (tier - step) % PLANES)
+            for tier in range(PLANES)
+            for place in range(plane)
+        ]
+        for step in range(PLANES)
+    ]
+
+    def pick(blocks, which):
+        return lax.dynamic_index_in_dim(blocks, which, axis=0, keepdims=False)
+
+    columns = jnp.broadcast_to(
+        late_weight.reshape(1, -1, plane, row_width // plane).transpose(0, 2, 1, 3),
+        (PLANES, plane, row_width // peers, row_width // plane),
+    ).reshape(peers, row_width // peers, row_width // plane)
+    column_weight = everywhere(columns).reshape(row_width, row_width // plane)
+
+    left, right = out_grad[:, : row_width // 2], out_grad[:, row_width // 2 :]
+    left_two = jnp.concatenate([left, moved(left, 2)], axis=0)
+    right_y = moved(right, 4)
+    right_two = jnp.concatenate([right, right_y], axis=0)
+    left_four = jnp.concatenate([left_two, moved(left_two, 4)], axis=0)
+    right_far = moved(right_two, 2)
+    right_four = jnp.concatenate(
+        [right, right_far[:token_rows], right_y, right_far[token_rows:]], axis=0
+    )
+    core_grad = jnp.concatenate([left_four, right_four], axis=1)
+    plane_grad = jnp.concatenate([core_grad, exchange(core_grad)], axis=0)
 
     all_buckets = mine[:, half].astype(jnp.int32).reshape(peers, 2, token_rows)
     own = jnp.where(first, all_buckets[:, 0], all_buckets[:, 1])
@@ -526,13 +557,29 @@
         (mine, other, slot, code),
     )
 
-    grad_kept, grad_passed = own_half(out_grad)
-    grad_pair = jnp.concatenate([grad_kept, exchange(grad_passed)], axis=0)
-    grad_part = jnp.dot(grad_pair, half_weight, preferred_element_type=jnp.float32)
-    attended_grad = (grad_part[:token_rows] + exchange(grad_part[token_rows:])).astype(
-        jnp.bfloat16
-    )
-    grad_mine = everywhere(by_head(attended_grad).reshape(peers, half, HEAD_DIM))
+    attended_grad = (
+        jnp.dot(plane_grad, column_weight, preferred_element_type=jnp.float32)
+        .astype(jnp.bfloat16)
+        .reshape(plane, token_rows, row_width // plane)
+    )
+    turns = [here ^ place for place in range(plane)]
+    attended_grad = jnp.stack(
+        [pick(attended_grad, turn // 2 + (plane // 2) * (turn % 2)) for turn in turns]
+    )
+    attended_grad = (
+        attended_grad.reshape(plane, 2, half, 2, HEAD_DIM)
+        .transpose(3, 1, 0, 2, 4)
+        .reshape(PLANES, plane * half, HEAD_DIM)
+    )
+    arrived = jnp.stack(
+        [
+            lax.ppermute(pick(attended_grad, (level - step) % PLANES), "ctx", down[step])
+            for step in range(PLANES)
+        ]
+    )
+    grad_mine = jnp.concatenate(
+        [pick(arrived, (tier - seat) % PLANES) for tier in range(PLANES)], axis=0
+    ).reshape(peers, half, HEAD_DIM)
     grad_rows = jnp.concatenate([grad_mine, exchange(grad_mine)], axis=1).astype(jnp.float32)
 
     chosen = slot[:, :, None] == jnp.arange(slots, dtype=jnp.int32)
@@ -557,7 +604,30 @@
         shift_slots.reshape(peers, peers, per_peer).transpose(1, 0, 2).reshape(peers, slots)
     )
 
-    attended_rows = by_token(everywhere(attended[:, :half]))
+    attended_half = attended[:, :half].reshape(PLANES, plane * half, HEAD_DIM)
+    arrived = jnp.stack(
+        [
+            lax.ppermute(
+                pick(attended_half, (seat + step) % PLANES),
+                "ctx",
+                [(target, source) for source, target in down[step]],
+            )
+            for step in range(PLANES)
+        ]
+    )
+    plane_attended = (
+        jnp.stack([pick(arrived, (level - place) % PLANES) for place in range(PLANES)])
+        .reshape(2, 2, plane, half, HEAD_DIM)
+        .transpose(2, 1, 3, 0, 4)
+        .reshape(plane, token_rows, row_width // plane)
+    )
+    parts = [pick(plane_attended, here ^ mask) for mask in masks]
+    plane_attended = jnp.concatenate(parts, axis=0)
+    landed = {
+        mask: part if mask == 0 else moved(part, mask) for mask, part in zip(masks, parts)
+    }
+    landed = jnp.stack([landed[mask] for mask in range(plane)])
+    attended_rows = jnp.concatenate([pick(landed, turn) for turn in turns], axis=1)
 
     attended_pair = jnp.concatenate([attended_rows, exchange(attended_rows)], axis=0)
     mixed_part = contract(attended_pair, half_weight, 1, 1).astype(jnp.bfloat16)
@@ -566,30 +636,6 @@
     mixed_odd = jnp.where(first, mixed_got, mixed_kept).reshape(token_rows, heads, 1, -1)
     mixed = jnp.concatenate([mixed_even, mixed_odd], axis=2).reshape(token_rows, row_width)
 
-    plane = peers // PLANES
-    groups = [[level * plane + place for place in range(plane)] for level in range(PLANES)]
-    plane_attended = lax.all_to_all(
-        attended_rows, "ctx", split_axis=1, concat_axis=0, tiled=True, axis_index_groups=groups
-    ).reshape(plane, token_rows, row_width // plane)
-    here = lax.axis_index("ctx") % plane
-    plane_attended = jnp.concatenate(
-        [
-            lax.dynamic_index_in_dim(plane_attended, here ^ mask, axis=0, keepdims=False)
-            for mask in (0, 2, 4, 6, 1, 3, 5, 7)
-        ],
-        axis=0,
-    )
-    left, right = out_grad[:, : row_width // 2], out_grad[:, row_width // 2 :]
-    left_two = jnp.concatenate([left, moved(left, 2)], axis=0)
-    right_x = moved(right, 4)
-    right_two = jnp.concatenate([right, right_x], axis=0)
-    left_four = jnp.concatenate([left_two, moved(left_two, 4)], axis=0)
-    right_far = moved(right_two, 2)
-    right_four = jnp.concatenate(
-        [right, right_far[:token_rows], right_x, right_far[token_rows:]], axis=0
-    )
-    core_grad = jnp.concatenate([left_four, right_four], axis=1)
-    plane_grad = jnp.concatenate([core_grad, exchange(core_grad)], axis=0)
     partial = contract(plane_grad, plane_attended, 0, 0) * (1.0 / math.sqrt(token_rows * peers))
     partial = partial.astype(jnp.bfloat16).reshape(
         peers, row_width // peers, row_width // plane

time: 284 us -> 301 us (1.060)
  starting transfers between devices: 37.7 us -> 78.1 us
  waiting for transfers between devices: 119 us -> 95.9 us
  local copies, waits for them, and re-layouts: 35.1 us -> 23.6 us
  other arithmetic: 22.2 us -> 33.4 us
    all_gather x1, waiting for transfers between devices: 43.2 us -> 0.01 us  [head_owner_device(): lax.all_gather(late_weight, 'ctx', axis=0, tiled=True, axis_index_groups=...]
    ppermute x0 -> x8, starting transfers between devices: none -> 33.7 us  [the longest x4 24.4 us: head_owner_device(): lax.ppermute(pick(attended_half, (seat + step) % PLANES), 'ctx', [(target...]
    ppermute x0 -> x8, waiting for transfers between devices: none -> 32.2 us  [the longest x4 31.4 us: head_owner_device(): lax.ppermute(pick(attended_grad, (level - step) % PLANES), 'ctx', down[st...]
    ppermute x4 -> x11, waiting for transfers between devices: 13 us -> 36.9 us  [moved(): lax.ppermute(block, 'ctx', [(device, device ^ mask) for device in range(p...]
    all_to_all x5 -> x4, waiting for transfers between devices: 46.3 us -> 26.3 us  [everywhere(): return lax.all_to_all(block, 'ctx', split_axis=0, concat_axis=0, tiled=True)]
    concatenate x1, other arithmetic: 3.12 us -> 13.3 us  [head_owner_device(): core_grad = jnp.concatenate([left_four, right_four], axis=1)]
    all_to_all x1 -> x0, waiting for transfers between devices: 9.7 us -> none  [head_owner_device(): lax.all_to_all(attended_rows, 'ctx', split_axis=1, concat_axis=0, tiled=T...]
    ppermute x4 -> x11, starting transfers between devices: 7.16 us -> 13 us  [moved(): lax.ppermute(block, 'ctx', [(device, device ^ mask) for device in range(p...]
  transfers between devices with their start and end apart: 21 -> 32, of which waited for: 10 -> 14; matrix products, arithmetic and copies ran while one was open for 21% -> 20% of each run, Pallas kernels for 15% -> 14%
where the time goes in v3:
time: 301 us; the launch traced here: 300 us
  waiting for transfers between devices  95.9 us (32%)
  starting transfers between devices  78.1 us (26%)
  Pallas kernels  42.5 us (14%)
  other arithmetic  33.4 us (11%)
  local copies, waits for them, and re-layouts  23.6 us (8%)
  between operations  15 us (5%)
  matrix products  11.7 us (4%)
    pallas_call x2, Pallas kernels, kernel_call(): pl.pallas_call(body, out_shape=out_shape, in_specs=[pl.BlockSpec(memory_s...  42.5 us
    ppermute x11, waiting for transfers between devices, moved(): lax.ppermute(block, 'ctx', [(device, device ^ mask) for device in range(p...  36.9 us
    ppermute x4, waiting for transfers between devices, head_owner_device(): lax.ppermute(pick(attended_grad, (level - step) % PLANES), 'ctx', down[st...  31.4 us
    all_to_all x4, starting transfers between devices, everywhere(): return lax.all_to_all(block, 'ctx', split_axis=0, concat_axis=0, tiled=True)  27 us
    all_to_all x4, waiting for transfers between devices, everywhere(): return lax.all_to_all(block, 'ctx', split_axis=0, concat_axis=0, tiled=True)  26.3 us
    ppermute x4, starting transfers between devices, head_owner_device(): lax.ppermute(pick(attended_half, (seat + step) % PLANES), 'ctx', [(target...  24.4 us
    concatenate x1, other arithmetic, head_owner_device(): core_grad = jnp.concatenate([left_four, right_four], axis=1)  13.3 us
    ppermute x11, starting transfers between devices, moved(): lax.ppermute(block, 'ctx', [(device, device ^ mask) for device in range(p...  13 us
  transfers between devices with their start and end apart: 32, of which 14 were waited for; matrix products, arithmetic and copies ran while one was open for 20% of the time, Pallas kernels for 14%

profile of v3, /device:TPU:0, one launch (start us, length us, event | category | flops | bytes accessed | tf_op | source)
XLA Modules:
  0.0 300.2 jit_solution(14672227223648302420)
XLA Ops:
  7.2 1.1 copy.120
  8.3 1.1 copy.121
  9.5 0.7 convert_bitcast_fusion
  10.6 1.1 pad_maximum_fusion.1
  11.7 7.3 %all-to-all-start = ((bf16[32,72,256]{2,1,0:T(8,128)(2,1)}), bf16[32,72,256]{2,1,0:T(8,128)(2,1)S(1)}, u32[]{:S(2)}, u32[]{:S(2)}) async-start(bf16[32,72,256]{2,1,0:T(8,128)(2,1)} %pad_maximum_fusion.1), calls=%async_computation | async-start | bytes 2359296 | tf_op jit(solution)/shard_map/all_to_all | solution.py:464
  19.2 1.8 collective-permute-start.18
  21.0 1.5 collective-permute-start.16
  22.4 15.0 %collective-permute-done.18 = bf16[128,1024]{1,0:T(8,128)(2,1)S(1)} collective-permute-done((bf16[128,1024]{1,0:T(8,128)(2,1)S(1)}, bf16[128,1024]{1,0:T(8,128)(2,1)S(1)}, u32[]{:S(2)}, u32[]{:S(2)}) %collective-permute-start.18) | collective-permute-done | bytes 262176 | tf_op jit(solution)/shard_map/ppermute | solution.py:475
  37.5 0.8 pad_maximum_fusion.8
  38.3 1.1 collective-permute-start.19
  39.4 0.8 pad_maximum_fusion.7
  40.2 0.8 collective-permute-start.17
  41.3 12.0 %collective-permute-done.19 = bf16[256,1024]{1,0:T(8,128)(2,1)S(1)} collective-permute-done((bf16[256,1024]{1,0:T(8,128)(2,1)}, bf16[256,1024]{1,0:T(8,128)(2,1)S(1)}, u32[]{:S(2)}, u32[]{:S(2)}) %collective-permute-start.19) | collective-permute-done | bytes 524320 | tf_op jit(solution)/shard_map/ppermute | solution.py:475
  53.4 2.1 collective-permute-done.17
  55.4 13.3 %maximum_maximum_fusion = bf16[512,2048]{1,0:T(8,128)(2,1)} fusion(bf16[128,1024]{1,0:T(8,128)(2,1)S(1)} %get-tuple-element.78, bf16[128,1024]{1,0:T(8,128)(2,1)S(1)} %collective-permute-done.18, bf16[128,1024]{1,0:T(8,128)(2,1)S(1)} %get-tuple-element.77, bf16[128,1024]{1,0:T(8,128)(2,1)S(1)} %get-tuple-element.76, ...), kind=kLoop, calls=%fused_computation.10 | loop fusion | flops 14680064 | bytes 4194304 | tf_op jit(solution)/shard_map/concatenate | solution.py:528
  68.8 1.1 slice.68
  70.4 1.0 copy.123
  71.5 1.2 broadcast_in_dim.78
  72.6 4.6 %all-to-all-start.1 = ((bf16[32,64,256]{2,1,0:T(8,128)(2,1)}), bf16[32,64,256]{2,1,0:T(8,128)(2,1)}, u32[]{:S(2)}, u32[]{:S(2)}) async-start(bf16[32,64,256]{2,1,0:T(8,128)(2,1)} %bitcast.50), calls=%async_computation.1 | async-start | bytes 2097152 | tf_op jit(solution)/shard_map/all_to_all | solution.py:464
  78.2 1.3 convert_reduce_fusion.1
  80.4 1.0 copy.99
  81.4 5.2 %pad_maximum_fusion = bf16[1024,2048]{1,0:T(8,128)(2,1)} fusion(bf16[512,2048]{1,0:T(8,128)(2,1)} %collective-permute-done.20, bf16[128,1024]{1,0:T(8,128)(2,1)} %copy-done.3, bf16[128,1024]{1,0:T(8,128)(2,1)S(1)} %collective-permute-done.18, bf16[128,1024]{1,0:T(8,128)(2,1)} %copy-done.2, bf16[128,1024]{1,0:T(8,128)(2,1)S(1)} %get-tuple-element.76, ...), kind=kLoop, calls=%fused_computation | loop fusion | flops 33554432 | bytes 8388608 | tf_op jit(solution)/shard_map/concatenate | solution.py:529
  86.6 21.4 %shard_map.84 = (bf16[32,128,128]{2,1,0:T(8,128)(2,1)S(1)}, f32[32,256]{1,0:T(8,128)S(1)}) custom-call(bf16[32,72,256]{2,1,0:T(8,128)(2,1)S(1)} %all-to-all-done.mine_ref, bf16[32,64,256]{2,1,0:T(8,128)(2,1)S(1)} %collective-permute-done.other_ref, s32[32,128]{1,0:T(8,128)S(1)} %add_select_fusion.slot_ref, f32[32,256]{1,0:T(8,128)S(1)} %select_select_fusion.code_ref), custom_call_target="tpu_custom_call" | custom-call | flops 20000000000 | bytes 8000000 | tf_op jit(solution)/shard_map/pallas_call | solution.py:433
  108.4 6.7 %all-to-all-done.1 = bf16[32,64,256]{2,1,0:T(8,128)(2,1)} async-done(((bf16[32,64,256]{2,1,0:T(8,128)(2,1)}), bf16[32,64,256]{2,1,0:T(8,128)(2,1)}, u32[]{:S(2)}, u32[]{:S(2)}) %all-to-all-start.1) | async-done | bytes 1048608 | tf_op jit(solution)/shard_map/all_to_all | solution.py:464
  115.1 3.8 %convolution_convert_fusion = bf16[1024,256]{1,0:T(8,128)(2,1)S(1)} fusion(bf16[1024,2048]{1,0:T(8,128)(2,1)} %pad_maximum_fusion, bf16[2048,256]{1,0:T(8,128)(2,1)} %bitcast.51), kind=kOutput, calls=%fused_computation.15 | convolution fusion | flops 1074003968 | bytes 5767168 | tf_op jit(solution)/shard_map/dot_general | solution.py:561
  120.0 3.3 %collective-permute-start.22 = (bf16[512,128]{1,0:T(8,128)(2,1)S(1)}, bf16[512,128]{1,0:T(8,128)(2,1)S(1)}, u32[]{:S(2)}, u32[]{:S(2)}) collective-permute-start(bf16[512,128]{1,0:T(8,128)(2,1)S(1)} %get-tuple-element.74), channel_id=1, source_target_pairs={{0,3},{1,7},{2,11},{3,15},{4,19},{5,23},{6,27},{7,31},{8,0},{9,4},... | collective-permute-start | bytes 393224 | tf_op jit(solution)/shard_map/ppermute | solution.py:576
  123.3 1.7 collective-permute-start.23
  125.1 3.5 %collective-permute-start.24 = (bf16[512,128]{1,0:T(8,128)(2,1)S(1)}, bf16[512,128]{1,0:T(8,128)(2,1)S(1)}, u32[]{:S(2)}, u32[]{:S(2)}) collective-permute-start(bf16[512,128]{1,0:T(8,128)(2,1)S(1)} %get-tuple-element.72), channel_id=1, source_target_pairs={{0,1},{1,5},{2,9},{3,13},{4,17},{5,21},{6,25},{7,29},{8,2},{9,6},{... | collective-permute-start | bytes 393224 | tf_op jit(solution)/shard_map/ppermute | solution.py:576
  128.6 1.4 select_reduce_fusion.1
  130.0 3.0 collective-permute-start.1
  133.0 15.5 %collective-permute-done.22 = bf16[512,128]{1,0:T(8,128)(2,1)S(1)} collective-permute-done((bf16[512,128]{1,0:T(8,128)(2,1)S(1)}, bf16[512,128]{1,0:T(8,128)(2,1)S(1)}, u32[]{:S(2)}, u32[]{:S(2)}) %collective-permute-start.22) | collective-permute-done | bytes 131104 | tf_op jit(solution)/shard_map/ppermute | solution.py:576
  148.5 15.9 %collective-permute-done.23 = bf16[512,128]{1,0:T(8,128)(2,1)S(1)} collective-permute-done((bf16[512,128]{1,0:T(8,128)(2,1)S(1)}, bf16[512,128]{1,0:T(8,128)(2,1)S(1)}, u32[]{:S(2)}, u32[]{:S(2)}) %collective-permute-start.23) | collective-permute-done | bytes 131104 | tf_op jit(solution)/shard_map/ppermute | solution.py:576
  164.8 1.3 fusion.11
  166.5 2.0 fusion.2
  168.6 0.7 dynamic-slice_bitcast_fusion.11
  169.3 1.6 collective-permute-start.3
  170.9 16.9 %collective-permute-start.4 = (bf16[512,128]{1,0:T(8,128)(2,1)S(1)}, bf16[512,128]{1,0:T(8,128)(2,1)S(1)}, u32[]{:S(2)}, u32[]{:S(2)}) collective-permute-start(bf16[512,128]{1,0:T(8,128)(2,1)S(1)} %get-tuple-element.66), channel_id=1, source_target_pairs={{3,0},{7,1},{11,2},{15,3},{19,4},{23,5},{27,6},{31,7},{0,8},{4,9},... | collective-permute-start | bytes 393224 | tf_op jit(solution)/shard_map/ppermute | solution.py:610
  187.7 2.2 collective-permute-start.5
  189.9 3.8 %collective-permute-start.6 = (bf16[512,128]{1,0:T(8,128)(2,1)S(1)}, bf16[512,128]{1,0:T(8,128)(2,1)S(1)}, u32[]{:S(2)}, u32[]{:S(2)}) collective-permute-start(bf16[512,128]{1,0:T(8,128)(2,1)S(1)} %get-tuple-element.64), channel_id=1, source_target_pairs={{1,0},{5,1},{9,2},{13,3},{17,4},{21,5},{25,6},{29,7},{2,8},{6,9},{... | collective-permute-start | bytes 393224 | tf_op jit(solution)/shard_map/ppermute | solution.py:610
  193.8 1.4 select_reduce_fusion
  196.9 1.0 pad_maximum_fusion.4
  198.1 1.3 copy.104
  199.4 1.4 reshape.242
  203.5 4.5 %fusion = bf16[2048,256]{1,0:T(8,128)(2,1)} fusion(bf16[1024,2048]{1,0:T(8,128)(2,1)} %pad_maximum_fusion, bf16[1024,256]{1,0:T(8,128)(2,1)S(1)} %get-tuple-element.38), kind=kOutput, calls=%fused_computation.7 | convolution fusion | flops 1074790400 | bytes 5767168 | tf_op jit(solution)/shard_map/dot_general | solution.py:326
  208.0 10.5 %all-to-all-start.3 = ((bf16[32,64,256]{2,1,0:T(8,128)(2,1)}), bf16[32,64,256]{2,1,0:T(8,128)(2,1)}, u32[]{:S(2)}, u32[]{:S(2)}) async-start(bf16[32,64,256]{2,1,0:T(8,128)(2,1)} %bitcast.185), calls=%async_computation.3 | async-start | bytes 2097152 | tf_op jit(solution)/shard_map/all_to_all | solution.py:464
  218.5 1.2 copy-done.1
  219.7 21.0 %shard_map.85 = bf16[32,128,256]{2,1,0:T(8,128)(2,1)S(1)} custom-call(bf16[32,72,256]{2,1,0:T(8,128)(2,1)S(1)} %all-to-all-done.mine_ref, bf16[32,64,256]{2,1,0:T(8,128)(2,1)S(1)} %copy-done.1, bf16[32,128,128]{2,1,0:T(8,128)(2,1)S(1)} %get-tuple-element.14.grad_ref, s32[32,128]{1,0:T(8,128)S(1)} %add_select_fusion.slot_ref, ...), custom_call_target="tpu_custom_call" | custom-call | flops 20000000000 | bytes 8000000 | tf_op jit(solution)/shard_map/pallas_call | solution.py:433
  240.9 2.5 collective-permute-start.13
  244.3 1.4 collective-permute-done.7
  245.7 1.5 collective-permute-start.8
  247.2 2.8 collective-permute-done.8
  250.0 1.5 collective-permute-start.10
  251.4 1.5 collective-permute-start.12
  253.0 2.0 collective-permute-done.10
  255.0 1.7 collective-permute-done.12
  256.7 1.4 add_convert_fusion
  258.1 4.6 %all-to-all-start.2 = ((bf16[32,64,256]{2,1,0:T(8,128)(2,1)}), bf16[32,64,256]{2,1,0:T(8,128)(2,1)S(1)}, u32[]{:S(2)}, u32[]{:S(2)}) async-start(bf16[32,64,256]{2,1,0:T(8,128)(2,1)} %add_convert_fusion), calls=%async_computation.2 | async-start | bytes 2097152 | tf_op jit(solution)/shard_map/all_to_all | solution.py:464
  263.2 1.4 convert_reduce_fusion
  264.7 0.8 copy.119
  265.5 3.5 %convolution_convert_fusion.1 = bf16[256,1024]{1,0:T(8,128)(2,1)S(1)} fusion(bf16[1024,2048]{1,0:T(8,128)(2,1)} %all-gather.2.cloned.1.call-done, bf16[128,2048]{1,0:T(8,128)(2,1)S(1)} %collective-permute-done.14, bf16[128,2048]{1,0:T(8,128)(2,1)S(1)} %constant_dynamic-update-slice_fusion.8), kind=kOutput, calls=%fused_computation.16 | convolution fusion | flops 1076101120 | bytes 5767168 | tf_op jit(solution)/shard_map/dot_general | solution.py:326
  269.4 19.6 %all-to-all-done.2 = bf16[32,64,256]{2,1,0:T(8,128)(2,1)S(1)} async-done(((bf16[32,64,256]{2,1,0:T(8,128)(2,1)}), bf16[32,64,256]{2,1,0:T(8,128)(2,1)S(1)}, u32[]{:S(2)}, u32[]{:S(2)}) %all-to-all-start.2) | async-done | bytes 1048608 | tf_op jit(solution)/shard_map/all_to_all | solution.py:464
  289.6 0.9 copy.131
  290.9 0.9 copy.132
  292.3 1.0 copy.116
  (136 shorter events, 13.2 us)
Async XLA Ops:
  10.2 8.9 %copy-start.5 = (bf16[128,2048]{1,0:T(8,128)(2,1)S(1)}, bf16[128,2048]{1,0:T(8,128)(2,1)}, u32[]{:S(2)}) copy-start(bf16[128,2048]{1,0:T(8,128)(2,1)} %param.7) | copy-start | bytes 1572868
  11.7 57.0 %all-to-all-start = ((bf16[32,72,256]{2,1,0:T(8,128)(2,1)}), bf16[32,72,256]{2,1,0:T(8,128)(2,1)S(1)}, u32[]{:S(2)}, u32[]{:S(2)}) async-start(bf16[32,72,256]{2,1,0:T(8,128)(2,1)} %pad_maximum_fusion.1), calls=%async_computation | async-start | bytes 2359296 | tf_op jit(solution)/shard_map/all_to_all | solution.py:464
  19.0 246.5 %all-gather.2.cloned.1.call-start = ((), (), s32[]{:S(2)}) async-start(), calls=%async_computation.4 | async-start | bytes 4456448 | tf_op jit(solution)/shard_map/all_gather | solution.py:488
  19.2 18.3 %collective-permute-start.18 = (bf16[128,1024]{1,0:T(8,128)(2,1)S(1)}, bf16[128,1024]{1,0:T(8,128)(2,1)S(1)}, u32[]{:S(2)}, u32[]{:S(2)}) collective-permute-start(bf16[128,1024]{1,0:T(8,128)(2,1)S(1)} %get-tuple-element.76), channel_id=1, source_target_pairs={{0,4},{1,5},{2,6},{3,7},{4,0},{5,1},{6,2},{7,3},{8,12},{9,13},{10,... | collective-permute-start | bytes 786440 | tf_op jit(solution)/shard_map/ppermute | solution.py:475
  21.0 18.4 %collective-permute-start.16 = (bf16[128,1024]{1,0:T(8,128)(2,1)S(1)}, bf16[128,1024]{1,0:T(8,128)(2,1)S(1)}, u32[]{:S(2)}, u32[]{:S(2)}) collective-permute-start(bf16[128,1024]{1,0:T(8,128)(2,1)S(1)} %get-tuple-element.75), channel_id=1, source_target_pairs={{0,2},{1,3},{2,0},{3,1},{4,6},{5,7},{6,4},{7,5},{8,10},{9,11},{10,... | collective-permute-start | bytes 786440 | tf_op jit(solution)/shard_map/ppermute | solution.py:475
  38.3 15.0 %collective-permute-start.19 = (bf16[256,1024]{1,0:T(8,128)(2,1)}, bf16[256,1024]{1,0:T(8,128)(2,1)S(1)}, u32[]{:S(2)}, u32[]{:S(2)}) collective-permute-start(bf16[256,1024]{1,0:T(8,128)(2,1)} %pad_maximum_fusion.8), channel_id=1, source_target_pairs={{0,2},{1,3},{2,0},{3,1},{4,6},{5,7},{6,4},{7,5},{8,10},{9,11},{10,... | collective-permute-start | bytes 1572872 | tf_op jit(solution)/shard_map/ppermute | solution.py:475
  40.2 15.2 %collective-permute-start.17 = (bf16[256,1024]{1,0:T(8,128)(2,1)}, bf16[256,1024]{1,0:T(8,128)(2,1)S(1)}, u32[]{:S(2)}, u32[]{:S(2)}) collective-permute-start(bf16[256,1024]{1,0:T(8,128)(2,1)} %pad_maximum_fusion.7), channel_id=1, source_target_pairs={{0,4},{1,5},{2,6},{3,7},{4,0},{5,1},{6,2},{7,3},{8,12},{9,13},{10,... | collective-permute-start | bytes 1572872 | tf_op jit(solution)/shard_map/ppermute | solution.py:475
  53.4 15.3 %copy-start.2 = (bf16[128,1024]{1,0:T(8,128)(2,1)}, bf16[128,1024]{1,0:T(8,128)(2,1)S(1)}, u32[]{:S(2)}) copy-start(bf16[128,1024]{1,0:T(8,128)(2,1)S(1)} %get-tuple-element.77) | copy-start | bytes 786436
  53.4 15.3 %copy-start.3 = (bf16[128,1024]{1,0:T(8,128)(2,1)}, bf16[128,1024]{1,0:T(8,128)(2,1)S(1)}, u32[]{:S(2)}) copy-start(bf16[128,1024]{1,0:T(8,128)(2,1)S(1)} %get-tuple-element.78) | copy-start | bytes 786436
  55.4 13.3 %copy-start.4 = (bf16[256,1024]{1,0:T(8,128)(2,1)}, bf16[256,1024]{1,0:T(8,128)(2,1)S(1)}, u32[]{:S(2)}) copy-start(bf16[256,1024]{1,0:T(8,128)(2,1)S(1)} %collective-permute-done.17) | copy-start | bytes 1572868
  68.7 12.7 %collective-permute-start.20 = (bf16[512,2048]{1,0:T(8,128)(2,1)}, bf16[512,2048]{1,0:T(8,128)(2,1)}, u32[]{:S(2)}, u32[]{:S(2)}) collective-permute-start(bf16[512,2048]{1,0:T(8,128)(2,1)} %maximum_maximum_fusion), channel_id=1, source_target_pairs={{0,1},{1,0},{2,3},{3,2},{4,5},{5,4},{6,7},{7,6},{8,9},{9,8},{10,11... | collective-permute-start | bytes 6291464 | tf_op jit(solution)/shard_map/ppermute | solution.py:458
  69.9 16.7 %collective-permute-start = (bf16[32,64,256]{2,1,0:T(8,128)(2,1)}, bf16[32,64,256]{2,1,0:T(8,128)(2,1)S(1)}, u32[]{:S(2)}, u32[]{:S(2)}) collective-permute-start(bf16[32,64,256]{2,1,0:T(8,128)(2,1)} %slice.68), channel_id=1, source_target_pairs={{0,1},{1,0},{2,3},{3,2},{4,5},{5,4},{6,7},{7,6},{8,9},{9,8},{10,11... | collective-permute-start | bytes 3145736 | tf_op jit(solution)/shard_map/ppermute | solution.py:458
  72.6 42.4 %all-to-all-start.1 = ((bf16[32,64,256]{2,1,0:T(8,128)(2,1)}), bf16[32,64,256]{2,1,0:T(8,128)(2,1)}, u32[]{:S(2)}, u32[]{:S(2)}) async-start(bf16[32,64,256]{2,1,0:T(8,128)(2,1)} %bitcast.50), calls=%async_computation.1 | async-start | bytes 2097152 | tf_op jit(solution)/shard_map/all_to_all | solution.py:464
  86.6 21.5 %copy-start = (bf16[32,64,256]{2,1,0:T(8,128)(2,1)}, bf16[32,64,256]{2,1,0:T(8,128)(2,1)S(1)}, u32[]{:S(2)}) copy-start(bf16[32,64,256]{2,1,0:T(8,128)(2,1)S(1)} %collective-permute-done.other_ref) | copy-start | bytes 3145732
  108.3 56.5 %collective-permute-start.2 = (bf16[32,128,128]{2,1,0:T(8,128)(2,1)S(1)}, bf16[32,128,128]{2,1,0:T(8,128)(2,1)}, u32[]{:S(2)}, u32[]{:S(2)}) collective-permute-start(bf16[32,128,128]{2,1,0:T(8,128)(2,1)S(1)} %get-tuple-element.12), channel_id=1, source_target_pairs={{0,1},{1,0},{2,3},{3,2},{4,5},{5,4},{6,7},{7,6},{8,9},{9,8},{10,11... | collective-permute-start | bytes 3145736 | tf_op jit(solution)/shard_map/ppermute | solution.py:458
  119.3 10.7 %collective-permute-start.21 = (bf16[512,128]{1,0:T(8,128)(2,1)S(1)}, bf16[512,128]{1,0:T(8,128)(2,1)S(1)}, u32[]{:S(2)}, u32[]{:S(2)}) collective-permute-start(bf16[512,128]{1,0:T(8,128)(2,1)S(1)} %get-tuple-element.71), channel_id=1, source_target_pairs={{0,0},{1,4},{2,8},{3,12},{4,16},{5,20},{6,24},{7,28},{8,1},{9,5},{... | collective-permute-start | bytes 393224 | tf_op jit(solution)/shard_map/ppermute | solution.py:576
  120.0 28.5 %collective-permute-start.22 = (bf16[512,128]{1,0:T(8,128)(2,1)S(1)}, bf16[512,128]{1,0:T(8,128)(2,1)S(1)}, u32[]{:S(2)}, u32[]{:S(2)}) collective-permute-start(bf16[512,128]{1,0:T(8,128)(2,1)S(1)} %get-tuple-element.74), channel_id=1, source_target_pairs={{0,3},{1,7},{2,11},{3,15},{4,19},{5,23},{6,27},{7,31},{8,0},{9,4},... | collective-permute-start | bytes 393224 | tf_op jit(solution)/shard_map/ppermute | solution.py:576
  123.3 41.0 %collective-permute-start.23 = (bf16[512,128]{1,0:T(8,128)(2,1)S(1)}, bf16[512,128]{1,0:T(8,128)(2,1)S(1)}, u32[]{:S(2)}, u32[]{:S(2)}) collective-permute-start(bf16[512,128]{1,0:T(8,128)(2,1)S(1)} %get-tuple-element.73), channel_id=1, source_target_pairs={{0,2},{1,6},{2,10},{3,14},{4,18},{5,22},{6,26},{7,30},{8,3},{9,7},... | collective-permute-start | bytes 393224 | tf_op jit(solution)/shard_map/ppermute | solution.py:576
  125.1 39.3 %collective-permute-start.24 = (bf16[512,128]{1,0:T(8,128)(2,1)S(1)}, bf16[512,128]{1,0:T(8,128)(2,1)S(1)}, u32[]{:S(2)}, u32[]{:S(2)}) collective-permute-start(bf16[512,128]{1,0:T(8,128)(2,1)S(1)} %get-tuple-element.72), channel_id=1, source_target_pairs={{0,1},{1,5},{2,9},{3,13},{4,17},{5,21},{6,25},{7,29},{8,2},{9,6},{... | collective-permute-start | bytes 393224 | tf_op jit(solution)/shard_map/ppermute | solution.py:576
  130.0 34.6 %collective-permute-start.1 = (f32[32,128]{1,0:T(8,128)S(1)}, f32[32,128]{1,0:T(8,128)S(1)}, u32[]{:S(2)}, u32[]{:S(2)}) collective-permute-start(f32[32,128]{1,0:T(8,128)S(1)} %select_reduce_fusion.1), channel_id=1, source_target_pairs={{0,1},{1,0},{2,3},{3,2},{4,5},{5,4},{6,7},{7,6},{8,9},{9,8},{10,11... | collective-permute-start | bytes 49160 | tf_op jit(solution)/shard_map/ppermute | solution.py:458
  164.5 2.0 collective-permute-start.25
  169.3 26.1 %collective-permute-start.3 = (bf16[512,128]{1,0:T(8,128)(2,1)}, bf16[512,128]{1,0:T(8,128)(2,1)S(1)}, u32[]{:S(2)}, u32[]{:S(2)}) collective-permute-start(bf16[512,128]{1,0:T(8,128)(2,1)} %get-tuple-element.63), channel_id=1, source_target_pairs={{0,0},{4,1},{8,2},{12,3},{16,4},{20,5},{24,6},{28,7},{1,8},{5,9},{... | collective-permute-start | bytes 393224 | tf_op jit(solution)/shard_map/ppermute | solution.py:610
  170.9 24.6 %collective-permute-start.4 = (bf16[512,128]{1,0:T(8,128)(2,1)S(1)}, bf16[512,128]{1,0:T(8,128)(2,1)S(1)}, u32[]{:S(2)}, u32[]{:S(2)}) collective-permute-start(bf16[512,128]{1,0:T(8,128)(2,1)S(1)} %get-tuple-element.66), channel_id=1, source_target_pairs={{3,0},{7,1},{11,2},{15,3},{19,4},{23,5},{27,6},{31,7},{0,8},{4,9},... | collective-permute-start | bytes 393224 | tf_op jit(solution)/shard_map/ppermute | solution.py:610
  187.7 7.9 %collective-permute-start.5 = (bf16[512,128]{1,0:T(8,128)(2,1)S(1)}, bf16[512,128]{1,0:T(8,128)(2,1)S(1)}, u32[]{:S(2)}, u32[]{:S(2)}) collective-permute-start(bf16[512,128]{1,0:T(8,128)(2,1)S(1)} %get-tuple-element.65), channel_id=1, source_target_pairs={{2,0},{6,1},{10,2},{14,3},{18,4},{22,5},{26,6},{30,7},{3,8},{7,9},... | collective-permute-start | bytes 393224 | tf_op jit(solution)/shard_map/ppermute | solution.py:610
  189.9 6.4 %collective-permute-start.6 = (bf16[512,128]{1,0:T(8,128)(2,1)S(1)}, bf16[512,128]{1,0:T(8,128)(2,1)S(1)}, u32[]{:S(2)}, u32[]{:S(2)}) collective-permute-start(bf16[512,128]{1,0:T(8,128)(2,1)S(1)} %get-tuple-element.64), channel_id=1, source_target_pairs={{1,0},{5,1},{9,2},{13,3},{17,4},{21,5},{25,6},{29,7},{2,8},{6,9},{... | collective-permute-start | bytes 393224 | tf_op jit(solution)/shard_map/ppermute | solution.py:610
  195.7 0.7 copy-start.6
  196.3 0.7 copy-start.7
  208.0 50.1 %all-to-all-start.3 = ((bf16[32,64,256]{2,1,0:T(8,128)(2,1)}), bf16[32,64,256]{2,1,0:T(8,128)(2,1)}, u32[]{:S(2)}, u32[]{:S(2)}) async-start(bf16[32,64,256]{2,1,0:T(8,128)(2,1)} %bitcast.185), calls=%async_computation.3 | async-start | bytes 2097152 | tf_op jit(solution)/shard_map/all_to_all | solution.py:464
  218.5 1.2 copy-start.1
  219.7 26.0 %copy-start.8 = (bf16[128,256]{1,0:T(8,128)(2,1)S(1)}, bf16[128,256]{1,0:T(8,128)(2,1)}, u32[]{:S(2)}) copy-start(bf16[128,256]{1,0:T(8,128)(2,1)} %get-tuple-element.51) | copy-start | bytes 196612
  240.8 15.9 %collective-permute-start.26 = (bf16[32,64,256]{2,1,0:T(8,128)(2,1)S(1)}, bf16[32,64,256]{2,1,0:T(8,128)(2,1)S(1)}, u32[]{:S(2)}, u32[]{:S(2)}) collective-permute-start(bf16[32,64,256]{2,1,0:T(8,128)(2,1)S(1)} %slice.98), channel_id=1, source_target_pairs={{0,1},{1,0},{2,3},{3,2},{4,5},{5,4},{6,7},{7,6},{8,9},{9,8},{10,11... | collective-permute-start | bytes 3145736 | tf_op jit(solution)/shard_map/ppermute | solution.py:458
  240.9 21.8 %collective-permute-start.13 = (bf16[128,256]{1,0:T(8,128)(2,1)S(1)}, bf16[128,256]{1,0:T(8,128)(2,1)S(1)}, u32[]{:S(2)}, u32[]{:S(2)}) collective-permute-start(bf16[128,256]{1,0:T(8,128)(2,1)S(1)} %get-tuple-element.39), channel_id=1, source_target_pairs={{0,7},{1,6},{2,5},{3,4},{4,3},{5,2},{6,1},{7,0},{8,15},{9,14},{10,... | collective-permute-start | bytes 196616 | tf_op jit(solution)/shard_map/ppermute | solution.py:475
  243.4 11.6 %collective-permute-start.11 = (bf16[128,256]{1,0:T(8,128)(2,1)}, bf16[128,256]{1,0:T(8,128)(2,1)S(1)}, u32[]{:S(2)}, u32[]{:S(2)}) collective-permute-start(bf16[128,256]{1,0:T(8,128)(2,1)} %get-tuple-element.41), channel_id=1, source_target_pairs={{0,5},{1,4},{2,7},{3,6},{4,1},{5,0},{6,3},{7,2},{8,13},{9,12},{10,... | collective-permute-start | bytes 196616 | tf_op jit(solution)/shard_map/ppermute | solution.py:475
  243.7 7.7 %collective-permute-start.9 = (bf16[128,256]{1,0:T(8,128)(2,1)}, bf16[128,256]{1,0:T(8,128)(2,1)S(1)}, u32[]{:S(2)}, u32[]{:S(2)}) collective-permute-start(bf16[128,256]{1,0:T(8,128)(2,1)} %get-tuple-element.43), channel_id=1, source_target_pairs={{0,3},{1,2},{2,1},{3,0},{4,7},{5,6},{6,5},{7,4},{8,11},{9,10},{10,... | collective-permute-start | bytes 196616 | tf_op jit(solution)/shard_map/ppermute | solution.py:475
  244.2 1.5 collective-permute-start.7
  245.7 4.3 %collective-permute-start.8 = (bf16[128,256]{1,0:T(8,128)(2,1)S(1)}, bf16[128,256]{1,0:T(8,128)(2,1)S(1)}, u32[]{:S(2)}, u32[]{:S(2)}) collective-permute-start(bf16[128,256]{1,0:T(8,128)(2,1)S(1)} %copy-done.8), channel_id=1, source_target_pairs={{0,2},{1,3},{2,0},{3,1},{4,6},{5,7},{6,4},{7,5},{8,10},{9,11},{10,... | collective-permute-start | bytes 196616 | tf_op jit(solution)/shard_map/ppermute | solution.py:475
  250.0 5.0 %collective-permute-start.10 = (bf16[128,256]{1,0:T(8,128)(2,1)S(1)}, bf16[128,256]{1,0:T(8,128)(2,1)S(1)}, u32[]{:S(2)}, u32[]{:S(2)}) collective-permute-start(bf16[128,256]{1,0:T(8,128)(2,1)S(1)} %get-tuple-element.49), channel_id=1, source_target_pairs={{0,4},{1,5},{2,6},{3,7},{4,0},{5,1},{6,2},{7,3},{8,12},{9,13},{10,... | collective-permute-start | bytes 196616 | tf_op jit(solution)/shard_map/ppermute | solution.py:475
  251.4 5.2 %collective-permute-start.12 = (bf16[128,256]{1,0:T(8,128)(2,1)S(1)}, bf16[128,256]{1,0:T(8,128)(2,1)S(1)}, u32[]{:S(2)}, u32[]{:S(2)}) collective-permute-start(bf16[128,256]{1,0:T(8,128)(2,1)S(1)} %get-tuple-element.47), channel_id=1, source_target_pairs={{0,6},{1,7},{2,4},{3,5},{4,2},{5,3},{6,0},{7,1},{8,14},{9,15},{10,... | collective-permute-start | bytes 196616 | tf_op jit(solution)/shard_map/ppermute | solution.py:475
  258.1 30.9 %all-to-all-start.2 = ((bf16[32,64,256]{2,1,0:T(8,128)(2,1)}), bf16[32,64,256]{2,1,0:T(8,128)(2,1)S(1)}, u32[]{:S(2)}, u32[]{:S(2)}) async-start(bf16[32,64,256]{2,1,0:T(8,128)(2,1)} %add_convert_fusion), calls=%async_computation.2 | async-start | bytes 2097152 | tf_op jit(solution)/shard_map/all_to_all | solution.py:464
  262.9 2.6 collective-permute-start.14
  269.0 22.8 %collective-permute-start.15 = (bf16[128,1024]{1,0:T(8,128)(2,1)S(1)}, bf16[128,1024]{1,0:T(8,128)(2,1)S(1)}, u32[]{:S(2)}, u32[]{:S(2)}) collective-permute-start(bf16[128,1024]{1,0:T(8,128)(2,1)S(1)} %slice.94), channel_id=1, source_target_pairs={{0,1},{1,0},{2,3},{3,2},{4,5},{5,4},{6,7},{7,6},{8,9},{9,8},{10,11... | collective-permute-start | bytes 786440 | tf_op jit(solution)/shard_map/ppermute | solution.py:458
Sparse Core Ops, SparseCore 0:
  70.5 110.7 all-gather.1

commit v4 on v2

--- a/solution.py
+++ b/solution.py
@@ -474,6 +474,21 @@
         kept, passed = jnp.where(first, even, odd), jnp.where(first, odd, even)
         return kept.reshape(rows.shape[0], -1), passed.reshape(rows.shape[0], -1)
 
+    plane = peers // PLANES
+    index = lax.axis_index("ctx")
+    level, here, seat = index // plane, index % plane, index % PLANES
+    up = [
+        [
+            (PLANES * place + (tier - step) % PLANES, tier * plane + place)
+            for tier in range(PLANES)
+            for place in range(plane)
+        ]
+        for step in range(PLANES)
+    ]
+
+    def pick(blocks, which):
+        return lax.dynamic_index_in_dim(blocks, which, axis=0, keepdims=False)
+
     def moved(block, mask):
         return lax.ppermute(block, "ctx", [(device, device ^ mask) for device in range(peers)])
 
@@ -528,6 +543,7 @@
 
     grad_kept, grad_passed = own_half(out_grad)
     grad_pair = jnp.concatenate([grad_kept, exchange(grad_passed)], axis=0)
+    grad_pair, result, log_slots = lax.optimization_barrier((grad_pair, result, log_slots))
     grad_part = jnp.dot(grad_pair, half_weight, preferred_element_type=jnp.float32)
     attended_grad = (grad_part[:token_rows] + exchange(grad_part[token_rows:])).astype(
         jnp.bfloat16
@@ -566,18 +582,21 @@
     mixed_odd = jnp.where(first, mixed_got, mixed_kept).reshape(token_rows, heads, 1, -1)
     mixed = jnp.concatenate([mixed_even, mixed_odd], axis=2).reshape(token_rows, row_width)
 
-    plane = peers // PLANES
-    groups = [[level * plane + place for place in range(plane)] for level in range(PLANES)]
-    plane_attended = lax.all_to_all(
-        attended_rows, "ctx", split_axis=1, concat_axis=0, tiled=True, axis_index_groups=groups
-    ).reshape(plane, token_rows, row_width // plane)
-    here = lax.axis_index("ctx") % plane
+    attended_half = attended[:, :half].reshape(PLANES, plane * half, HEAD_DIM)
+    arrived = jnp.stack(
+        [
+            lax.ppermute(pick(attended_half, (seat + step) % PLANES), "ctx", up[step])
+            for step in range(PLANES)
+        ]
+    )
+    plane_attended = (
+        jnp.stack([pick(arrived, (level - place) % PLANES) for place in range(PLANES)])
+        .reshape(2, 2, plane, half, HEAD_DIM)
+        .transpose(2, 1, 3, 0, 4)
+        .reshape(plane, token_rows, row_width // plane)
+    )
     plane_attended = jnp.concatenate(
-        [
-            lax.dynamic_index_in_dim(plane_attended, here ^ mask, axis=0, keepdims=False)
-            for mask in (0, 2, 4, 6, 1, 3, 5, 7)
-        ],
-        axis=0,
+        [pick(plane_attended, here ^ mask) for mask in (0, 2, 4, 6, 1, 3, 5, 7)], axis=0
     )
     left, right = out_grad[:, : row_width // 2], out_grad[:, row_width // 2 :]
     left_two = jnp.concatenate([left, moved(left, 2)], axis=0)

time: 284 us -> 277 us (0.975)
  waiting for transfers between devices: 119 us -> 103 us
  starting transfers between devices: 37.7 us -> 50.7 us
  local copies, waits for them, and re-layouts: 35.1 us -> 31.5 us
    all_gather x1, waiting for transfers between devices: 43.2 us -> 9.01 us  [head_owner_device(): lax.all_gather(out_weight, 'ctx', axis=0, tiled=True, axis_index_groups=[...]
    ppermute x4, waiting for transfers between devices: 13 us -> 26.4 us  [moved(): lax.ppermute(block, 'ctx', [(device, device ^ mask) for device in range(p...]
    all_to_all x5, waiting for transfers between devices: 46.3 us -> 56.9 us  [everywhere(): return lax.all_to_all(block, 'ctx', split_axis=0, concat_axis=0, tiled=True)]
    ppermute x0 -> x4, starting transfers between devices: none -> 10.3 us  [head_owner_device(): lax.ppermute(pick(attended_half, (seat + step) % PLANES), 'ctx', up[step])]
    all_to_all x1 -> x0, waiting for transfers between devices: 9.7 us -> none  [head_owner_device(): lax.all_to_all(attended_rows, 'ctx', split_axis=1, concat_axis=0, tiled=T...]
    all_to_all x5, starting transfers between devices: 24.6 us -> 33.2 us  [everywhere(): return lax.all_to_all(block, 'ctx', split_axis=0, concat_axis=0, tiled=True)]
    all_to_all x1 -> x0, starting transfers between devices: 4.14 us -> none  [head_owner_device(): lax.all_to_all(attended_rows, 'ctx', split_axis=1, concat_axis=0, tiled=T...]
    all_to_all x2 -> x0, local copies, waits for them, and re-layouts: 3.94 us -> none  [head_owner_device(): lax.all_to_all(attended_rows, 'ctx', split_axis=1, concat_axis=0, tiled=T...]
  transfers between devices with their start and end apart: 21 -> 24, of which waited for: 10 -> 12; matrix products, arithmetic and copies ran while one was open for 21% -> 21% of each run, Pallas kernels for 15% -> 15%
where the time goes in v4:
time: 277 us; the launch traced here: 275 us
  waiting for transfers between devices  103 us (37%)
  starting transfers between devices  50.7 us (18%)
  Pallas kernels  42.5 us (15%)
  local copies, waits for them, and re-layouts  31.5 us (11%)
  other arithmetic  21.8 us (8%)
  between operations  14.6 us (5%)
  matrix products  11.6 us (4%)
    all_to_all x5, waiting for transfers between devices, everywhere(): return lax.all_to_all(block, 'ctx', split_axis=0, concat_axis=0, tiled=True)  56.9 us
    pallas_call x2, Pallas kernels, kernel_call(): pl.pallas_call(body, out_shape=out_shape, in_specs=[pl.BlockSpec(memory_s...  42.5 us
    all_to_all x5, starting transfers between devices, everywhere(): return lax.all_to_all(block, 'ctx', split_axis=0, concat_axis=0, tiled=True)  33.2 us
    ppermute x4, waiting for transfers between devices, moved(): lax.ppermute(block, 'ctx', [(device, device ^ mask) for device in range(p...  26.4 us
    unnamed x28, local copies, waits for them, and re-layouts  13.3 us
    ppermute x4, starting transfers between devices, head_owner_device(): lax.ppermute(pick(attended_half, (seat + step) % PLANES), 'ctx', up[step])  10.3 us
    ppermute x10, waiting for transfers between devices, exchange(): return lax.ppermute(block, 'ctx', partners)  9.59 us
    all_gather x1, waiting for transfers between devices, head_owner_device(): lax.all_gather(out_weight, 'ctx', axis=0, tiled=True, axis_index_groups=[...  9.01 us
  transfers between devices with their start and end apart: 24, of which 12 were waited for; matrix products, arithmetic and copies ran while one was open for 21% of the time, Pallas kernels for 15%

profile of v4, /device:TPU:0, one launch (start us, length us, event | category | flops | bytes accessed | tf_op | source)
XLA Modules:
  0.0 275.3 jit_solution(53003270975572189)
XLA Ops:
  8.6 1.1 copy.127
  9.7 1.1 copy.126
  11.4 1.1 pad_maximum_fusion
  12.5 7.3 %all-to-all-start = ((bf16[32,72,256]{2,1,0:T(8,128)(2,1)}), bf16[32,72,256]{2,1,0:T(8,128)(2,1)S(1)}, u32[]{:S(2)}, u32[]{:S(2)}) async-start(bf16[32,72,256]{2,1,0:T(8,128)(2,1)} %pad_maximum_fusion), calls=%async_computation | async-start | bytes 2359296 | tf_op jit(solution)/shard_map/all_to_all | solution.py:461
  20.6 1.2 collective-permute-done
  21.8 0.9 pad_maximum_fusion.3
  22.6 43.0 %all-to-all-done.mine_ref = bf16[32,72,256]{2,1,0:T(8,128)(2,1)S(1)} async-done(((bf16[32,72,256]{2,1,0:T(8,128)(2,1)}), bf16[32,72,256]{2,1,0:T(8,128)(2,1)S(1)}, u32[]{:S(2)}, u32[]{:S(2)}) %all-to-all-start) | async-done | bytes 1179680 | tf_op jit(solution)/shard_map/all_to_all | solution.py:461
  67.0 1.3 convert_reduce_fusion.1
  68.5 21.4 %shard_map.84 = (bf16[32,128,128]{2,1,0:T(8,128)(2,1)S(1)}, f32[32,256]{1,0:T(8,128)S(1)}) custom-call(bf16[32,72,256]{2,1,0:T(8,128)(2,1)S(1)} %all-to-all-done.mine_ref, bf16[32,64,256]{2,1,0:T(8,128)(2,1)S(1)} %collective-permute-done.1.other_ref, s32[32,128]{1,0:T(8,128)S(1)} %add_select_fusion.slot_ref, f32[32,256]{1,0:T(8,128)S(1)} %select_select_fusion.code_ref), custom_call_target="tpu_custom_call" | custom-call | tf_op jit(solution)/shard_map/pallas_call | solution.py:433
  90.0 9.0 %all-gather.2.cloned.1.call-done = bf16[1024,2048]{1,0:T(8,128)(2,1)} async-done(((bf16[64,2048]{1,0:T(8,128)(2,1)}), bf16[1024,2048]{1,0:T(8,128)(2,1)}) %all-gather.2.cloned.1.call-update) | async-done | bytes 4194320 | tf_op jit(solution)/shard_map/all_gather | solution.py:495
  99.0 3.6 %fusion.41 = f32[256,2048]{1,0:T(8,128)S(1)} fusion(bf16[256,1024]{0,1:T(8,128)(2,1)} %pad_maximum_fusion.3, bf16[1024,2048]{1,0:T(8,128)(2,1)} %all-gather.2.cloned.1.call-done), kind=kOutput, calls=%fused_computation.103 | convolution fusion | flops 1073741824 | bytes 6815744 | tf_op jit(solution)/shard_map/dot_general | solution.py:547
  102.8 0.9 copy-done.4
  104.4 1.5 collective-permute-start.10
  105.9 6.3 %collective-permute-done.10 = bf16[128,1024]{1,0:T(8,128)(2,1)S(1)} collective-permute-done((bf16[128,1024]{1,0:T(8,128)(2,1)S(1)}, bf16[128,1024]{1,0:T(8,128)(2,1)S(1)}, u32[]{:S(2)}, u32[]{:S(2)}) %collective-permute-start.10) | collective-permute-done | bytes 262176 | tf_op jit(solution)/shard_map/ppermute | solution.py:493
  112.2 0.9 pad_maximum_fusion.6
  113.1 1.4 collective-permute-start.11
  115.4 0.9 copy.114
  116.3 3.6 %all-to-all-start.2 = ((bf16[32,64,128]{2,1,0:T(8,128)(2,1)}), bf16[32,64,128]{2,1,0:T(8,128)(2,1)}, u32[]{:S(2)}, u32[]{:S(2)}) async-start(bf16[32,64,128]{2,1,0:T(8,128)(2,1)} %bitcast.117), calls=%async_computation.2 | async-start | bytes 1048576 | tf_op jit(solution)/shard_map/all_to_all | solution.py:461
  119.9 16.6 %collective-permute-done.8 = bf16[128,1024]{1,0:T(8,128)(2,1)} collective-permute-done((bf16[128,1024]{1,0:T(8,128)(2,1)}, bf16[128,1024]{1,0:T(8,128)(2,1)}, u32[]{:S(2)}, u32[]{:S(2)}) %collective-permute-start.8) | collective-permute-done | bytes 262176 | tf_op jit(solution)/shard_map/ppermute | solution.py:493
  136.5 1.9 pad_maximum_fusion.5
  138.4 1.5 collective-permute-start.9
  139.9 1.9 fusion.37
  142.5 1.0 copy.108
  143.6 1.4 select_reduce_fusion.1
  145.6 3.5 %collective-permute-done.9 = bf16[256,1024]{1,0:T(8,128)(2,1)} collective-permute-done((bf16[256,1024]{1,0:T(8,128)(2,1)}, bf16[256,1024]{1,0:T(8,128)(2,1)}, u32[]{:S(2)}, u32[]{:S(2)}) %collective-permute-start.9) | collective-permute-done | bytes 524320 | tf_op jit(solution)/shard_map/ppermute | solution.py:493
  149.1 3.1 %maximum_maximum_fusion = bf16[512,2048]{1,0:T(8,128)(2,1)} fusion(bf16[128,1024]{1,0:T(8,128)(2,1)} %get-tuple-element.50, bf16[128,1024]{1,0:T(8,128)(2,1)} %copy-done.5, bf16[128,1024]{1,0:T(8,128)(2,1)} %get-tuple-element.49, bf16[128,1024]{1,0:T(8,128)(2,1)} %copy-done.2, bf16[256,1024]{1,0:T(8,128)(2,1)} %collective-permute-done.9, ...), kind=kLoop, calls=%fused_computation.25 | loop fusion | flops 14680064 | bytes 4194304 | tf_op jit(solution)/shard_map/concatenate | solution.py:610
  152.9 1.3 fusion.35
  154.2 2.8 %collective-permute-done.7 = bf16[32,64,128]{2,1,0:T(8,128)(2,1)S(1)} collective-permute-done((bf16[32,64,128]{2,1,0:T(8,128)(2,1)}, bf16[32,64,128]{2,1,0:T(8,128)(2,1)S(1)}, u32[]{:S(2)}, u32[]{:S(2)}) %collective-permute-start.7) | collective-permute-done | bytes 524320 | tf_op jit(solution)/shard_map/ppermute | solution.py:455
  157.0 3.6 %fusion.23 = (f32[32,128]{1,0:T(8,128)S(1)}, bf16[32,128,128]{2,1,0:T(8,128)(2,1)S(1)}, bf16[32,128,128]{2,1,0:T(8,128)(2,1)S(1)}) fusion(bf16[32,64,128]{2,1,0:T(8,128)(2,1)S(1)} %collective-permute-done.7, bf16[32,64,128]{2,1,0:T(8,128)(2,1)} %all-to-all-done.2, bf16[32,64,128]{2,1,0:T(8,128)(2,1)S(1)} %get-tuple-element.44, ...), kind=kLoop, calls=%fused_computation.24 | loop fusion | flops 9433088 | bytes 5292032 | tf_op jit(solution)/shard_map/reduce_sum | solution.py:568
  160.7 0.8 copy-done.1
  162.2 4.8 %collective-permute-start.16 = (bf16[512,128]{1,0:T(8,128)(2,1)}, bf16[512,128]{1,0:T(8,128)(2,1)}, u32[]{:S(2)}, u32[]{:S(2)}) collective-permute-start(bf16[512,128]{1,0:T(8,128)(2,1)} %get-tuple-element.56), channel_id=1, source_target_pairs={{1,0},{5,1},{9,2},{13,3},{17,4},{21,5},{25,6},{29,7},{2,8},{6,9},{... | collective-permute-start | bytes 393224 | tf_op jit(solution)/shard_map/ppermute | solution.py:588
  167.0 1.8 collective-permute-start.15
  168.8 2.3 collective-permute-start.14
  171.2 1.3 collective-permute-start.13
  172.5 6.6 %all-to-all-start.1 = ((bf16[32,64,128]{2,1,0:T(8,128)(2,1)}), bf16[32,64,128]{2,1,0:T(8,128)(2,1)}, u32[]{:S(2)}, u32[]{:S(2)}) async-start(bf16[32,64,128]{2,1,0:T(8,128)(2,1)} %copy-done.1), calls=%async_computation.1 | async-start | bytes 1048576 | tf_op jit(solution)/shard_map/all_to_all | solution.py:461
  179.1 1.2 pad_maximum_fusion.7
  180.4 1.3 copy.115
  181.7 2.2 reshape.254
  183.9 0.8 bitcast_dynamic-update-slice_fusion.7
  184.7 0.8 bitcast_dynamic-update-slice_fusion.6
  185.6 0.8 bitcast_dynamic-update-slice_fusion.5
  186.4 0.8 bitcast_dynamic-update-slice_fusion.4
  187.3 0.8 bitcast_dynamic-update-slice_fusion.3
  188.1 0.8 bitcast_dynamic-update-slice_fusion.2
  189.0 0.8 bitcast_dynamic-update-slice_fusion.1
  189.8 0.8 bitcast_dynamic-update-slice_fusion
  190.7 4.5 %fusion.19 = bf16[2048,256]{1,0:T(8,128)(2,1)} fusion(bf16[1024,256]{1,0:T(8,128)(2,1)S(1)} %bitcast_dynamic-update-slice_fusion, bf16[512,2048]{1,0:T(8,128)(2,1)} %collective-permute-done.12, bf16[128,1024]{1,0:T(8,128)(2,1)} %get-tuple-element.50, bf16[128,1024]{1,0:T(8,128)(2,1)} %copy-done.5, bf16[128,1024]{1,0:T(8,128)(2,1)} %get-tuple-element.49, ...), kind=kOutput, calls=%fused_computation.22 | convolution fusion | flops 1108344832 | bytes 5767168 | tf_op jit(solution)/shard_map/dot_general | solution.py:326
  195.2 10.1 %all-to-all-start.4 = ((bf16[32,64,256]{2,1,0:T(8,128)(2,1)}), bf16[32,64,256]{2,1,0:T(8,128)(2,1)}, u32[]{:S(2)}, u32[]{:S(2)}) async-start(bf16[32,64,256]{2,1,0:T(8,128)(2,1)} %bitcast.129), calls=%async_computation.4 | async-start | bytes 2097152 | tf_op jit(solution)/shard_map/all_to_all | solution.py:461
  205.3 1.4 select_reduce_fusion
  207.6 1.0 copy.118.shift_ref
  208.6 21.0 %shard_map.85 = bf16[32,128,256]{2,1,0:T(8,128)(2,1)S(1)} custom-call(bf16[32,72,256]{2,1,0:T(8,128)(2,1)S(1)} %all-to-all-done.mine_ref, bf16[32,64,256]{2,1,0:T(8,128)(2,1)S(1)} %collective-permute-done.1.other_ref, bf16[32,128,128]{2,1,0:T(8,128)(2,1)S(1)} %get-tuple-element.16.grad_ref, s32[32,128]{1,0:T(8,128)S(1)} %add_select_fusion.slot_ref, ...), custom_call_target="tpu_custom_call" | custom-call | tf_op jit(solution)/shard_map/pallas_call | solution.py:433
  229.8 2.6 collective-permute-done.17
  232.4 1.4 add_convert_fusion
  233.8 5.6 %all-to-all-start.3 = ((bf16[32,64,256]{2,1,0:T(8,128)(2,1)}), bf16[32,64,256]{2,1,0:T(8,128)(2,1)S(1)}, u32[]{:S(2)}, u32[]{:S(2)}) async-start(bf16[32,64,256]{2,1,0:T(8,128)(2,1)} %add_convert_fusion), calls=%async_computation.3 | async-start | bytes 2097152 | tf_op jit(solution)/shard_map/all_to_all | solution.py:461
  239.4 1.4 copy.110
  241.2 1.7 collective-permute-done.4
  242.9 3.5 %convolution_convert_fusion = bf16[256,1024]{1,0:T(8,128)(2,1)S(1)} fusion(bf16[1024,2048]{1,0:T(8,128)(2,1)} %all-gather.2.cloned.1.call-done, bf16[128,2048]{1,0:T(8,128)(2,1)S(1)} %collective-permute-done.4, bf16[128,2048]{1,0:T(8,128)(2,1)S(1)} %bitcast.142), kind=kOutput, calls=%fused_computation.30 | convolution fusion | flops 1076101120 | bytes 5767168 | tf_op jit(solution)/shard_map/dot_general | solution.py:326
  246.7 1.3 collective-permute-done.5
  248.5 1.0 copy.122
  249.5 1.4 convert_reduce_fusion
  250.9 0.8 copy.125
  251.8 13.8 %all-to-all-done.3 = bf16[32,64,256]{2,1,0:T(8,128)(2,1)S(1)} async-done(((bf16[32,64,256]{2,1,0:T(8,128)(2,1)}), bf16[32,64,256]{2,1,0:T(8,128)(2,1)S(1)}, u32[]{:S(2)}, u32[]{:S(2)}) %all-to-all-start.3) | async-done | bytes 1048608 | tf_op jit(solution)/shard_map/all_to_all | solution.py:461
  266.3 0.9 copy.140
  267.5 0.9 copy.139
  (88 shorter events, 12.1 us)
Async XLA Ops:
  7.2 91.8 %all-gather.2.cloned.1.call-start = ((), (), s32[]{:S(2)}) async-start(), calls=%async_computation.5 | async-start | bytes 4456448 | tf_op jit(solution)/shard_map/all_gather | solution.py:495
  11.4 8.5 %copy-start.3 = (bf16[128,2048]{1,0:T(8,128)(2,1)S(1)}, bf16[128,2048]{1,0:T(8,128)(2,1)}, u32[]{:S(2)}) copy-start(bf16[128,2048]{1,0:T(8,128)(2,1)} %param.7) | copy-start | bytes 1572868
  12.5 53.1 %all-to-all-start = ((bf16[32,72,256]{2,1,0:T(8,128)(2,1)}), bf16[32,72,256]{2,1,0:T(8,128)(2,1)S(1)}, u32[]{:S(2)}, u32[]{:S(2)}) async-start(bf16[32,72,256]{2,1,0:T(8,128)(2,1)} %pad_maximum_fusion), calls=%async_computation | async-start | bytes 2359296 | tf_op jit(solution)/shard_map/all_to_all | solution.py:461
  20.2 1.6 collective-permute-start
  65.8 2.7 collective-permute-start.1
  90.0 49.9 %copy-start = (bf16[32,128,128]{2,1,0:T(8,128)(2,1)}, bf16[32,128,128]{2,1,0:T(8,128)(2,1)S(1)}, u32[]{:S(2)}) copy-start(bf16[32,128,128]{2,1,0:T(8,128)(2,1)S(1)} %get-tuple-element.14) | copy-start | bytes 3145732
  102.6 1.0 copy-start.4
  102.7 12.4 %collective-permute-start.6 = (f32[128,2048]{1,0:T(8,128)S(1)}, f32[128,2048]{1,0:T(8,128)S(1)}, u32[]{:S(2)}, u32[]{:S(2)}) collective-permute-start(f32[128,2048]{1,0:T(8,128)S(1)} %slice.117), channel_id=1, source_target_pairs={{0,1},{1,0},{2,3},{3,2},{4,5},{5,4},{6,7},{7,6},{8,9},{9,8},{10,11... | collective-permute-start | bytes 3145736 | tf_op jit(solution)/shard_map/ppermute | solution.py:455
  104.4 7.8 %copy-start.2 = (bf16[128,1024]{1,0:T(8,128)(2,1)}, bf16[128,1024]{1,0:T(8,128)(2,1)S(1)}, u32[]{:S(2)}) copy-start(bf16[128,1024]{1,0:T(8,128)(2,1)S(1)} %get-tuple-element.48) | copy-start | bytes 786436
  104.4 7.8 %collective-permute-start.10 = (bf16[128,1024]{1,0:T(8,128)(2,1)S(1)}, bf16[128,1024]{1,0:T(8,128)(2,1)S(1)}, u32[]{:S(2)}, u32[]{:S(2)}) collective-permute-start(bf16[128,1024]{1,0:T(8,128)(2,1)S(1)} %get-tuple-element.48), channel_id=1, source_target_pairs={{0,4},{1,5},{2,6},{3,7},{4,0},{5,1},{6,2},{7,3},{8,12},{9,13},{10,... | collective-permute-start | bytes 786440 | tf_op jit(solution)/shard_map/ppermute | solution.py:493
  112.2 2.9 %copy-start.5 = (bf16[128,1024]{1,0:T(8,128)(2,1)}, bf16[128,1024]{1,0:T(8,128)(2,1)S(1)}, u32[]{:S(2)}) copy-start(bf16[128,1024]{1,0:T(8,128)(2,1)S(1)} %collective-permute-done.10) | copy-start | bytes 786436
  113.1 26.8 %collective-permute-start.11 = (bf16[256,1024]{1,0:T(8,128)(2,1)}, bf16[256,1024]{1,0:T(8,128)(2,1)}, u32[]{:S(2)}, u32[]{:S(2)}) collective-permute-start(bf16[256,1024]{1,0:T(8,128)(2,1)} %pad_maximum_fusion.6), channel_id=1, source_target_pairs={{0,2},{1,3},{2,0},{3,1},{4,6},{5,7},{6,4},{7,5},{8,10},{9,11},{10,... | collective-permute-start | bytes 1572872 | tf_op jit(solution)/shard_map/ppermute | solution.py:493
  114.6 22.0 %collective-permute-start.8 = (bf16[128,1024]{1,0:T(8,128)(2,1)}, bf16[128,1024]{1,0:T(8,128)(2,1)}, u32[]{:S(2)}, u32[]{:S(2)}) collective-permute-start(bf16[128,1024]{1,0:T(8,128)(2,1)} %get-tuple-element.47), channel_id=1, source_target_pairs={{0,2},{1,3},{2,0},{3,1},{4,6},{5,7},{6,4},{7,5},{8,10},{9,11},{10,... | collective-permute-start | bytes 786440 | tf_op jit(solution)/shard_map/ppermute | solution.py:493
  116.3 35.9 %all-to-all-start.2 = ((bf16[32,64,128]{2,1,0:T(8,128)(2,1)}), bf16[32,64,128]{2,1,0:T(8,128)(2,1)}, u32[]{:S(2)}, u32[]{:S(2)}) async-start(bf16[32,64,128]{2,1,0:T(8,128)(2,1)} %bitcast.117), calls=%async_computation.2 | async-start | bytes 1048576 | tf_op jit(solution)/shard_map/all_to_all | solution.py:461
  138.4 10.7 %collective-permute-start.9 = (bf16[256,1024]{1,0:T(8,128)(2,1)}, bf16[256,1024]{1,0:T(8,128)(2,1)}, u32[]{:S(2)}, u32[]{:S(2)}) collective-permute-start(bf16[256,1024]{1,0:T(8,128)(2,1)} %pad_maximum_fusion.5), channel_id=1, source_target_pairs={{0,4},{1,5},{2,6},{3,7},{4,0},{5,1},{6,2},{7,3},{8,12},{9,13},{10,... | collective-permute-start | bytes 1572872 | tf_op jit(solution)/shard_map/ppermute | solution.py:493
  139.9 13.0 %collective-permute-start.3 = (bf16[32,128,128]{2,1,0:T(8,128)(2,1)S(1)}, bf16[32,128,128]{2,1,0:T(8,128)(2,1)}, u32[]{:S(2)}, u32[]{:S(2)}) collective-permute-start(bf16[32,128,128]{2,1,0:T(8,128)(2,1)S(1)} %get-tuple-element.14), channel_id=1, source_target_pairs={{0,1},{1,0},{2,3},{3,2},{4,5},{5,4},{6,7},{7,6},{8,9},{9,8},{10,11... | collective-permute-start | bytes 3145736 | tf_op jit(solution)/shard_map/ppermute | solution.py:455
  145.0 7.7 %collective-permute-start.2 = (f32[32,128]{1,0:T(8,128)S(1)}, f32[32,128]{1,0:T(8,128)S(1)}, u32[]{:S(2)}, u32[]{:S(2)}) collective-permute-start(f32[32,128]{1,0:T(8,128)S(1)} %select_reduce_fusion.1), channel_id=1, source_target_pairs={{0,1},{1,0},{2,3},{3,2},{4,5},{5,4},{6,7},{7,6},{8,9},{9,8},{10,11... | collective-permute-start | bytes 49160 | tf_op jit(solution)/shard_map/ppermute | solution.py:455
  152.2 38.4 %collective-permute-start.12 = (bf16[512,2048]{1,0:T(8,128)(2,1)}, bf16[512,2048]{1,0:T(8,128)(2,1)}, u32[]{:S(2)}, u32[]{:S(2)}) collective-permute-start(bf16[512,2048]{1,0:T(8,128)(2,1)} %maximum_maximum_fusion), channel_id=1, source_target_pairs={{0,1},{1,0},{2,3},{3,2},{4,5},{5,4},{6,7},{7,6},{8,9},{9,8},{10,11... | collective-permute-start | bytes 6291464 | tf_op jit(solution)/shard_map/ppermute | solution.py:455
  152.2 4.7 %collective-permute-start.7 = (bf16[32,64,128]{2,1,0:T(8,128)(2,1)}, bf16[32,64,128]{2,1,0:T(8,128)(2,1)S(1)}, u32[]{:S(2)}, u32[]{:S(2)}) collective-permute-start(bf16[32,64,128]{2,1,0:T(8,128)(2,1)} %all-to-all-done.2), channel_id=1, source_target_pairs={{0,1},{1,0},{2,3},{3,2},{4,5},{5,4},{6,7},{7,6},{8,9},{9,8},{10,11... | collective-permute-start | bytes 1572872 | tf_op jit(solution)/shard_map/ppermute | solution.py:455
  160.6 0.8 copy-start.1
  162.2 16.9 %collective-permute-start.16 = (bf16[512,128]{1,0:T(8,128)(2,1)}, bf16[512,128]{1,0:T(8,128)(2,1)}, u32[]{:S(2)}, u32[]{:S(2)}) collective-permute-start(bf16[512,128]{1,0:T(8,128)(2,1)} %get-tuple-element.56), channel_id=1, source_target_pairs={{1,0},{5,1},{9,2},{13,3},{17,4},{21,5},{25,6},{29,7},{2,8},{6,9},{... | collective-permute-start | bytes 393224 | tf_op jit(solution)/shard_map/ppermute | solution.py:588
  167.0 12.0 %collective-permute-start.15 = (bf16[512,128]{1,0:T(8,128)(2,1)}, bf16[512,128]{1,0:T(8,128)(2,1)}, u32[]{:S(2)}, u32[]{:S(2)}) collective-permute-start(bf16[512,128]{1,0:T(8,128)(2,1)} %get-tuple-element.57), channel_id=1, source_target_pairs={{2,0},{6,1},{10,2},{14,3},{18,4},{22,5},{26,6},{30,7},{3,8},{7,9},... | collective-permute-start | bytes 393224 | tf_op jit(solution)/shard_map/ppermute | solution.py:588
  168.8 10.2 %collective-permute-start.14 = (bf16[512,128]{1,0:T(8,128)(2,1)}, bf16[512,128]{1,0:T(8,128)(2,1)}, u32[]{:S(2)}, u32[]{:S(2)}) collective-permute-start(bf16[512,128]{1,0:T(8,128)(2,1)} %get-tuple-element.58), channel_id=1, source_target_pairs={{3,0},{7,1},{11,2},{15,3},{19,4},{23,5},{27,6},{31,7},{0,8},{4,9},... | collective-permute-start | bytes 393224 | tf_op jit(solution)/shard_map/ppermute | solution.py:588
  171.2 7.9 %collective-permute-start.13 = (bf16[512,128]{1,0:T(8,128)(2,1)S(1)}, bf16[512,128]{1,0:T(8,128)(2,1)}, u32[]{:S(2)}, u32[]{:S(2)}) collective-permute-start(bf16[512,128]{1,0:T(8,128)(2,1)S(1)} %get-tuple-element.55), channel_id=1, source_target_pairs={{0,0},{4,1},{8,2},{12,3},{16,4},{20,5},{24,6},{28,7},{1,8},{5,9},{... | collective-permute-start | bytes 393224 | tf_op jit(solution)/shard_map/ppermute | solution.py:588
  172.5 22.7 %all-to-all-start.1 = ((bf16[32,64,128]{2,1,0:T(8,128)(2,1)}), bf16[32,64,128]{2,1,0:T(8,128)(2,1)}, u32[]{:S(2)}, u32[]{:S(2)}) async-start(bf16[32,64,128]{2,1,0:T(8,128)(2,1)} %copy-done.1), calls=%async_computation.1 | async-start | bytes 1048576 | tf_op jit(solution)/shard_map/all_to_all | solution.py:461
  195.2 38.6 %all-to-all-start.4 = ((bf16[32,64,256]{2,1,0:T(8,128)(2,1)}), bf16[32,64,256]{2,1,0:T(8,128)(2,1)}, u32[]{:S(2)}, u32[]{:S(2)}) async-start(bf16[32,64,256]{2,1,0:T(8,128)(2,1)} %bitcast.129), calls=%async_computation.4 | async-start | bytes 2097152 | tf_op jit(solution)/shard_map/all_to_all | solution.py:461
  229.7 2.7 collective-permute-start.17
  233.8 31.8 %all-to-all-start.3 = ((bf16[32,64,256]{2,1,0:T(8,128)(2,1)}), bf16[32,64,256]{2,1,0:T(8,128)(2,1)S(1)}, u32[]{:S(2)}, u32[]{:S(2)}) async-start(bf16[32,64,256]{2,1,0:T(8,128)(2,1)} %add_convert_fusion), calls=%async_computation.3 | async-start | bytes 2097152 | tf_op jit(solution)/shard_map/all_to_all | solution.py:461
  240.9 2.0 collective-permute-start.4
  246.4 1.6 collective-permute-start.5
Sparse Core Ops, SparseCore 0:
  10.8 88.1 all-gather.1

commit v5 on v4

--- a/solution.py
+++ b/solution.py
@@ -510,6 +510,18 @@
         axis=1,
     )
     mine = everywhere(sent)
+    left, right = out_grad[:, : row_width // 2], out_grad[:, row_width // 2 :]
+    left_two = jnp.concatenate([left, moved(left, 2)], axis=0)
+    right_x = moved(right, 4)
+    right_two = jnp.concatenate([right, right_x], axis=0)
+    left_four = jnp.concatenate([left_two, moved(left_two, 4)], axis=0)
+    right_far = moved(right_two, 2)
+    right_four = jnp.concatenate(
+        [right, right_far[:token_rows], right_x, right_far[token_rows:]], axis=0
+    )
+    core_grad = jnp.concatenate([left_four, right_four], axis=1)
+    plane_grad = jnp.concatenate([core_grad, exchange(core_grad)], axis=0)
+    mine, plane_grad = lax.optimization_barrier((mine, plane_grad))
     other = exchange(mine[:, :half])
 
     all_buckets = mine[:, half].astype(jnp.int32).reshape(peers, 2, token_rows)
@@ -541,16 +553,6 @@
         (mine, other, slot, code),
     )
 
-    grad_kept, grad_passed = own_half(out_grad)
-    grad_pair = jnp.concatenate([grad_kept, exchange(grad_passed)], axis=0)
-    grad_pair, result, log_slots = lax.optimization_barrier((grad_pair, result, log_slots))
-    grad_part = jnp.dot(grad_pair, half_weight, preferred_element_type=jnp.float32)
-    attended_grad = (grad_part[:token_rows] + exchange(grad_part[token_rows:])).astype(
-        jnp.bfloat16
-    )
-    grad_mine = everywhere(by_head(attended_grad).reshape(peers, half, HEAD_DIM))
-    grad_rows = jnp.concatenate([grad_mine, exchange(grad_mine)], axis=1).astype(jnp.float32)
-
     chosen = slot[:, :, None] == jnp.arange(slots, dtype=jnp.int32)
     log_by_source = log_slots.reshape(peers, peers, per_peer).transpose(1, 0, 2).reshape(peers, slots)
     log_own = jnp.sum(jnp.where(chosen, log_by_source[:, None, :], 0.0), axis=2)
@@ -565,6 +567,18 @@
         + weight_other[:, :, None] * result_other.astype(jnp.float32)
     ).astype(jnp.bfloat16)
 
+    grad_kept, grad_passed = own_half(out_grad)
+    grad_pair = jnp.concatenate([grad_kept, exchange(grad_passed)], axis=0)
+    grad_pair, attended = lax.optimization_barrier((grad_pair, attended))
+    attended_rows = by_token(everywhere(attended[:, :half]))
+    grad_part = jnp.dot(grad_pair, half_weight, preferred_element_type=jnp.float32)
+    attended_grad = (grad_part[:token_rows] + exchange(grad_part[token_rows:])).astype(
+        jnp.bfloat16
+    )
+    attended_grad, attended_rows = lax.optimization_barrier((attended_grad, attended_rows))
+    grad_mine = everywhere(by_head(attended_grad).reshape(peers, half, HEAD_DIM))
+    grad_rows = jnp.concatenate([grad_mine, exchange(grad_mine)], axis=1).astype(jnp.float32)
+
     inner = jnp.sum(grad_rows * attended.astype(jnp.float32), axis=-1)
     shift = weight_own * inner
     query_grad = (weight_own[:, :, None] * grad_rows).astype(jnp.bfloat16)
@@ -573,8 +587,6 @@
         shift_slots.reshape(peers, peers, per_peer).transpose(1, 0, 2).reshape(peers, slots)
     )
 
-    attended_rows = by_token(everywhere(attended[:, :half]))
-
     attended_pair = jnp.concatenate([attended_rows, exchange(attended_rows)], axis=0)
     mixed_part = contract(attended_pair, half_weight, 1, 1).astype(jnp.bfloat16)
     mixed_kept, mixed_got = mixed_part[:token_rows], exchange(mixed_part[token_rows:])
@@ -598,17 +610,6 @@
     plane_attended = jnp.concatenate(
         [pick(plane_attended, here ^ mask) for mask in (0, 2, 4, 6, 1, 3, 5, 7)], axis=0
     )
-    left, right = out_grad[:, : row_width // 2], out_grad[:, row_width // 2 :]
-    left_two = jnp.concatenate([left, moved(left, 2)], axis=0)
-    right_x = moved(right, 4)
-    right_two = jnp.concatenate([right, right_x], axis=0)
-    left_four = jnp.concatenate([left_two, moved(left_two, 4)], axis=0)
-    right_far = moved(right_two, 2)
-    right_four = jnp.concatenate(
-        [right, right_far[:token_rows], right_x, right_far[token_rows:]], axis=0
-    )
-    core_grad = jnp.concatenate([left_four, right_four], axis=1)
-    plane_grad = jnp.concatenate([core_grad, exchange(core_grad)], axis=0)
     partial = contract(plane_grad, plane_attended, 0, 0) * (1.0 / math.sqrt(token_rows * peers))
     partial = partial.astype(jnp.bfloat16).reshape(
         peers, row_width // peers, row_width // plane

time: 277 us -> 285 us (1.029)
  other arithmetic: 21.8 us -> 38.5 us
  waiting for transfers between devices: 103 us -> 96.6 us
    all_to_all x5, waiting for transfers between devices: 56.9 us -> 68.6 us  [everywhere(): return lax.all_to_all(block, 'ctx', split_axis=0, concat_axis=0, tiled=True)]
    concatenate x1, other arithmetic: 3.11 us -> 13.3 us  [head_owner_device(): core_grad = jnp.concatenate([left_four, right_four], axis=1)]
    ppermute x4, waiting for transfers between devices: 26.4 us -> 16.3 us  [moved(): lax.ppermute(block, 'ctx', [(device, device ^ mask) for device in range(p...]
    all_gather x1, waiting for transfers between devices: 9.01 us -> 0.01 us  [head_owner_device(): lax.all_gather(out_weight, 'ctx', axis=0, tiled=True, axis_index_groups=[...]
    concatenate x0 -> x1, other arithmetic: none -> 5.19 us  [head_owner_device(): plane_grad = jnp.concatenate([core_grad, exchange(core_grad)], axis=0)]
    ppermute x4, waiting for transfers between devices: 0.01 us -> 5.12 us  [head_owner_device(): lax.ppermute(pick(attended_half, (seat + step) % PLANES), 'ctx', up[step])]
    all_to_all x5, starting transfers between devices: 33.2 us -> 28.4 us  [everywhere(): return lax.all_to_all(block, 'ctx', split_axis=0, concat_axis=0, tiled=True)]
    convert_element_type x0 -> x2, other arithmetic: none -> 3.35 us  [the longest x1 2.02 us: head_owner_device(): attended = (weight_own[:, :, None] * result.astype(jnp.float32) + weight_...]
  transfers between devices with their start and end apart: 24 -> 24, of which waited for: 12 -> 13; matrix products, arithmetic and copies ran while one was open for 21% -> 23% of each run, Pallas kernels for 15% -> 15%
where the time goes in v5:
time: 285 us; the launch traced here: 284 us
  waiting for transfers between devices  96.6 us (34%)
  starting transfers between devices  50.8 us (18%)
  Pallas kernels  42.5 us (15%)
  other arithmetic  38.5 us (14%)
  local copies, waits for them, and re-layouts  29.2 us (10%)
  between operations  14.8 us (5%)
  matrix products  11.8 us (4%)
    all_to_all x5, waiting for transfers between devices, everywhere(): return lax.all_to_all(block, 'ctx', split_axis=0, concat_axis=0, tiled=True)  68.6 us
    pallas_call x2, Pallas kernels, kernel_call(): pl.pallas_call(body, out_shape=out_shape, in_specs=[pl.BlockSpec(memory_s...  42.5 us
    all_to_all x5, starting transfers between devices, everywhere(): return lax.all_to_all(block, 'ctx', split_axis=0, concat_axis=0, tiled=True)  28.4 us
    ppermute x4, waiting for transfers between devices, moved(): lax.ppermute(block, 'ctx', [(device, device ^ mask) for device in range(p...  16.3 us
    concatenate x1, other arithmetic, head_owner_device(): core_grad = jnp.concatenate([left_four, right_four], axis=1)  13.3 us
    ppermute x4, starting transfers between devices, head_owner_device(): lax.ppermute(pick(attended_half, (seat + step) % PLANES), 'ctx', up[step])  12.4 us
    unnamed x40, local copies, waits for them, and re-layouts  11.6 us
    dot_general x2, matrix products, contract(): lax.dot_general(left, right, (((left_dim,), (right_dim,)), ((), ())), pre...  8.21 us
  transfers between devices with their start and end apart: 24, of which 13 were waited for; matrix products, arithmetic and copies ran while one was open for 23% of the time, Pallas kernels for 15%

profile of v5, /device:TPU:0, one launch (start us, length us, event | category | flops | bytes accessed | tf_op | source)
XLA Modules:
  0.0 284.3 jit_solution(6735544502282432289)
XLA Ops:
  7.2 1.1 fusion.13
  8.3 3.0 %collective-permute-start.3 = (bf16[128,1024]{1,0:T(8,128)(2,1)S(1)}, bf16[128,1024]{1,0:T(8,128)(2,1)S(1)}, u32[]{:S(2)}, u32[]{:S(2)}) collective-permute-start(bf16[128,1024]{1,0:T(8,128)(2,1)S(1)} %get-tuple-element.61), channel_id=1, source_target_pairs={{0,4},{1,5},{2,6},{3,7},{4,0},{5,1},{6,2},{7,3},{8,12},{9,13},{10,... | collective-permute-start | bytes 786440 | tf_op jit(solution)/shard_map/ppermute | solution.py:493
  11.3 1.5 collective-permute-start.1
  12.8 4.8 %collective-permute-done.3 = bf16[128,1024]{1,0:T(8,128)(2,1)S(1)} collective-permute-done((bf16[128,1024]{1,0:T(8,128)(2,1)S(1)}, bf16[128,1024]{1,0:T(8,128)(2,1)S(1)}, u32[]{:S(2)}, u32[]{:S(2)}) %collective-permute-start.3) | collective-permute-done | bytes 262176 | tf_op jit(solution)/shard_map/ppermute | solution.py:493
  17.7 1.8 collective-permute-start.4
  19.5 1.6 collective-permute-start.2
  21.1 9.7 %collective-permute-done.4 = bf16[256,1024]{1,0:T(8,128)(2,1)S(1)} collective-permute-done((bf16[256,1024]{1,0:T(8,128)(2,1)S(1)}, bf16[256,1024]{1,0:T(8,128)(2,1)S(1)}, u32[]{:S(2)}, u32[]{:S(2)}) %collective-permute-start.4) | collective-permute-done | bytes 524320 | tf_op jit(solution)/shard_map/ppermute | solution.py:493
  30.9 1.7 collective-permute-done.2
  32.6 13.3 %maximum_maximum_fusion = bf16[512,2048]{1,0:T(8,128)(2,1)} fusion(bf16[128,1024]{1,0:T(8,128)(2,1)S(1)} %get-tuple-element.63, bf16[128,1024]{1,0:T(8,128)(2,1)S(1)} %collective-permute-done.3, bf16[128,1024]{1,0:T(8,128)(2,1)S(1)} %get-tuple-element.62, bf16[128,1024]{1,0:T(8,128)(2,1)S(1)} %get-tuple-element.61, ...), kind=kLoop, calls=%fused_computation.10 | loop fusion | flops 14680064 | bytes 4194304 | tf_op jit(solution)/shard_map/concatenate | solution.py:522
  46.7 1.1 pad_maximum_fusion.1
  47.8 6.2 %all-to-all-start = ((bf16[32,72,256]{2,1,0:T(8,128)(2,1)}), bf16[32,72,256]{2,1,0:T(8,128)(2,1)S(1)}, u32[]{:S(2)}, u32[]{:S(2)}) async-start(bf16[32,72,256]{2,1,0:T(8,128)(2,1)} %pad_maximum_fusion.1), calls=%async_computation | async-start | bytes 2359296 | tf_op jit(solution)/shard_map/all_to_all | solution.py:461
  54.0 1.0 copy.100
  55.2 5.2 %pad_maximum_fusion = bf16[1024,2048]{1,0:T(8,128)(2,1)} fusion(bf16[512,2048]{1,0:T(8,128)(2,1)} %collective-permute-done.5, bf16[128,1024]{1,0:T(8,128)(2,1)S(1)} %get-tuple-element.63, bf16[128,1024]{1,0:T(8,128)(2,1)S(1)} %collective-permute-done.3, bf16[128,1024]{1,0:T(8,128)(2,1)S(1)} %get-tuple-element.62, bf16[128,1024]{1,0:T(8,128)(2,1)S(1)} %get-tuple-element.61, ...), kind=kLoop, calls=%fused_computation | loop fusion | flops 33554432 | bytes 8388608 | tf_op jit(solution)/shard_map/concatenate | solution.py:523
  60.4 45.2 %all-to-all-done.mine_ref = bf16[32,72,256]{2,1,0:T(8,128)(2,1)S(1)} async-done(((bf16[32,72,256]{2,1,0:T(8,128)(2,1)}), bf16[32,72,256]{2,1,0:T(8,128)(2,1)S(1)}, u32[]{:S(2)}, u32[]{:S(2)}) %all-to-all-start) | async-done | bytes 1179680 | tf_op jit(solution)/shard_map/all_to_all | solution.py:461
  106.9 1.3 convert_reduce_fusion.1
  108.4 1.2 collective-permute-done.6.other_ref
  109.6 21.5 %shard_map.84 = (bf16[32,128,128]{2,1,0:T(8,128)(2,1)S(1)}, f32[32,256]{1,0:T(8,128)S(1)}) custom-call(bf16[32,72,256]{2,1,0:T(8,128)(2,1)S(1)} %all-to-all-done.mine_ref, bf16[32,64,256]{2,1,0:T(8,128)(2,1)S(1)} %collective-permute-done.6.other_ref, s32[32,128]{1,0:T(8,128)S(1)} %add_select_fusion.slot_ref, f32[32,256]{1,0:T(8,128)S(1)} %select_select_fusion.code_ref), custom_call_target="tpu_custom_call" | custom-call | tf_op jit(solution)/shard_map/pallas_call | solution.py:433
  131.2 1.9 broadcast_select_fusion.1
  133.5 0.8 copy.107
  134.2 1.0 copy.108
  135.3 1.4 select_reduce_fusion.1
  136.9 1.9 pad_maximum_fusion.4
  138.9 1.3 fusion.12
  140.2 2.0 add_convert_fusion.1
  142.2 3.6 %fusion.18 = f32[256,2048]{1,0:T(8,128)S(1)} fusion(bf16[256,1024]{0,1:T(8,128)(2,1)} %pad_maximum_fusion.4, bf16[1024,2048]{1,0:T(8,128)(2,1)} %all-gather.2.cloned.1.call-done), kind=kOutput, calls=%fused_computation.86 | convolution fusion | flops 1073741824 | bytes 6815744 | tf_op jit(solution)/shard_map/dot_general | solution.py:574
  145.9 1.4 copy-done.3
  147.2 1.1 slice.114
  148.8 0.8 slice.94
  149.7 2.6 all-to-all-start.1
  152.4 1.8 dynamic-slice_bitcast_fusion.3
  154.2 1.6 collective-permute-start.13
  155.7 8.1 %collective-permute-start.16 = (bf16[512,128]{1,0:T(8,128)(2,1)S(1)}, bf16[512,128]{1,0:T(8,128)(2,1)S(1)}, u32[]{:S(2)}, u32[]{:S(2)}) collective-permute-start(bf16[512,128]{1,0:T(8,128)(2,1)S(1)} %get-tuple-element.57), channel_id=1, source_target_pairs={{1,0},{5,1},{9,2},{13,3},{17,4},{21,5},{25,6},{29,7},{2,8},{6,9},{... | collective-permute-start | bytes 393224 | tf_op jit(solution)/shard_map/ppermute | solution.py:600
  164.2 2.4 collective-permute-start.14
  166.8 0.9 collective-permute-done.16
  167.7 2.8 collective-permute-done.15
  170.5 1.4 collective-permute-done.14
  171.9 1.1 pad_maximum_fusion.8
  173.4 0.9 copy.141
  174.8 1.3 fusion.3
  176.3 0.9 copy.114
  177.2 10.4 %all-to-all-start.2 = ((bf16[32,64,128]{2,1,0:T(8,128)(2,1)}), bf16[32,64,128]{2,1,0:T(8,128)(2,1)S(1)}, u32[]{:S(2)}, u32[]{:S(2)}) async-start(bf16[32,64,128]{2,1,0:T(8,128)(2,1)} %bitcast.21), calls=%async_computation.2 | async-start | bytes 1048576 | tf_op jit(solution)/shard_map/all_to_all | solution.py:461
  187.7 1.3 copy.115
  189.0 1.4 reshape.254
  194.9 8.0 %all-to-all-done.2 = bf16[32,64,128]{2,1,0:T(8,128)(2,1)S(1)} async-done(((bf16[32,64,128]{2,1,0:T(8,128)(2,1)}), bf16[32,64,128]{2,1,0:T(8,128)(2,1)S(1)}, u32[]{:S(2)}, u32[]{:S(2)}) %all-to-all-start.2) | async-done | bytes 524320 | tf_op jit(solution)/shard_map/all_to_all | solution.py:461
  202.9 0.7 bitcast_dynamic-update-slice_fusion
  203.6 4.7 %fusion = bf16[2048,256]{1,0:T(8,128)(2,1)} fusion(bf16[1024,2048]{1,0:T(8,128)(2,1)} %pad_maximum_fusion, bf16[1024,256]{1,0:T(8,128)(2,1)} %bitcast_dynamic-update-slice_fusion), kind=kOutput, calls=%fused_computation.7 | convolution fusion | flops 1074790400 | bytes 5767168 | tf_op jit(solution)/shard_map/dot_general | solution.py:326
  208.3 2.4 fusion.2
  210.7 3.4 %all-to-all-start.4 = ((bf16[32,64,256]{2,1,0:T(8,128)(2,1)}), bf16[32,64,256]{2,1,0:T(8,128)(2,1)}, u32[]{:S(2)}, u32[]{:S(2)}) async-start(bf16[32,64,256]{2,1,0:T(8,128)(2,1)} %bitcast.129), calls=%async_computation.4 | async-start | bytes 2097152 | tf_op jit(solution)/shard_map/all_to_all | solution.py:461
  214.1 1.4 select_reduce_fusion
  215.6 0.8 copy.117
  216.4 1.0 copy.118.shift_ref
  217.4 21.0 %shard_map.85 = bf16[32,128,256]{2,1,0:T(8,128)(2,1)S(1)} custom-call(bf16[32,72,256]{2,1,0:T(8,128)(2,1)S(1)} %all-to-all-done.mine_ref, bf16[32,64,256]{2,1,0:T(8,128)(2,1)S(1)} %collective-permute-done.6.other_ref, bf16[32,128,128]{2,1,0:T(8,128)(2,1)S(1)} %get-tuple-element.22.grad_ref, s32[32,128]{1,0:T(8,128)S(1)} %add_select_fusion.slot_ref, ...), custom_call_target="tpu_custom_call" | custom-call | tf_op jit(solution)/shard_map/pallas_call | solution.py:433
  238.8 2.5 collective-permute-done.17
  241.2 1.4 add_convert_fusion
  242.6 5.8 %all-to-all-start.3 = ((bf16[32,64,256]{2,1,0:T(8,128)(2,1)}), bf16[32,64,256]{2,1,0:T(8,128)(2,1)S(1)}, u32[]{:S(2)}, u32[]{:S(2)}) async-start(bf16[32,64,256]{2,1,0:T(8,128)(2,1)} %add_convert_fusion), calls=%async_computation.3 | async-start | bytes 2097152 | tf_op jit(solution)/shard_map/all_to_all | solution.py:461
  248.7 1.7 collective-permute-done.10
  250.3 3.5 %convolution_convert_fusion = bf16[256,1024]{1,0:T(8,128)(2,1)S(1)} fusion(bf16[1024,2048]{1,0:T(8,128)(2,1)} %all-gather.2.cloned.1.call-done, bf16[128,2048]{1,0:T(8,128)(2,1)S(1)} %collective-permute-done.10, bf16[128,2048]{1,0:T(8,128)(2,1)S(1)} %bitcast.140), kind=kOutput, calls=%fused_computation.15 | convolution fusion | flops 1076101120 | bytes 5767168 | tf_op jit(solution)/shard_map/dot_general | solution.py:326
  254.2 1.3 collective-permute-done.11
  256.0 1.0 copy.122
  257.0 1.4 convert_reduce_fusion
  258.4 0.8 copy.125
  259.3 15.3 %all-to-all-done.3 = bf16[32,64,256]{2,1,0:T(8,128)(2,1)S(1)} async-done(((bf16[32,64,256]{2,1,0:T(8,128)(2,1)}), bf16[32,64,256]{2,1,0:T(8,128)(2,1)S(1)}, u32[]{:S(2)}, u32[]{:S(2)}) %all-to-all-start.3) | async-done | bytes 1048608 | tf_op jit(solution)/shard_map/all_to_all | solution.py:461
  275.2 0.9 copy.139
  276.5 0.9 copy.140
  (102 shorter events, 12.4 us)
Async XLA Ops:
  7.2 135.1 %all-gather.2.cloned.1.call-start = ((), (), s32[]{:S(2)}) async-start(), calls=%async_computation.5 | async-start | bytes 4456448 | tf_op jit(solution)/shard_map/all_gather | solution.py:495
  8.3 9.3 %collective-permute-start.3 = (bf16[128,1024]{1,0:T(8,128)(2,1)S(1)}, bf16[128,1024]{1,0:T(8,128)(2,1)S(1)}, u32[]{:S(2)}, u32[]{:S(2)}) collective-permute-start(bf16[128,1024]{1,0:T(8,128)(2,1)S(1)} %get-tuple-element.61), channel_id=1, source_target_pairs={{0,4},{1,5},{2,6},{3,7},{4,0},{5,1},{6,2},{7,3},{8,12},{9,13},{10,... | collective-permute-start | bytes 786440 | tf_op jit(solution)/shard_map/ppermute | solution.py:493
  11.3 8.1 %collective-permute-start.1 = (bf16[128,1024]{1,0:T(8,128)(2,1)S(1)}, bf16[128,1024]{1,0:T(8,128)(2,1)S(1)}, u32[]{:S(2)}, u32[]{:S(2)}) collective-permute-start(bf16[128,1024]{1,0:T(8,128)(2,1)S(1)} %get-tuple-element.60), channel_id=1, source_target_pairs={{0,2},{1,3},{2,0},{3,1},{4,6},{5,7},{6,4},{7,5},{8,10},{9,11},{10,... | collective-permute-start | bytes 786440 | tf_op jit(solution)/shard_map/ppermute | solution.py:493
  17.7 13.2 %collective-permute-start.4 = (bf16[256,1024]{1,0:T(8,128)(2,1)S(1)}, bf16[256,1024]{1,0:T(8,128)(2,1)S(1)}, u32[]{:S(2)}, u32[]{:S(2)}) collective-permute-start(bf16[256,1024]{1,0:T(8,128)(2,1)S(1)} %pad_maximum_fusion.6), channel_id=1, source_target_pairs={{0,2},{1,3},{2,0},{3,1},{4,6},{5,7},{6,4},{7,5},{8,10},{9,11},{10,... | collective-permute-start | bytes 1572872 | tf_op jit(solution)/shard_map/ppermute | solution.py:493
  19.5 13.2 %collective-permute-start.2 = (bf16[256,1024]{1,0:T(8,128)(2,1)S(1)}, bf16[256,1024]{1,0:T(8,128)(2,1)S(1)}, u32[]{:S(2)}, u32[]{:S(2)}) collective-permute-start(bf16[256,1024]{1,0:T(8,128)(2,1)S(1)} %pad_maximum_fusion.5), channel_id=1, source_target_pairs={{0,4},{1,5},{2,6},{3,7},{4,0},{5,1},{6,2},{7,3},{8,12},{9,13},{10,... | collective-permute-start | bytes 1572872 | tf_op jit(solution)/shard_map/ppermute | solution.py:493
  30.9 15.0 %copy-start.11 = (s32[2,128]{1,0:T(2,128)S(1)}, s32[2,128]{1,0:T(2,128)}, u32[]{:S(2)}) copy-start(s32[2,128]{1,0:T(2,128)} %param.9) | copy-start | bytes 3076
  30.9 15.0 %copy-start.7 = (bf16[128,2048]{1,0:T(8,128)(2,1)S(1)}, bf16[128,2048]{1,0:T(8,128)(2,1)}, u32[]{:S(2)}) copy-start(bf16[128,2048]{1,0:T(8,128)(2,1)} %param.5) | copy-start | bytes 1572868
  32.6 13.3 %copy-start.6 = (bf16[256,1024]{1,0:T(8,128)(2,1)}, bf16[256,1024]{1,0:T(8,128)(2,1)S(1)}, u32[]{:S(2)}) copy-start(bf16[256,1024]{1,0:T(8,128)(2,1)S(1)} %collective-permute-done.2) | copy-start | bytes 1572868
  32.6 13.4 %copy-start.8 = (bf16[128,2048]{1,0:T(8,128)(2,1)S(1)}, bf16[128,2048]{1,0:T(8,128)(2,1)}, u32[]{:S(2)}) copy-start(bf16[128,2048]{1,0:T(8,128)(2,1)} %param.6) | copy-start | bytes 1572868
  45.9 9.3 %collective-permute-start.5 = (bf16[512,2048]{1,0:T(8,128)(2,1)}, bf16[512,2048]{1,0:T(8,128)(2,1)}, u32[]{:S(2)}, u32[]{:S(2)}) collective-permute-start(bf16[512,2048]{1,0:T(8,128)(2,1)} %maximum_maximum_fusion), channel_id=1, source_target_pairs={{0,1},{1,0},{2,3},{3,2},{4,5},{5,4},{6,7},{7,6},{8,9},{9,8},{10,11... | collective-permute-start | bytes 6291464 | tf_op jit(solution)/shard_map/ppermute | solution.py:455
  46.7 7.4 %copy-start.5 = (bf16[128,2048]{1,0:T(8,128)(2,1)S(1)}, bf16[128,2048]{1,0:T(8,128)(2,1)}, u32[]{:S(2)}) copy-start(bf16[128,2048]{1,0:T(8,128)(2,1)} %param.7) | copy-start | bytes 1572868
  47.8 57.8 %all-to-all-start = ((bf16[32,72,256]{2,1,0:T(8,128)(2,1)}), bf16[32,72,256]{2,1,0:T(8,128)(2,1)S(1)}, u32[]{:S(2)}, u32[]{:S(2)}) async-start(bf16[32,72,256]{2,1,0:T(8,128)(2,1)} %pad_maximum_fusion.1), calls=%async_computation | async-start | bytes 2359296 | tf_op jit(solution)/shard_map/all_to_all | solution.py:461
  106.9 2.7 collective-permute-start.6
  131.0 7.9 %collective-permute-start.8 = (bf16[32,128,128]{2,1,0:T(8,128)(2,1)S(1)}, bf16[32,128,128]{2,1,0:T(8,128)(2,1)}, u32[]{:S(2)}, u32[]{:S(2)}) collective-permute-start(bf16[32,128,128]{2,1,0:T(8,128)(2,1)S(1)} %get-tuple-element.16), channel_id=1, source_target_pairs={{0,1},{1,0},{2,3},{3,2},{4,5},{5,4},{6,7},{7,6},{8,9},{9,8},{10,11... | collective-permute-start | bytes 3145736 | tf_op jit(solution)/shard_map/ppermute | solution.py:455
  133.1 3.8 %collective-permute-start = (bf16[128,1024]{0,1:T(8,128)(2,1)}, bf16[128,1024]{0,1:T(8,128)(2,1)}, u32[]{:S(2)}, u32[]{:S(2)}) collective-permute-start(bf16[128,1024]{0,1:T(8,128)(2,1)} %bitcast.2), channel_id=1, source_target_pairs={{0,1},{1,0},{2,3},{3,2},{4,5},{5,4},{6,7},{7,6},{8,9},{9,8},{10,11... | collective-permute-start | bytes 786440 | tf_op jit(solution)/shard_map/ppermute | solution.py:455
  136.7 2.1 collective-permute-start.7
  145.9 1.4 copy-start.3
  147.2 1.6 copy-start
  148.3 26.0 %collective-permute-start.9 = (f32[128,2048]{1,0:T(8,128)}, f32[128,2048]{1,0:T(8,128)}, u32[]{:S(2)}, u32[]{:S(2)}) collective-permute-start(f32[128,2048]{1,0:T(8,128)} %slice.114), channel_id=1, source_target_pairs={{0,1},{1,0},{2,3},{3,2},{4,5},{5,4},{6,7},{7,6},{8,9},{9,8},{10,11... | collective-permute-start | bytes 3145736 | tf_op jit(solution)/shard_map/ppermute | solution.py:455
  149.7 23.3 %all-to-all-start.1 = ((bf16[32,64,128]{2,1,0:T(8,128)(2,1)}), bf16[32,64,128]{2,1,0:T(8,128)(2,1)S(1)}, u32[]{:S(2)}, u32[]{:S(2)}) async-start(bf16[32,64,128]{2,1,0:T(8,128)(2,1)} %slice.94), calls=%async_computation.1 | async-start | bytes 1048576 | tf_op jit(solution)/shard_map/all_to_all | solution.py:461
  154.2 12.6 %collective-permute-start.13 = (bf16[512,128]{1,0:T(8,128)(2,1)}, bf16[512,128]{1,0:T(8,128)(2,1)S(1)}, u32[]{:S(2)}, u32[]{:S(2)}) collective-permute-start(bf16[512,128]{1,0:T(8,128)(2,1)} %get-tuple-element.56), channel_id=1, source_target_pairs={{0,0},{4,1},{8,2},{12,3},{16,4},{20,5},{24,6},{28,7},{1,8},{5,9},{... | collective-permute-start | bytes 393224 | tf_op jit(solution)/shard_map/ppermute | solution.py:600
  155.7 12.0 %collective-permute-start.16 = (bf16[512,128]{1,0:T(8,128)(2,1)S(1)}, bf16[512,128]{1,0:T(8,128)(2,1)S(1)}, u32[]{:S(2)}, u32[]{:S(2)}) collective-permute-start(bf16[512,128]{1,0:T(8,128)(2,1)S(1)} %get-tuple-element.57), channel_id=1, source_target_pairs={{1,0},{5,1},{9,2},{13,3},{17,4},{21,5},{25,6},{29,7},{2,8},{6,9},{... | collective-permute-start | bytes 393224 | tf_op jit(solution)/shard_map/ppermute | solution.py:600
  163.8 6.7 %collective-permute-start.15 = (bf16[512,128]{1,0:T(8,128)(2,1)S(1)}, bf16[512,128]{1,0:T(8,128)(2,1)}, u32[]{:S(2)}, u32[]{:S(2)}) collective-permute-start(bf16[512,128]{1,0:T(8,128)(2,1)S(1)} %get-tuple-element.58), channel_id=1, source_target_pairs={{2,0},{6,1},{10,2},{14,3},{18,4},{22,5},{26,6},{30,7},{3,8},{7,9},... | collective-permute-start | bytes 393224 | tf_op jit(solution)/shard_map/ppermute | solution.py:600
  164.2 7.7 %collective-permute-start.14 = (bf16[512,128]{1,0:T(8,128)(2,1)S(1)}, bf16[512,128]{1,0:T(8,128)(2,1)}, u32[]{:S(2)}, u32[]{:S(2)}) collective-permute-start(bf16[512,128]{1,0:T(8,128)(2,1)S(1)} %get-tuple-element.59), channel_id=1, source_target_pairs={{3,0},{7,1},{11,2},{15,3},{19,4},{23,5},{27,6},{31,7},{0,8},{4,9},... | collective-permute-start | bytes 393224 | tf_op jit(solution)/shard_map/ppermute | solution.py:600
  167.7 4.2 %copy-start.10 = (bf16[512,128]{1,0:T(8,128)(2,1)}, bf16[512,128]{1,0:T(8,128)(2,1)S(1)}, u32[]{:S(2)}) copy-start(bf16[512,128]{1,0:T(8,128)(2,1)S(1)} %collective-permute-done.16) | copy-start | bytes 393220
  173.0 1.8 copy-start.4
  177.2 25.7 %all-to-all-start.2 = ((bf16[32,64,128]{2,1,0:T(8,128)(2,1)}), bf16[32,64,128]{2,1,0:T(8,128)(2,1)S(1)}, u32[]{:S(2)}, u32[]{:S(2)}) async-start(bf16[32,64,128]{2,1,0:T(8,128)(2,1)} %bitcast.21), calls=%async_computation.2 | async-start | bytes 1048576 | tf_op jit(solution)/shard_map/all_to_all | solution.py:461
  202.9 5.4 %copy-start.2 = (bf16[32,64,128]{2,1,0:T(8,128)(2,1)}, bf16[32,64,128]{2,1,0:T(8,128)(2,1)S(1)}, u32[]{:S(2)}) copy-start(bf16[32,64,128]{2,1,0:T(8,128)(2,1)S(1)} %all-to-all-done.2) | copy-start | bytes 1572868
  202.9 5.4 %collective-permute-start.12 = (bf16[32,64,128]{2,1,0:T(8,128)(2,1)S(1)}, bf16[32,64,128]{2,1,0:T(8,128)(2,1)S(1)}, u32[]{:S(2)}, u32[]{:S(2)}) collective-permute-start(bf16[32,64,128]{2,1,0:T(8,128)(2,1)S(1)} %all-to-all-done.2), channel_id=1, source_target_pairs={{0,1},{1,0},{2,3},{3,2},{4,5},{5,4},{6,7},{7,6},{8,9},{9,8},{10,11... | collective-permute-start | bytes 1572872 | tf_op jit(solution)/shard_map/ppermute | solution.py:455
  203.6 4.8 %copy-start.1 = (bf16[32,128,128]{2,1,0:T(8,128)(2,1)S(1)}, bf16[32,128,128]{2,1,0:T(8,128)(2,1)}, u32[]{:S(2)}) copy-start(bf16[32,128,128]{2,1,0:T(8,128)(2,1)} %add_convert_fusion.1) | copy-start | bytes 3145732
  210.7 31.9 %all-to-all-start.4 = ((bf16[32,64,256]{2,1,0:T(8,128)(2,1)}), bf16[32,64,256]{2,1,0:T(8,128)(2,1)}, u32[]{:S(2)}, u32[]{:S(2)}) async-start(bf16[32,64,256]{2,1,0:T(8,128)(2,1)} %bitcast.129), calls=%async_computation.4 | async-start | bytes 2097152 | tf_op jit(solution)/shard_map/all_to_all | solution.py:461
  238.5 9.9 %copy-start.9 = (bf16[16,8,16,128]{3,1,2,0:T(8,128)(2,1)S(1)}, bf16[16,8,16,128]{3,1,2,0:T(8,128)(2,1)}, u32[]{:S(2)}) copy-start(bf16[16,8,16,128]{3,1,2,0:T(8,128)(2,1)} %copy.141) | copy-start | bytes 1572868
  238.5 2.7 collective-permute-start.17
  242.6 32.0 %all-to-all-start.3 = ((bf16[32,64,256]{2,1,0:T(8,128)(2,1)}), bf16[32,64,256]{2,1,0:T(8,128)(2,1)S(1)}, u32[]{:S(2)}, u32[]{:S(2)}) async-start(bf16[32,64,256]{2,1,0:T(8,128)(2,1)} %add_convert_fusion), calls=%async_computation.3 | async-start | bytes 2097152 | tf_op jit(solution)/shard_map/all_to_all | solution.py:461
  248.4 2.0 collective-permute-start.10
  253.8 1.6 collective-permute-start.11
Sparse Core Ops, SparseCore 0:
  21.2 90.5 all-gather.1

commit v6 on v1

--- a/solution.py
+++ b/solution.py
@@ -318,6 +318,7 @@
 
 PLANES = 4
 TALL = 256
+HALF = 64
 VMEM_BYTES = 48 * 1024 * 1024
 
 
@@ -350,7 +351,7 @@
     buckets = slots // per_peer
 
     def group(source, carry):
-        rows = jnp.concatenate([mine_ref[source], other_ref[source]], axis=0)
+        rows = jnp.concatenate([mine_ref[source, :HALF], other_ref[source]], axis=0)
         grouped[source] = contract(slot_pick(slot_ref, source), rows, 1, 0)
         return carry
 
@@ -388,7 +389,7 @@
     both = 2 * HEAD_DIM
 
     def group(source, carry):
-        rows = jnp.concatenate([mine_ref[source], other_ref[source]], axis=0)
+        rows = jnp.concatenate([mine_ref[source, :HALF], other_ref[source]], axis=0)
         pick = slot_pick(slot_ref, source)
         grouped[source, :, :both] = contract(pick, rows, 1, 0)
         grouped[source, :, both:] = contract(pick, grad_ref[source], 1, 0)
@@ -467,9 +468,21 @@
             token_rows, row_width
         )
 
-    all_buckets = lax.all_gather(buckets, "ctx", axis=0)
     whole_weight = lax.all_gather(out_weight, "ctx", axis=0, tiled=True)
 
+    tag = jnp.pad(buckets.astype(jnp.bfloat16).reshape(1, -1), ((0, 7), (0, 0)))
+    sent = jnp.concatenate([by_head(shared_qk), by_head(values)], axis=-1)
+    sent = jnp.concatenate(
+        [
+            sent.reshape(peers, half, 2 * HEAD_DIM),
+            jnp.broadcast_to(tag[None], (peers, 8, 2 * HEAD_DIM)),
+        ],
+        axis=1,
+    )
+    mine = everywhere(sent)
+    other = exchange(mine[:, :half])
+
+    all_buckets = mine[:, half].astype(jnp.int32).reshape(peers, 2, token_rows)
     own = jnp.where(first, all_buckets[:, 0], all_buckets[:, 1])
     order = jnp.arange(token_rows, dtype=jnp.int32)
     same = (own[:, :, None] == own[:, None, :]) & (order[None, :] < order[:, None])[None]
@@ -485,10 +498,6 @@
     code = jnp.where(live, jnp.where(starts[:, :, None] + within >= SPAN, 2.0, 1.0), 0.0)
     code = code.astype(jnp.float32).transpose(1, 0, 2).reshape(peers, peers * per_peer)
 
-    sent = jnp.concatenate([by_head(shared_qk), by_head(values)], axis=-1)
-    mine = everywhere(sent.reshape(peers, half, 2 * HEAD_DIM))
-    other = exchange(mine)
-
     result, log_slots = kernel_call(
         forward_kernel,
         (
@@ -502,7 +511,8 @@
         (mine, other, slot, code),
     )
 
-    attended_grad = jnp.dot(out_grad, whole_weight, preferred_element_type=jnp.float32).astype(
+    late_grad, result, log_slots = lax.optimization_barrier((out_grad, result, log_slots))
+    attended_grad = jnp.dot(late_grad, whole_weight, preferred_element_type=jnp.float32).astype(
         jnp.bfloat16
     )
     grad_mine = everywhere(by_head(attended_grad).reshape(peers, half, HEAD_DIM))

time: 256 us -> 244 us (0.953)
  blocking collectives: 57.2 us -> 0 us
  waiting for transfers between devices: 64.5 us -> 114 us
  starting transfers between devices: 29.8 us -> 26.3 us
    all_to_all x5, waiting for transfers between devices: 37.4 us -> 95.3 us  [everywhere(): return lax.all_to_all(block, 'ctx', split_axis=0, concat_axis=0, tiled=True)]
    all_gather x1 -> x0, blocking collectives: 57.2 us -> none  [head_owner_device(): all_buckets = lax.all_gather(buckets, 'ctx', axis=0)]
    all_gather x1, waiting for transfers between devices: 17.9 us -> 8.55 us  [head_owner_device(): whole_weight = lax.all_gather(out_weight, 'ctx', axis=0, tiled=True)]
    all_to_all x5, starting transfers between devices: 24.2 us -> 21.5 us  [everywhere(): return lax.all_to_all(block, 'ctx', split_axis=0, concat_axis=0, tiled=True)]
    unnamed x15 -> x18, local copies, waits for them, and re-layouts: 6.74 us -> 7.78 us
  transfers between devices with their start and end apart: 13 -> 13, of which waited for: 5 -> 8; matrix products, arithmetic and copies ran while one was open for 17% -> 17% of each run, Pallas kernels for 17% -> 17%
where the time goes in v6:
time: 244 us; the launch traced here: 243 us
  waiting for transfers between devices  114 us (47%)
  Pallas kernels  42.4 us (17%)
  starting transfers between devices  26.3 us (11%)
  local copies, waits for them, and re-layouts  18.9 us (8%)
  matrix products  15.3 us (6%)
  between operations  14.4 us (6%)
  other arithmetic  12 us (5%)
    all_to_all x5, waiting for transfers between devices, everywhere(): return lax.all_to_all(block, 'ctx', split_axis=0, concat_axis=0, tiled=True)  95.3 us
    pallas_call x2, Pallas kernels, kernel_call(): pl.pallas_call(body, out_shape=out_shape, in_specs=[pl.BlockSpec(memory_s...  42.4 us
    all_to_all x5, starting transfers between devices, everywhere(): return lax.all_to_all(block, 'ctx', split_axis=0, concat_axis=0, tiled=True)  21.5 us
    dot_general x2, matrix products, contract(): lax.dot_general(left, right, (((left_dim,), (right_dim,)), ((), ())), pre...  10.7 us
    all_gather x1, waiting for transfers between devices, head_owner_device(): whole_weight = lax.all_gather(out_weight, 'ctx', axis=0, tiled=True)  8.55 us
    unnamed x18, local copies, waits for them, and re-layouts  7.78 us
    all_to_all x1, waiting for transfers between devices, head_owner_device(): lax.all_to_all(attended_rows, 'ctx', split_axis=1, concat_axis=0, tiled=T...  7.14 us
  transfers between devices with their start and end apart: 13, of which 8 were waited for; matrix products, arithmetic and copies ran while one was open for 17% of the time, Pallas kernels for 17%

profile of v6, /device:TPU:0, one launch (start us, length us, event | category | flops | bytes accessed | tf_op | source)
XLA Modules:
  0.0 243.4 jit_solution(437974095527298227)
XLA Ops:
  7.2 0.7 all-gather.3.cloned.1.call-update
  7.9 1.1 copy.89
  9.1 1.1 copy.90
  10.3 0.3 copy_bitcast_fusion.2
  10.5 0.1 pad_maximum_fusion.1
  10.7 1.2 pad_maximum_fusion
  11.9 7.3 %all-to-all-start = ((bf16[32,72,256]{2,1,0:T(8,128)(2,1)}), bf16[32,72,256]{2,1,0:T(8,128)(2,1)S(1)}, u32[]{:S(2)}, u32[]{:S(2)}) async-start(bf16[32,72,256]{2,1,0:T(8,128)(2,1)} %pad_maximum_fusion), calls=%async_computation | async-start | bytes 2359296 | tf_op jit(solution)/shard_map/all_to_all | solution.py:461
  19.2 0.7 all-gather.5.cloned.1.call-update
  20.0 0.1 lt.74
  20.1 44.8 %all-to-all-done.mine_ref = bf16[32,72,256]{2,1,0:T(8,128)(2,1)S(1)} async-done(((bf16[32,72,256]{2,1,0:T(8,128)(2,1)}), bf16[32,72,256]{2,1,0:T(8,128)(2,1)S(1)}, u32[]{:S(2)}, u32[]{:S(2)}) %all-to-all-start) | async-done | bytes 1179680 | tf_op jit(solution)/shard_map/all_to_all | solution.py:461
  64.9 0.6 convert_reduce_fusion.2
  65.5 0.2 multiply_reduce_fusion
  65.8 0.1 copy.72
  65.9 0.1 slice.65
  66.2 1.3 convert_reduce_fusion.1
  67.5 0.1 add_select_fusion.slot_ref
  67.6 1.2 collective-permute-done.other_ref
  68.8 21.4 %shard_map.84 = (bf16[32,128,128]{2,1,0:T(8,128)(2,1)S(1)}, f32[32,256]{1,0:T(8,128)S(1)}) custom-call(bf16[32,72,256]{2,1,0:T(8,128)(2,1)S(1)} %all-to-all-done.mine_ref, bf16[32,64,256]{2,1,0:T(8,128)(2,1)S(1)} %collective-permute-done.other_ref, s32[32,128]{1,0:T(8,128)S(1)} %add_select_fusion.slot_ref, f32[32,256]{1,0:T(8,128)S(1)} %select_select_fusion.code_ref), custom_call_target="tpu_custom_call" | custom-call | tf_op jit(solution)/shard_map/pallas_call | solution.py:433
  90.3 1.0 copy-done.1
  91.3 8.6 %all-gather.3.cloned.1.call-done = bf16[2048,2048]{1,0:T(8,128)(2,1)} async-done(((bf16[64,2048]{1,0:T(8,128)(2,1)}), bf16[2048,2048]{1,0:T(8,128)(2,1)}) %all-gather.3.cloned.1.call-update) | async-done | bytes 8388624 | tf_op jit(solution)/shard_map/all_gather | solution.py:471
  99.8 4.7 %fusion.4 = bf16[16,8,16,128]{3,1,2,0:T(8,128)(2,1)S(1)} fusion(bf16[128,2048]{1,0:T(8,128)(2,1)S(1)} %copy-done.3, bf16[2048,2048]{1,0:T(8,128)(2,1)} %all-gather.3.cloned.1.call-done), kind=kOutput, calls=%fused_computation.16 | convolution fusion | flops 1074003968 | bytes 9437184 | tf_op jit(solution)/shard_map/dot_general | solution.py:515
  104.5 0.1 copy.93
  104.6 0.9 copy.77
  105.6 3.3 %all-to-all-start.2 = ((bf16[32,64,128]{2,1,0:T(8,128)(2,1)}), bf16[32,64,128]{2,1,0:T(8,128)(2,1)S(1)}, u32[]{:S(2)}, u32[]{:S(2)}) async-start(bf16[32,64,128]{2,1,0:T(8,128)(2,1)} %bitcast.15), calls=%async_computation.2 | async-start | bytes 1048576 | tf_op jit(solution)/shard_map/all_to_all | solution.py:461
  108.9 0.3 collective-permute-start.2
  109.2 0.1 copy.73
  109.3 0.1 copy.74
  109.5 1.4 select_reduce_fusion.1
  110.8 0.3 collective-permute-start.1
  111.2 13.2 %all-to-all-done.2 = bf16[32,64,128]{2,1,0:T(8,128)(2,1)S(1)} async-done(((bf16[32,64,128]{2,1,0:T(8,128)(2,1)}), bf16[32,64,128]{2,1,0:T(8,128)(2,1)S(1)}, u32[]{:S(2)}, u32[]{:S(2)}) %all-to-all-start.2) | async-done | bytes 524320 | tf_op jit(solution)/shard_map/all_to_all | solution.py:461
  124.4 0.1 fusion.13
  124.5 0.1 add_divide_fusion.1
  124.6 1.3 fusion.11
  125.9 0.4 collective-permute-done.3
  126.3 2.7 %fusion.3 = (f32[32,128]{1,0:T(8,128)S(1)}, bf16[32,128,128]{2,1,0:T(8,128)(2,1)S(1)}, bf16[32,128,128]{2,1,0:T(8,128)(2,1)}) fusion(bf16[32,64,128]{2,1,0:T(8,128)(2,1)S(1)} %collective-permute-done.3, bf16[32,64,128]{2,1,0:T(8,128)(2,1)S(1)} %all-to-all-done.2, bf16[32,64,128]{2,1,0:T(8,128)(2,1)S(1)} %get-tuple-element.20, ...), kind=kLoop, calls=%fused_computation.11 | loop fusion | flops 9433088 | bytes 5292032 | tf_op jit(solution)/shard_map/reduce_sum | solution.py:535
  129.0 0.8 slice.70
  129.9 3.3 %all-to-all-start.1 = ((bf16[32,64,128]{2,1,0:T(8,128)(2,1)}), bf16[32,64,128]{2,1,0:T(8,128)(2,1)}, u32[]{:S(2)}, u32[]{:S(2)}) async-start(bf16[32,64,128]{2,1,0:T(8,128)(2,1)} %slice.70), calls=%async_computation.1 | async-start | bytes 1048576 | tf_op jit(solution)/shard_map/all_to_all | solution.py:461
  133.2 1.4 select_reduce_fusion
  134.6 0.1 copy.78
  134.7 0.1 copy.79
  134.9 1.2 copy-done
  136.2 1.2 copy-done.2
  137.4 21.0 %shard_map.85 = bf16[32,128,256]{2,1,0:T(8,128)(2,1)S(1)} custom-call(bf16[32,72,256]{2,1,0:T(8,128)(2,1)S(1)} %all-to-all-done.mine_ref, bf16[32,64,256]{2,1,0:T(8,128)(2,1)S(1)} %copy-done.2, bf16[32,128,128]{2,1,0:T(8,128)(2,1)S(1)} %copy-done, s32[32,128]{1,0:T(8,128)S(1)} %add_select_fusion.slot_ref, f32[32,256]{1,0:T(8,128)S(1)} %select_select_fusion.code_ref, ...), custom_call_target="tpu_custom_call" | custom-call | tf_op jit(solution)/shard_map/pallas_call | solution.py:433
  158.4 1.1 slice.72
  159.5 1.4 copy.110
  160.9 0.2 all_to_all.33
  161.1 0.9 copy.83
  162.0 3.9 %all-to-all-start.4 = ((bf16[128,8,256]{2,0,1:T(8,128)(2,1)}), bf16[128,8,256]{2,0,1:T(8,128)(2,1)S(1)}, u32[]{:S(2)}, u32[]{:S(2)}) async-start(bf16[128,8,256]{2,0,1:T(8,128)(2,1)} %copy.83), calls=%async_computation.4 | async-start | bytes 1048576 | tf_op jit(solution)/shard_map/all_to_all | solution.py:567
  165.9 2.6 %add_convert_fusion = bf16[32,64,256]{2,1,0:T(8,128)(2,1)} fusion(bf16[32,64,256]{2,1,0:T(8,128)(2,1)} %collective-permute-done.4, bf16[32,128,256]{2,1,0:T(8,128)(2,1)S(1)} %shard_map.85), kind=kLoop, calls=%fused_computation.13 | loop fusion | flops 2097152 | bytes 3145728 | tf_op jit(solution)/shard_map/convert_element_type | solution.py:555
  168.5 7.1 %all-to-all-done.4 = bf16[128,8,256]{2,0,1:T(8,128)(2,1)S(1)} async-done(((bf16[128,8,256]{2,0,1:T(8,128)(2,1)}), bf16[128,8,256]{2,0,1:T(8,128)(2,1)S(1)}, u32[]{:S(2)}, u32[]{:S(2)}) %all-to-all-start.4) | async-done | bytes 524320 | tf_op jit(solution)/shard_map/all_to_all | solution.py:567
  175.7 3.8 %all-to-all-start.3 = ((bf16[32,64,256]{2,1,0:T(8,128)(2,1)}), bf16[32,64,256]{2,1,0:T(8,128)(2,1)S(1)}, u32[]{:S(2)}, u32[]{:S(2)}) async-start(bf16[32,64,256]{2,1,0:T(8,128)(2,1)} %add_convert_fusion), calls=%async_computation.3 | async-start | bytes 2097152 | tf_op jit(solution)/shard_map/all_to_all | solution.py:461
  179.5 3.6 %fusion.1 = bf16[2048,256]{0,1:T(8,128)(2,1)S(1)} fusion(bf16[1024,256]{1,0:T(8,128)(2,1)} %bitcast.104, bf16[1024,2048]{1,0:T(8,128)(2,1)} %all-gather.5.cloned.1.call-done), kind=kOutput, calls=%fused_computation.7 | convolution fusion | flops 1074790400 | bytes 5767168 | tf_op jit(solution)/shard_map/dot_general | solution.py:326
  183.2 1.4 copy.84
  184.5 21.2 %all-to-all-done.3 = bf16[32,64,256]{2,1,0:T(8,128)(2,1)S(1)} async-done(((bf16[32,64,256]{2,1,0:T(8,128)(2,1)}), bf16[32,64,256]{2,1,0:T(8,128)(2,1)S(1)}, u32[]{:S(2)}, u32[]{:S(2)}) %all-to-all-start.3) | async-done | bytes 1048608 | tf_op jit(solution)/shard_map/all_to_all | solution.py:461
  205.7 3.8 %all-to-all-start.5 = ((bf16[32,64,256]{2,1,0:T(8,128)(2,1)}), bf16[32,64,256]{2,1,0:T(8,128)(2,1)S(1)}, u32[]{:S(2)}, u32[]{:S(2)}) async-start(bf16[32,64,256]{2,1,0:T(8,128)(2,1)} %bitcast.26), calls=%async_computation.5 | async-start | bytes 2097152 | tf_op jit(solution)/shard_map/all_to_all | solution.py:461
  209.5 7.1 %convolution_convert_fusion.1 = bf16[128,2048]{1,0:T(8,128)(2,1)} fusion(bf16[2048,2048]{1,0:T(8,128)(2,1)} %all-gather.3.cloned.1.call-done, bf16[16,8,16,128]{3,2,1,0:T(8,128)(2,1)S(1)} %bitcast.87), kind=kOutput, calls=%fused_computation.9 | convolution fusion | flops 1074003968 | bytes 9437184 | tf_op jit(solution)/shard_map/dot_general | solution.py:326
  216.6 0.3 fusion.10
  216.9 0.3 copy.82
  217.3 0.9 copy.107
  218.2 0.3 copy.81
  218.5 0.9 copy.108
  219.5 16.1 %all-to-all-done.5 = bf16[32,64,256]{2,1,0:T(8,128)(2,1)S(1)} async-done(((bf16[32,64,256]{2,1,0:T(8,128)(2,1)}), bf16[32,64,256]{2,1,0:T(8,128)(2,1)S(1)}, u32[]{:S(2)}, u32[]{:S(2)}) %all-to-all-start.5) | async-done | bytes 1048608 | tf_op jit(solution)/shard_map/all_to_all | solution.py:461
  235.6 0.2 convert_reduce_fusion
  235.8 0.8 copy.88
  (38 shorter events, 0.7 us)
Async XLA Ops:
  7.2 3.1 %copy-start.5 = (s32[2,128]{1,0:T(2,128)S(1)}, s32[2,128]{1,0:T(2,128)}, u32[]{:S(2)}) copy-start(s32[2,128]{1,0:T(2,128)} %param.9) | copy-start | bytes 3076
  7.2 92.7 %all-gather.3.cloned.1.call-start = ((), (), s32[]{:S(2)}) async-start(), calls=%async_computation.6 | async-start | bytes 8650752 | tf_op jit(solution)/shard_map/all_gather | solution.py:471
  11.9 53.0 %all-to-all-start = ((bf16[32,72,256]{2,1,0:T(8,128)(2,1)}), bf16[32,72,256]{2,1,0:T(8,128)(2,1)S(1)}, u32[]{:S(2)}, u32[]{:S(2)}) async-start(bf16[32,72,256]{2,1,0:T(8,128)(2,1)} %pad_maximum_fusion), calls=%async_computation | async-start | bytes 2359296 | tf_op jit(solution)/shard_map/all_to_all | solution.py:461
  19.2 160.3 %all-gather.5.cloned.1.call-start = ((), (), s32[]{:S(2)}) async-start(), calls=%async_computation.7 | async-start | bytes 4718592 | tf_op jit(solution)/shard_map/all_gather | solution.py:566
  65.9 33.9 %copy-start.3 = (bf16[128,2048]{1,0:T(8,128)(2,1)S(1)}, bf16[128,2048]{1,0:T(8,128)(2,1)}, u32[]{:S(2)}) copy-start(bf16[128,2048]{1,0:T(8,128)(2,1)} %param.7) | copy-start | bytes 1572868
  66.1 2.7 %collective-permute-start = (bf16[32,64,256]{2,1,0:T(8,128)(2,1)S(1)}, bf16[32,64,256]{2,1,0:T(8,128)(2,1)S(1)}, u32[]{:S(2)}, u32[]{:S(2)}) collective-permute-start(bf16[32,64,256]{2,1,0:T(8,128)(2,1)S(1)} %slice.65), channel_id=1, source_target_pairs={{0,1},{1,0},{2,3},{3,2},{4,5},{5,4},{6,7},{7,6},{8,9},{9,8},{10,11... | collective-permute-start | bytes 3145736 | tf_op jit(solution)/shard_map/ppermute | solution.py:455
  90.3 1.0 copy-start.1
  105.6 18.8 %all-to-all-start.2 = ((bf16[32,64,128]{2,1,0:T(8,128)(2,1)}), bf16[32,64,128]{2,1,0:T(8,128)(2,1)S(1)}, u32[]{:S(2)}, u32[]{:S(2)}) async-start(bf16[32,64,128]{2,1,0:T(8,128)(2,1)} %bitcast.15), calls=%async_computation.2 | async-start | bytes 1048576 | tf_op jit(solution)/shard_map/all_to_all | solution.py:461
  108.9 15.7 %collective-permute-start.2 = (bf16[32,128,128]{2,1,0:T(8,128)(2,1)S(1)}, bf16[32,128,128]{2,1,0:T(8,128)(2,1)}, u32[]{:S(2)}, u32[]{:S(2)}) collective-permute-start(bf16[32,128,128]{2,1,0:T(8,128)(2,1)S(1)} %get-tuple-element.12), channel_id=1, source_target_pairs={{0,1},{1,0},{2,3},{3,2},{4,5},{5,4},{6,7},{7,6},{8,9},{9,8},{10,11... | collective-permute-start | bytes 3145736 | tf_op jit(solution)/shard_map/ppermute | solution.py:455
  110.8 13.6 %collective-permute-start.1 = (f32[32,128]{1,0:T(8,128)S(1)}, f32[32,128]{1,0:T(8,128)S(1)}, u32[]{:S(2)}, u32[]{:S(2)}) collective-permute-start(f32[32,128]{1,0:T(8,128)S(1)} %select_reduce_fusion.1), channel_id=1, source_target_pairs={{0,1},{1,0},{2,3},{3,2},{4,5},{5,4},{6,7},{7,6},{8,9},{9,8},{10,11... | collective-permute-start | bytes 49160 | tf_op jit(solution)/shard_map/ppermute | solution.py:455
  124.4 1.9 collective-permute-start.3
  129.9 29.6 %all-to-all-start.1 = ((bf16[32,64,128]{2,1,0:T(8,128)(2,1)}), bf16[32,64,128]{2,1,0:T(8,128)(2,1)}, u32[]{:S(2)}, u32[]{:S(2)}) async-start(bf16[32,64,128]{2,1,0:T(8,128)(2,1)} %slice.70), calls=%async_computation.1 | async-start | bytes 1048576 | tf_op jit(solution)/shard_map/all_to_all | solution.py:461
  134.9 1.2 copy-start
  136.2 1.2 copy-start.2
  159.5 6.4 %collective-permute-start.4 = (bf16[32,64,256]{2,1,0:T(8,128)(2,1)}, bf16[32,64,256]{2,1,0:T(8,128)(2,1)}, u32[]{:S(2)}, u32[]{:S(2)}) collective-permute-start(bf16[32,64,256]{2,1,0:T(8,128)(2,1)} %slice.72), channel_id=1, source_target_pairs={{0,1},{1,0},{2,3},{3,2},{4,5},{5,4},{6,7},{7,6},{8,9},{9,8},{10,11... | collective-permute-start | bytes 3145736 | tf_op jit(solution)/shard_map/ppermute | solution.py:455
  162.0 13.7 %all-to-all-start.4 = ((bf16[128,8,256]{2,0,1:T(8,128)(2,1)}), bf16[128,8,256]{2,0,1:T(8,128)(2,1)S(1)}, u32[]{:S(2)}, u32[]{:S(2)}) async-start(bf16[128,8,256]{2,0,1:T(8,128)(2,1)} %copy.83), calls=%async_computation.4 | async-start | bytes 1048576 | tf_op jit(solution)/shard_map/all_to_all | solution.py:567
  175.7 3.9 %copy-start.4 = (bf16[128,8,256]{2,0,1:T(8,128)(2,1)}, bf16[128,8,256]{2,0,1:T(8,128)(2,1)S(1)}, u32[]{:S(2)}) copy-start(bf16[128,8,256]{2,0,1:T(8,128)(2,1)S(1)} %all-to-all-done.4) | copy-start | bytes 1572868
  175.7 30.1 %all-to-all-start.3 = ((bf16[32,64,256]{2,1,0:T(8,128)(2,1)}), bf16[32,64,256]{2,1,0:T(8,128)(2,1)S(1)}, u32[]{:S(2)}, u32[]{:S(2)}) async-start(bf16[32,64,256]{2,1,0:T(8,128)(2,1)} %add_convert_fusion), calls=%async_computation.3 | async-start | bytes 2097152 | tf_op jit(solution)/shard_map/all_to_all | solution.py:461
  205.7 29.9 %all-to-all-start.5 = ((bf16[32,64,256]{2,1,0:T(8,128)(2,1)}), bf16[32,64,256]{2,1,0:T(8,128)(2,1)S(1)}, u32[]{:S(2)}, u32[]{:S(2)}) async-start(bf16[32,64,256]{2,1,0:T(8,128)(2,1)} %bitcast.26), calls=%async_computation.5 | async-start | bytes 2097152 | tf_op jit(solution)/shard_map/all_to_all | solution.py:461
Sparse Core Ops, SparseCore 0:
  10.9 88.9 all-gather.2
  101.7 45.8 all-gather.4
